TPU v7x, 256 devices: a whole 4x4x8 slice. The times are simulated.
256 devices in a mesh: ctx: 128 (over z, y, x), head: 2 (over core).
Axes of the slice: x: 4, y: 4, z: 8, core: 2. Of those that a mesh axis runs over, the one named last changes fastest.
Arguments:
- hidden_in: bfloat16 [2, 16384, 4096], P(None, 'ctx', 'head'), may hold values from -5 to 5
- norm_gain: bfloat16 [4096], replicated, may hold values from 0.099609375 to 1.8984375
- w_query: bfloat16 [4096, 2048], P('ctx', 'head'), may hold values from -0.35 to 0.35
- w_key: bfloat16 [4096, 512], P('ctx', 'head'), may hold values from -0.35 to 0.35
- w_value: bfloat16 [4096, 512], P('ctx', 'head'), may hold values from -0.09375 to 0.09375
- doc_ids: int32 [2, 16384], P(None, 'ctx'), may hold values from 0 to 31, never falling along the last dimension, each value on 1 to 1920 neighbouring positions
Outputs:
- attended: bfloat16 [2, 16384, 2048], P(None, 'ctx', 'head')
Inputs may be any that keep to these rules, and one draw needn't show every extreme that they name: `doc_ids`: document numbers never fall along a sequence; each document of each sequence has 1 to 1920 positions and one has exactly 1920.
All inputs are finite; a program needn't handle non-finite values.
Results may differ from a plain program's by a relative error of at most 0.012.
Values may be sent and summed in bfloat16 or wider, within the bound.
No kernel may reach another device: no remote copies, remote signals or barrier semaphores. Data moves between devices by JAX's collectives and lax.ppermute only.
A program may use at most 128 MiB of HBM per device.

v0:
```python
import functools

import jax
import jax.numpy as jnp
from jax import lax
from jax.experimental import pallas as pl
from jax.experimental.pallas import tpu as pltpu
from jax.sharding import Mesh, PartitionSpec as P

HD = 128
NZ, NY, NX, NC = 8, 4, 4, 2
AXES = ("z", "y", "x", "head")
THETA = 500000.0
EPS = 1e-05
WIDTH = 4096
HALF = WIDTH // 2
COLS = 6 * HD
LOG2E = 1.4426950408889634
BF = jnp.bfloat16
F32 = jnp.float32


def flat(z, y, x, c):
    return ((z * NY + y) * NX + x) * NC + c


def permute(value, to):
    pairs = [
        (flat(z, y, x, c), flat(*to(z, y, x, c)))
        for z in range(NZ)
        for y in range(NY)
        for x in range(NX)
        for c in range(NC)
    ]
    return lax.ppermute(value, AXES, pairs)


def along_x(value, by):
    return permute(value, lambda z, y, x, c: (z, y, (x + by) % NX, c))


def along_z(value, by):
    return permute(value, lambda z, y, x, c: ((z + by) % NZ, y, x, c))


def along_y(value, by):
    return permute(value, lambda z, y, x, c: (z, (y + by) % NY, x, c))


def spread(by):
    def to(z, y, x, c):
        b = (x + by) % 2
        return 2 * (z % 4) + y // 2, 2 * (y % 2) + x // 2, 2 * c + b, z // 4

    return to


def back(k):
    def to(z, y, x, c):
        return z, y, (2 * (x % 2) + c) ^ k, x // 2

    return to


VMEM = pl.BlockSpec(memory_space=pltpu.VMEM)
SMEM = pl.BlockSpec(memory_space=pltpu.SMEM)
ROWS = 8 * HD + 16


def begin_kernel(idx, hidden, query, key, value, first, second, squares):
    x = idx[2]
    for by, out in ((0, first), (1, second)):
        b = lax.rem(x + by, 2)
        out[:, :512] = query[:, pl.ds(pl.multiple_of(b * 512, 512), 512)]
        out[:, 512:640] = key[:, pl.ds(pl.multiple_of(b * 128, 128), 128)]
        out[:, 640:] = value[:, pl.ds(pl.multiple_of(b * 128, 128), 128)]

    for s in range(2):
        wide = hidden[s].astype(F32)
        total = jnp.sum(wide * wide, axis=-1, keepdims=True)
        squares[s : s + 1, :] = jnp.broadcast_to(total, (HD, HD)).T[:1, :]


def tell_kernel(squares, others, docs, out):
    scale = lax.rsqrt((squares[...] + others[...]) * (1.0 / WIDTH) + EPS)
    out[0:2, :] = docs[...].astype(F32)
    out[2:4, :] = scale


def merge_kernel(idx, first, second, out):
    odd = lax.rem(idx[2], 2) == 1
    top, low = first[...].astype(F32), second[...].astype(F32)
    out[:32, :] = jnp.where(odd, low, top).astype(BF)
    out[32:, :] = jnp.where(odd, top, low).astype(BF)


def norm_kernel(idx, gain, *refs):
    told, hidden, x_all = refs[:4], refs[4:12], refs[12]
    x, c = idx[2], idx[3]
    g = gain[:, pl.ds(pl.multiple_of(c * HALF, HALF), HALF)].astype(F32)
    for n, ref in enumerate(hidden):
        s, d = n // 4, (0, -1, 1, 2)[n % 4]
        chip = lax.rem(x + d + NX, NX)
        base = jnp.where(c == s, 0, 512) + chip * 128
        scale = jnp.broadcast_to(told[-d % NX][2 + s : 3 + s, :], (HD, HD)).T
        for t in range(4):
            rows = slice(t * 32, t * 32 + 32)
            wide = ref[rows, :].astype(F32) * scale[rows, :1] * g
            x_all[pl.ds(pl.multiple_of(base + t * 32, 32), 32), :] = wide.astype(BF)


def multiply(x_all, w_all, keep, send):
    for t in range(2):
        at = t * 256
        send[at : at + 256, :] = jnp.dot(
            x_all[512 + at : 768 + at, :], w_all, preferred_element_type=F32
        )
    for t in range(2):
        at = t * 256
        keep[at : at + 256, :] = jnp.dot(
            x_all[at : at + 256, :], w_all, preferred_element_type=F32
        )


def project_kernel(idx, x_all, own, up, down, far_up, far_down, keep, send, w_all):
    columns = own.shape[1]
    for ref, d, first in ((own, 0, 0), (up, -1, 0), (down, 1, 0), (far_up, 2, 0), (far_down, 2, 4)):
        shift = pl.multiple_of(lax.rem(idx[1] + d + NY, NY) * 64, 64)
        for z in range(ref.shape[0] // 64):
            w_all[first + z, pl.ds(shift, 64), :] = ref[z * 64 : z * 64 + 64, :]
    multiply(x_all, w_all[...].reshape(HALF, columns), keep, send)


def turned(value, cos, sin):
    cosine = jnp.concatenate([cos, cos], axis=1)
    sine = jnp.concatenate([-sin, sin], axis=1)
    return value * cosine + pltpu.roll(value, 64, 1) * sine


def rotate_kv_kernel(idx, keep, got, cos, sin, *refs):
    told, kv = refs[:4], refs[4]
    for i in range(4):
        rows = slice(i * 128, i * 128 + 128)
        value = keep[rows, :] + got[rows, :]
        at = i * 256
        kv[at : at + 128, :] = turned(value[:, :128], cos[rows, :], sin[rows, :]).astype(BF)
        kv[at + 128 : at + 256, :] = value[:, 128:].T.astype(BF)
    docs = jnp.zeros((16, HD), F32)
    row = lax.broadcasted_iota(jnp.int32, (16, HD), 0)
    for n in range(NX):
        piece = jnp.where(idx[3] == 0, told[n][0:1, :], told[n][1:2, :])
        docs = jnp.where(row == lax.rem(idx[2] - n + NX, NX), piece, docs)
    kv[1024:1040, :] = docs.astype(BF)


def rotate_q_kernel(keep, got, cos, sin, query):
    for i in range(4):
        rows = slice(i * 128, i * 128 + 128)
        for h in range(4):
            cols = slice(h * 128, h * 128 + 128)
            value = keep[rows, cols] + got[rows, cols]
            query[i, h * 128 : h * 128 + 128, :] = turned(value, cos[rows, :], sin[rows, :]).astype(BF)


def attend(idx, query, start, kv, scores, acc, outs, part):
    c = idx[3]
    m = jnp.bitwise_xor(lax.rem(idx[2], 2), part)
    first = jnp.concatenate([start[2 * m], start[2 * m + 1]], axis=1)
    rows = query[pl.ds(2 * m, 2)].reshape(1024, HD)
    sub = lax.broadcasted_iota(jnp.int32, (256, 1024), 0)
    lane = lax.broadcasted_iota(jnp.int32, (256, 1024), 1)
    lane = lax.div(lane, 512) * 128 + lax.rem(lane, 128)
    last = 8 + m
    low = jnp.minimum(lax.div(jnp.maximum(jnp.min(first), 0), 256), last)
    contract = (((1,), (1,)), ((), ()))

    def score(p):
        keys = kv[pl.ds(2 * p, 2), 0].reshape(256, HD)
        return lax.dot_general(keys, rows, contract, preferred_element_type=F32)

    def top(s):
        return jnp.max(s.reshape(32, 8, 1024), axis=0)

    def scan(p, best):
        s = jnp.where(sub >= first - 256 * p, score(p), -1e30)
        scores[pl.ds(pl.multiple_of(p * 256, 256), 256), :] = s
        return jnp.maximum(best, top(s))

    s = jnp.where((sub >= first - 256 * last) & (sub <= lane), score(last), -1e30)
    scores[pl.ds(pl.multiple_of(256 * last, 256), 256), :] = s
    best = lax.fori_loop(low, last, scan, top(s))
    best = jnp.max(best, axis=0, keepdims=True)
    acc[...] = jnp.zeros((HD, 1024), F32)

    def gather(p, total):
        s = scores[pl.ds(pl.multiple_of(p * 256, 256), 256), :]
        e = jnp.exp2((s - best) * (LOG2E * HD**-0.5))
        values = jnp.concatenate([kv[2 * p, 1], kv[2 * p + 1, 1]], axis=1)
        acc[...] += jnp.dot(values, e.astype(BF), preferred_element_type=F32)
        return total + jnp.sum(e.reshape(32, 8, 1024), axis=0)

    total = lax.fori_loop(low, last + 1, gather, jnp.zeros((8, 1024), F32))
    mixed = acc[...] / jnp.sum(total, axis=0, keepdims=True)
    for h in range(4):
        cols = slice(h * 128, h * 128 + 128)
        blocks = [mixed[:, j * 512 + h * 128 : j * 512 + h * 128 + 128].T for j in range(2)]
        outs[0][:, cols] = jnp.where(c == 0, blocks[0], blocks[1]).astype(BF)
        outs[1][:, cols] = jnp.where(c == 0, blocks[1], blocks[0]).astype(BF)


def collect_kernel(idx, *refs):
    pieces, (kv, start, docs) = refs[:5], refs[5:]
    z, y = idx[0], idx[1]
    docs[...] = jnp.zeros((128, HD), F32)
    for n, piece in enumerate(pieces):
        kv[4 * n : 4 * n + 4] = piece[:1024, :].reshape(4, 2, 128, HD)
        before = (z == 0) & (y + n < 4)
        docs[4 * n : 4 * n + 4, :] = jnp.where(before, -1.0, piece[1024:1040, :].astype(F32)[:4, :])
    columns = docs[...].T
    mine = jnp.concatenate([docs[16 + i : 17 + i, :] for i in range(4)], axis=1)
    count = jnp.zeros((8, 512), F32)
    for n in range(20):
        smaller = jnp.where(columns[:, n : n + 1] < mine, 1.0, 0.0)
        count = count + jnp.sum(smaller.reshape(16, 8, 512), axis=0)
    count = jnp.sum(count, axis=0, keepdims=True).astype(jnp.int32)
    for i in range(4):
        row = count[:, i * 128 : i * 128 + 128]
        start[i] = jnp.concatenate([row] * 4, axis=1)


def attend_kernel(part, idx, query, kv, start, out0, out1, scores, acc):
    attend(idx, query, start, kv, scores, acc, (out0, out1), part)


def place_kernel(idx, *refs):
    out = refs[4]
    for k in range(4):
        slot = jnp.bitwise_xor(idx[2], k)
        at = pl.multiple_of(lax.div(slot, 2) * 512, 512)
        out[lax.rem(slot, 2), :, pl.ds(at, 512)] = refs[k][...]


def call(kernel, shapes, args, scratch=(), cost=None, smem=1, mib=16):
    return pl.pallas_call(
        kernel,
        out_shape=shapes,
        in_specs=[SMEM] * smem + [VMEM] * (len(args) - smem),
        out_specs=jax.tree.map(lambda _: VMEM, shapes),
        scratch_shapes=list(scratch),
        cost_estimate=cost,
        compiler_params=pltpu.CompilerParams(vmem_limit_bytes=mib * 1024 * 1024),
    )(*args)


def cost(flops, nbytes):
    return pl.CostEstimate(flops=flops, bytes_accessed=nbytes, transcendentals=0)


def tie(*values):
    return lax.optimization_barrier(values)


def copies(value, axis, count):
    return lax.all_to_all(
        jnp.broadcast_to(value[None], (count, *value.shape)), axis, 0, 0, tiled=True
    )


def local(hidden_in, norm_gain, w_query, w_key, w_value, doc_ids):
    z, y, x, c = (lax.axis_index(a) for a in AXES)
    shape = jax.ShapeDtypeStruct
    where = jnp.stack([z, y, x, c]).astype(jnp.int32)

    seq_a, seq_b = hidden_in[0], hidden_in[1]
    right_a, left_b = along_x(seq_a, 1), along_x(seq_b, -1)
    right_b, left_a = along_x(seq_b, 1), along_x(seq_a, -1)

    piece = shape((32, COLS), BF)
    first, second, squares = call(
        begin_kernel,
        (piece, piece, shape((2, HD), F32)),
        (where, hidden_in, w_query, w_key, w_value),
        cost=cost(1 << 20, 2 << 20),
    )
    first, second = permute(first, spread(0)), permute(second, spread(1))
    others = permute(squares, lambda z, y, x, c: (z, y, x, 1 - c))
    told = call(
        tell_kernel,
        shape((4, HD), F32),
        (squares, others, doc_ids),
        cost=cost(0, 1 << 14),
        smem=0,
    )
    told1, told2, told3 = (along_x(told, n) for n in (1, 2, 3))
    first, second, right_a, left_b = tie(first, second, right_a, left_b)
    far_a, far_b = along_x(right_a, 1), along_x(left_b, -1)
    rows = call(merge_kernel, shape((64, COLS), BF), (where, first, second), cost=cost(0, 1 << 18))
    w_z = copies(rows, "z", NZ).reshape(512, COLS)
    w_z, right_b, left_a, told1, told2, told3 = tie(w_z, right_b, left_a, told1, told2, told3)
    told = (told, told1, told2, told3)
    around = []
    for cols in (slice(512, COLS), slice(0, 512)):
        own = w_z[:, cols]
        if around:
            own, up, down = tie(own, *around[0][1:3])
            around[0] = (around[0][0], up, down, *around[0][3:])
        up, down = along_y(own, 1), along_y(own, -1)
        around.append((own, up, down, along_y(up[:256], 1), along_y(down[256:], -1)))
    x_all = call(
        norm_kernel,
        shape((1024, HALF), BF),
        (where, norm_gain.reshape(1, WIDTH), *told)
        + (seq_a, right_a, left_a, far_a, seq_b, right_b, left_b, far_b),
        cost=cost(1 << 22, 8 << 20),
    )

    position = (512 * (z * NY + y) + jnp.arange(512, dtype=jnp.int32)).astype(F32)
    inverse = THETA ** (-jnp.arange(64, dtype=F32) * 2.0 / HD)
    angle = position[:, None] * inverse[None, :]
    cos, sin = jnp.cos(angle), jnp.sin(angle)

    x_all, cos, sin = tie(x_all, cos, sin)
    keep, send = call(
        project_kernel,
        (shape((512, 256), F32), shape((512, 256), F32)),
        (where, x_all, *around[0]),
        (pltpu.VMEM((NZ, 256, 256), BF),),
        cost(2 * 1024 * HALF * 256, 10 << 20),
    )
    got = permute(send, lambda z, y, x, c: (z, y, x, 1 - c))
    own = call(
        rotate_kv_kernel,
        shape((ROWS, HD), BF),
        (where, keep, got, cos, sin, *told),
        cost=cost(1 << 20, 2 << 20),
    )
    x_all, own = tie(x_all, own)
    earlier = [
        permute(own, lambda z, y, x, c: (*divmod((z * NY + y + n) % (NZ * NY), NY), x, c))
        for n in (4, 3, 2, 1)
    ]
    keep, send = call(
        project_kernel,
        (shape((512, 512), F32), shape((512, 512), F32)),
        (where, x_all, *around[1]),
        (pltpu.VMEM((NZ, 256, 512), BF),),
        cost(2 * 1024 * HALF * 512, 10 << 20),
    )
    got = permute(send, lambda z, y, x, c: (z, y, x, 1 - c))
    query = call(
        rotate_q_kernel,
        shape((4, 512, HD), BF),
        (keep, got, cos, sin),
        cost=cost(4 << 20, 3 << 20),
        smem=0,
    )
    kv, start = call(
        collect_kernel,
        (shape((20, 2, 128, HD), BF), shape((4, 1, 512), jnp.int32)),
        (where, *earlier, own),
        (pltpu.VMEM((128, HD), F32),),
        cost(1 << 36, 4 << 20),
    )
    block = shape((128, 512), BF)

    def blocks(part, flops):
        return call(
            functools.partial(attend_kernel, part),
            (block, block),
            (where, query, kv, start),
            (pltpu.VMEM((2560, 1024), F32), pltpu.VMEM((HD, 1024), F32)),
            cost(flops, 4 << 20),
            mib=24,
        )

    out0, out1 = blocks(0, 1 << 30)
    out0, out1 = permute(out0, back(0)), permute(out1, back(1))
    out2, out3 = blocks(1, 1 << 33)
    out0, out1, out2, out3 = tie(out0, out1, out2, out3)
    out2, out3 = permute(out2, back(2)), permute(out3, back(3))
    return call(
        place_kernel, shape((2, 128, 1024), BF), (where, out0, out1, out2, out3), cost=cost(0, 1 << 20)
    )


def solution(mesh):
    fine = Mesh(mesh.devices.reshape(NZ, NY, NX, NC), AXES)
    ctx = ("z", "y", "x")
    return jax.shard_map(
        local,
        mesh=fine,
        in_specs=(
            P(None, ctx, "head"),
            P(),
            P(ctx, "head"),
            P(ctx, "head"),
            P(ctx, "head"),
            P(None, ctx),
        ),
        out_specs=P(None, ctx, "head"),
        check_vma=False,
    )
```

profile of v0, /device:TPU:1, one launch (start us, length us, event | category | flops | bytes accessed | tf_op | source)
XLA Modules:
  0.0 152.0 jit_solution(13077369242768503115)
XLA Ops:
  1.3 2.1 %collective-permute-start.3 = (bf16[128,2048]{1,0:T(8,128)(2,1)S(1)}, bf16[128,2048]{1,0:T(8,128)(2,1)S(1)}, u32[]{:S(2)}, u32[]{:S(2)}) collective-permute-start(bf16[128,2048]{1,0:T(8,128)(2,1)S(1)} %get-tuple-element.76.refs_4_), channel_id=1, source_target_pairs={{0,2},{1,3},{2,4},{3,5},{4,6},{5,7},{6,0},{7,1},{8,10},{9,11},{10,... | collective-permute-start | bytes 1572872 | tf_op jit(solution)/shard_map/ppermute | solution.py:35
  9.2 4.7 %collective-permute-start.1 = (bf16[32,768]{1,0:T(8,128)(2,1)S(1)}, bf16[32,768]{1,0:T(8,128)(2,1)S(1)}, u32[]{:S(2)}, u32[]{:S(2)}) collective-permute-start(bf16[32,768]{1,0:T(8,128)(2,1)S(1)} %get-tuple-element.41), channel_id=1, source_target_pairs={{0,0},{1,4},{2,2},{3,6},{4,8},{5,12},{6,10},{7,14},{8,16},{9,20},{... | collective-permute-start | bytes 147464 | tf_op jit(solution)/shard_map/ppermute | solution.py:35
  13.9 2.2 %collective-permute-start.2 = (bf16[32,768]{1,0:T(8,128)(2,1)S(1)}, bf16[32,768]{1,0:T(8,128)(2,1)S(1)}, u32[]{:S(2)}, u32[]{:S(2)}) collective-permute-start(bf16[32,768]{1,0:T(8,128)(2,1)S(1)} %get-tuple-element.42), channel_id=1, source_target_pairs={{0,2},{1,6},{2,0},{3,4},{4,10},{5,14},{6,8},{7,12},{8,18},{9,22},{... | collective-permute-start | bytes 147464 | tf_op jit(solution)/shard_map/ppermute | solution.py:35
  16.2 4.9 %collective-permute-done.1.first = bf16[32,768]{1,0:T(8,128)(2,1)S(1)} collective-permute-done((bf16[32,768]{1,0:T(8,128)(2,1)S(1)}, bf16[32,768]{1,0:T(8,128)(2,1)S(1)}, u32[]{:S(2)}, u32[]{:S(2)}) %collective-permute-start.1) | collective-permute-done | bytes 49184 | tf_op jit(solution)/shard_map/ppermute | solution.py:35
  23.8 9.7 %all-to-all-start = ((bf16[8,64,768]{2,1,0:T(8,128)(2,1)}), bf16[8,64,768]{2,1,0:T(8,128)(2,1)}, u32[]{:S(2)}, u32[]{:S(2)}) async-start(bf16[8,64,768]{2,1,0:T(8,128)(2,1)} %broadcast_in_dim.2), calls=%async_computation | async-start | bytes 1572864 | tf_op jit(solution)/shard_map/all_to_all | solution.py:264
  34.2 2.0 %collective-permute-start.6 = (bf16[128,2048]{1,0:T(8,128)(2,1)S(1)}, bf16[128,2048]{1,0:T(8,128)(2,1)S(1)}, u32[]{:S(2)}, u32[]{:S(2)}) collective-permute-start(bf16[128,2048]{1,0:T(8,128)(2,1)S(1)} %get-tuple-element.76.refs_4_), channel_id=1, source_target_pairs={{0,6},{1,7},{2,0},{3,1},{4,2},{5,3},{6,4},{7,5},{8,14},{9,15},{10,... | collective-permute-start | bytes 1572872 | tf_op jit(solution)/shard_map/ppermute | solution.py:35
  36.2 2.7 %collective-permute-start.11 = (bf16[128,2048]{1,0:T(8,128)(2,1)S(1)}, bf16[128,2048]{1,0:T(8,128)(2,1)}, u32[]{:S(2)}, u32[]{:S(2)}) collective-permute-start(bf16[128,2048]{1,0:T(8,128)(2,1)S(1)} %collective-permute-done.4.refs_10_), channel_id=1, source_target_pairs={{0,6},{1,7},{2,0},{3,1},{4,2},{5,3},{6,4},{7,5},{8,14},{9,15},{10,... | collective-permute-start | bytes 1572872 | tf_op jit(solution)/shard_map/ppermute | solution.py:35
  41.1 18.6 %collective-permute-done.7.refs_1_ = f32[4,128]{1,0:T(4,128)S(1)} collective-permute-done((f32[4,128]{1,0:T(4,128)S(1)}, f32[4,128]{1,0:T(4,128)S(1)}, u32[]{:S(2)}, u32[]{:S(2)}) %collective-permute-start.7) | collective-permute-done | bytes 2080 | tf_op jit(solution)/shard_map/ppermute | solution.py:35
  59.6 3.9 %collective-permute-done.8.refs_2_ = f32[4,128]{1,0:T(4,128)S(1)} collective-permute-done((f32[4,128]{1,0:T(4,128)S(1)}, f32[4,128]{1,0:T(4,128)S(1)}, u32[]{:S(2)}, u32[]{:S(2)}) %collective-permute-start.8) | collective-permute-done | bytes 2080 | tf_op jit(solution)/shard_map/ppermute | solution.py:35
  63.6 2.4 %collective-permute-done.9.refs_3_ = f32[4,128]{1,0:T(4,128)S(1)} collective-permute-done((f32[4,128]{1,0:T(4,128)S(1)}, f32[4,128]{1,0:T(4,128)S(1)}, u32[]{:S(2)}, u32[]{:S(2)}) %collective-permute-start.9) | collective-permute-done | bytes 2080 | tf_op jit(solution)/shard_map/ppermute | solution.py:35
  67.8 2.4 %collective-permute-start.12 = (bf16[512,256]{1,0:T(8,128)(2,1)S(1)}, bf16[512,256]{1,0:T(8,128)(2,1)S(1)}, u32[]{:S(2)}, u32[]{:S(2)}) collective-permute-start(bf16[512,256]{1,0:T(8,128)(2,1)S(1)} %slice.26.own), channel_id=1, source_target_pairs={{0,8},{1,9},{2,10},{3,11},{4,12},{5,13},{6,14},{7,15},{8,16},{9,17... | collective-permute-start | bytes 786440 | tf_op jit(solution)/shard_map/ppermute | solution.py:35
  70.2 2.4 %collective-permute-start.13 = (bf16[512,256]{1,0:T(8,128)(2,1)S(1)}, bf16[512,256]{1,0:T(8,128)(2,1)S(1)}, u32[]{:S(2)}, u32[]{:S(2)}) collective-permute-start(bf16[512,256]{1,0:T(8,128)(2,1)S(1)} %slice.26.own), channel_id=1, source_target_pairs={{0,24},{1,25},{2,26},{3,27},{4,28},{5,29},{6,30},{7,31},{8,0},{9,1... | collective-permute-start | bytes 786440 | tf_op jit(solution)/shard_map/ppermute | solution.py:35
  73.7 2.6 %collective-permute-done.12.up = bf16[512,256]{1,0:T(8,128)(2,1)S(1)} collective-permute-done((bf16[512,256]{1,0:T(8,128)(2,1)S(1)}, bf16[512,256]{1,0:T(8,128)(2,1)S(1)}, u32[]{:S(2)}, u32[]{:S(2)}) %collective-permute-start.12) | collective-permute-done | bytes 262176 | tf_op jit(solution)/shard_map/ppermute | solution.py:35
  77.5 1.6 %collective-permute-start.18 = (bf16[512,512]{1,0:T(8,128)(2,1)S(1)}, bf16[512,512]{1,0:T(8,128)(2,1)S(1)}, u32[]{:S(2)}, u32[]{:S(2)}) collective-permute-start(bf16[512,512]{1,0:T(8,128)(2,1)S(1)} %slice.27.own), channel_id=1, source_target_pairs={{0,24},{1,25},{2,26},{3,27},{4,28},{5,29},{6,30},{7,31},{8,0},{9,1... | collective-permute-start | bytes 1572872 | tf_op jit(solution)/shard_map/ppermute | solution.py:35
  79.4 2.7 %collective-permute-start.15 = (bf16[256,256]{1,0:T(8,128)(2,1)S(1)}, bf16[256,256]{1,0:T(8,128)(2,1)S(1)}, u32[]{:S(2)}, u32[]{:S(2)}) collective-permute-start(bf16[256,256]{1,0:T(8,128)(2,1)S(1)} %slice.33), channel_id=1, source_target_pairs={{0,24},{1,25},{2,26},{3,27},{4,28},{5,29},{6,30},{7,31},{8,0},{9,1... | collective-permute-start | bytes 393224 | tf_op jit(solution)/shard_map/ppermute | solution.py:35
  84.2 2.3 %shard_map.67.x_all = bf16[1024,2048]{1,0:T(8,128)(2,1)S(1)} custom-call(s32[4]{0:T(128)S(1)} %pad_add_fusion.idx, bf16[1,4096]{1,0:T(2,128)(2,1)S(1)} %reshape.18.gain, f32[4,128]{1,0:T(4,128)S(1)} %shard_map.65.refs_0_, f32[4,128]{1,0:T(4,128)S(1)} %collective-permute-done.7.refs_1_, f32[4,128]{1,0:T(4,128)S(1)} %collective-permute-done.8.refs_2_, ...), custom_call_target="tpu_custom_call" | custom-call | flops 4194304 | bytes 8388608 | tf_op jit(solution)/shard_map/pallas_call | solution.py:244
  86.5 3.4 %collective-permute-done.14.far_up = bf16[256,256]{1,0:T(8,128)(2,1)S(1)} collective-permute-done((bf16[256,256]{1,0:T(8,128)(2,1)S(1)}, bf16[256,256]{1,0:T(8,128)(2,1)S(1)}, u32[]{:S(2)}, u32[]{:S(2)}) %collective-permute-start.14) | collective-permute-done | bytes 131104 | tf_op jit(solution)/shard_map/ppermute | solution.py:35
  89.9 1.8 %shard_map.68 = (f32[512,256]{1,0:T(8,128)S(1)}, f32[512,256]{1,0:T(8,128)S(1)}) custom-call(s32[4]{0:T(128)S(1)} %pad_add_fusion.idx, bf16[1024,2048]{1,0:T(8,128)(2,1)S(1)} %shard_map.67.x_all, bf16[512,256]{1,0:T(8,128)(2,1)S(1)} %slice.26.own, bf16[512,256]{1,0:T(8,128)(2,1)S(1)} %collective-permute-done.12.up, ...), custom_call_target="tpu_custom_call" | custom-call | flops 1073741824 | bytes 10485760 | tf_op jit(solution)/shard_map/pallas_call | solution.py:244
  91.8 4.9 %collective-permute-start.16 = (f32[512,256]{1,0:T(8,128)S(1)}, f32[512,256]{1,0:T(8,128)S(1)}, u32[]{:S(2)}, u32[]{:S(2)}) collective-permute-start(f32[512,256]{1,0:T(8,128)S(1)} %get-tuple-element.57), channel_id=1, source_target_pairs={{0,1},{1,0},{2,3},{3,2},{4,5},{5,4},{6,7},{7,6},{8,9},{9,8},{10,11... | collective-permute-start | bytes 1572872 | tf_op jit(solution)/shard_map/ppermute | solution.py:35
  97.9 1.7 %collective-permute-start.20 = (bf16[256,512]{1,0:T(8,128)(2,1)S(1)}, bf16[256,512]{1,0:T(8,128)(2,1)S(1)}, u32[]{:S(2)}, u32[]{:S(2)}) collective-permute-start(bf16[256,512]{1,0:T(8,128)(2,1)S(1)} %slice.35), channel_id=1, source_target_pairs={{0,24},{1,25},{2,26},{3,27},{4,28},{5,29},{6,30},{7,31},{8,0},{9,1... | collective-permute-start | bytes 786440 | tf_op jit(solution)/shard_map/ppermute | solution.py:35
  103.4 2.0 %collective-permute-start.24 = (bf16[1040,128]{1,0:T(8,128)(2,1)S(1)}, bf16[1040,128]{1,0:T(8,128)(2,1)S(1)}, u32[]{:S(2)}, u32[]{:S(2)}) collective-permute-start(bf16[1040,128]{1,0:T(8,128)(2,1)S(1)} %shard_map.69.refs_4_), channel_id=1, source_target_pairs={{0,16},{1,17},{2,18},{3,19},{4,20},{5,21},{6,22},{7,23},{8,24},{9,... | collective-permute-start | bytes 798728 | tf_op jit(solution)/shard_map/ppermute | solution.py:35
  106.1 3.1 %shard_map.70 = (f32[512,512]{1,0:T(8,128)S(1)}, f32[512,512]{1,0:T(8,128)S(1)}) custom-call(s32[4]{0:T(128)S(1)} %pad_add_fusion.idx, bf16[1024,2048]{1,0:T(8,128)(2,1)S(1)} %shard_map.67.x_all, bf16[512,512]{1,0:T(8,128)(2,1)S(1)} %slice.27.own, bf16[512,512]{1,0:T(8,128)(2,1)S(1)} %collective-permute-done.17.up, ...), custom_call_target="tpu_custom_call" | custom-call | flops 2147483648 | bytes 10485760 | tf_op jit(solution)/shard_map/pallas_call | solution.py:244
  109.2 2.0 %collective-permute-start.21 = (f32[512,512]{1,0:T(8,128)S(1)}, f32[512,512]{1,0:T(8,128)S(1)}, u32[]{:S(2)}, u32[]{:S(2)}) collective-permute-start(f32[512,512]{1,0:T(8,128)S(1)} %get-tuple-element.63), channel_id=1, source_target_pairs={{0,1},{1,0},{2,3},{3,2},{4,5},{5,4},{6,7},{7,6},{8,9},{9,8},{10,11... | collective-permute-start | bytes 3145736 | tf_op jit(solution)/shard_map/ppermute | solution.py:35
  111.2 3.3 %collective-permute-done.23.refs_1_ = bf16[1040,128]{1,0:T(8,128)(2,1)S(1)} collective-permute-done((bf16[1040,128]{1,0:T(8,128)(2,1)S(1)}, bf16[1040,128]{1,0:T(8,128)(2,1)S(1)}, u32[]{:S(2)}, u32[]{:S(2)}) %collective-permute-start.23) | collective-permute-done | bytes 266272 | tf_op jit(solution)/shard_map/ppermute | solution.py:35
  114.5 7.2 %collective-permute-done.24.refs_2_ = bf16[1040,128]{1,0:T(8,128)(2,1)S(1)} collective-permute-done((bf16[1040,128]{1,0:T(8,128)(2,1)S(1)}, bf16[1040,128]{1,0:T(8,128)(2,1)S(1)}, u32[]{:S(2)}, u32[]{:S(2)}) %collective-permute-start.24) | collective-permute-done | bytes 266272 | tf_op jit(solution)/shard_map/ppermute | solution.py:35
  121.8 5.7 %collective-permute-done.25.refs_3_ = bf16[1040,128]{1,0:T(8,128)(2,1)S(1)} collective-permute-done((bf16[1040,128]{1,0:T(8,128)(2,1)S(1)}, bf16[1040,128]{1,0:T(8,128)(2,1)S(1)}, u32[]{:S(2)}, u32[]{:S(2)}) %collective-permute-start.25) | collective-permute-done | bytes 266272 | tf_op jit(solution)/shard_map/ppermute | solution.py:35
  131.4 3.6 %collective-permute-start.26 = (bf16[128,512]{1,0:T(8,128)(2,1)S(1)}, bf16[128,512]{1,0:T(8,128)(2,1)S(1)}, u32[]{:S(2)}, u32[]{:S(2)}) collective-permute-start(bf16[128,512]{1,0:T(8,128)(2,1)S(1)} %get-tuple-element.67), channel_id=1, source_target_pairs={{0,0},{1,2},{2,4},{3,6},{4,1},{5,3},{6,5},{7,7},{8,8},{9,10},{10,1... | collective-permute-start | bytes 393224 | tf_op jit(solution)/shard_map/ppermute | solution.py:35
  135.1 2.2 %shard_map.74 = (bf16[128,512]{1,0:T(8,128)(2,1)S(1)}, bf16[128,512]{1,0:T(8,128)(2,1)S(1)}) custom-call(s32[4]{0:T(128)S(1)} %pad_add_fusion.idx, bf16[4,512,128]{2,1,0:T(8,128)(2,1)S(1)} %shard_map.71.query, bf16[20,2,128,128]{3,2,1,0:T(8,128)(2,1)S(1)} %get-tuple-element.65.kv, s32[4,1,512]{2,1,0:T(1,128)S(1)} %get-tuple-element.66.start), custom_call_target="tpu_custom_call" | custom-call | flops 8589934592 | bytes 4194304 | tf_op jit(solution)/shard_map/pallas_call | solution.py:244
  137.3 2.0 %collective-permute-done.26.refs_0_ = bf16[128,512]{1,0:T(8,128)(2,1)S(1)} collective-permute-done((bf16[128,512]{1,0:T(8,128)(2,1)S(1)}, bf16[128,512]{1,0:T(8,128)(2,1)S(1)}, u32[]{:S(2)}, u32[]{:S(2)}) %collective-permute-start.26) | collective-permute-done | bytes 131104 | tf_op jit(solution)/shard_map/ppermute | solution.py:35
  140.5 3.2 %collective-permute-start.28 = (bf16[128,512]{1,0:T(8,128)(2,1)S(1)}, bf16[128,512]{1,0:T(8,128)(2,1)S(1)}, u32[]{:S(2)}, u32[]{:S(2)}) collective-permute-start(bf16[128,512]{1,0:T(8,128)(2,1)S(1)} %get-tuple-element.73), channel_id=1, source_target_pairs={{0,4},{1,6},{2,0},{3,2},{4,5},{5,7},{6,1},{7,3},{8,12},{9,14},{10,... | collective-permute-start | bytes 393224 | tf_op jit(solution)/shard_map/ppermute | solution.py:35
  143.7 1.9 %collective-permute-start.29 = (bf16[128,512]{1,0:T(8,128)(2,1)S(1)}, bf16[128,512]{1,0:T(8,128)(2,1)S(1)}, u32[]{:S(2)}, u32[]{:S(2)}) collective-permute-start(bf16[128,512]{1,0:T(8,128)(2,1)S(1)} %get-tuple-element.74), channel_id=1, source_target_pairs={{0,6},{1,4},{2,2},{3,0},{4,7},{5,5},{6,3},{7,1},{8,14},{9,12},{10,... | collective-permute-start | bytes 393224 | tf_op jit(solution)/shard_map/ppermute | solution.py:35
  146.4 4.3 %collective-permute-done.29.refs_3_ = bf16[128,512]{1,0:T(8,128)(2,1)S(1)} collective-permute-done((bf16[128,512]{1,0:T(8,128)(2,1)S(1)}, bf16[128,512]{1,0:T(8,128)(2,1)S(1)}, u32[]{:S(2)}, u32[]{:S(2)}) %collective-permute-start.29) | collective-permute-done | bytes 131104 | tf_op jit(solution)/shard_map/ppermute | solution.py:35
  (71 shorter events, 32.2 us)
Async XLA Ops:
  0.0 83.1 %copy-start.7 = (bf16[4096]{0:T(1024)(128)(2,1)S(1)}, bf16[4096]{0:T(1024)(128)(2,1)}, u32[]{:S(2)}) copy-start(bf16[4096]{0:T(1024)(128)(2,1)} %param.7) | copy-start | bytes 24580
  1.3 21.0 %collective-permute-start.3 = (bf16[128,2048]{1,0:T(8,128)(2,1)S(1)}, bf16[128,2048]{1,0:T(8,128)(2,1)S(1)}, u32[]{:S(2)}, u32[]{:S(2)}) collective-permute-start(bf16[128,2048]{1,0:T(8,128)(2,1)S(1)} %get-tuple-element.76.refs_4_), channel_id=1, source_target_pairs={{0,2},{1,3},{2,4},{3,5},{4,6},{5,7},{6,0},{7,1},{8,10},{9,11},{10,... | collective-permute-start | bytes 1572872 | tf_op jit(solution)/shard_map/ppermute | solution.py:35
  3.5 18.9 %collective-permute-start.4 = (bf16[128,2048]{1,0:T(8,128)(2,1)S(1)}, bf16[128,2048]{1,0:T(8,128)(2,1)S(1)}, u32[]{:S(2)}, u32[]{:S(2)}) collective-permute-start(bf16[128,2048]{1,0:T(8,128)(2,1)S(1)} %get-tuple-element.75.refs_8_), channel_id=1, source_target_pairs={{0,6},{1,7},{2,0},{3,1},{4,2},{5,3},{6,4},{7,5},{8,14},{9,15},{10,... | collective-permute-start | bytes 1572872 | tf_op jit(solution)/shard_map/ppermute | solution.py:35
  9.2 11.8 %collective-permute-start.1 = (bf16[32,768]{1,0:T(8,128)(2,1)S(1)}, bf16[32,768]{1,0:T(8,128)(2,1)S(1)}, u32[]{:S(2)}, u32[]{:S(2)}) collective-permute-start(bf16[32,768]{1,0:T(8,128)(2,1)S(1)} %get-tuple-element.41), channel_id=1, source_target_pairs={{0,0},{1,4},{2,2},{3,6},{4,8},{5,12},{6,10},{7,14},{8,16},{9,20},{... | collective-permute-start | bytes 147464 | tf_op jit(solution)/shard_map/ppermute | solution.py:35
  13.9 8.4 %collective-permute-start.2 = (bf16[32,768]{1,0:T(8,128)(2,1)S(1)}, bf16[32,768]{1,0:T(8,128)(2,1)S(1)}, u32[]{:S(2)}, u32[]{:S(2)}) collective-permute-start(bf16[32,768]{1,0:T(8,128)(2,1)S(1)} %get-tuple-element.42), channel_id=1, source_target_pairs={{0,2},{1,6},{2,0},{3,4},{4,10},{5,14},{6,8},{7,12},{8,18},{9,22},{... | collective-permute-start | bytes 147464 | tf_op jit(solution)/shard_map/ppermute | solution.py:35
  23.8 43.0 %all-to-all-start = ((bf16[8,64,768]{2,1,0:T(8,128)(2,1)}), bf16[8,64,768]{2,1,0:T(8,128)(2,1)}, u32[]{:S(2)}, u32[]{:S(2)}) async-start(bf16[8,64,768]{2,1,0:T(8,128)(2,1)} %broadcast_in_dim.2), calls=%async_computation | async-start | bytes 1572864 | tf_op jit(solution)/shard_map/all_to_all | solution.py:264
  33.5 32.5 %collective-permute-start.5 = (bf16[128,2048]{1,0:T(8,128)(2,1)S(1)}, bf16[128,2048]{1,0:T(8,128)(2,1)S(1)}, u32[]{:S(2)}, u32[]{:S(2)}) collective-permute-start(bf16[128,2048]{1,0:T(8,128)(2,1)S(1)} %get-tuple-element.75.refs_8_), channel_id=1, source_target_pairs={{0,2},{1,3},{2,4},{3,5},{4,6},{5,7},{6,0},{7,1},{8,10},{9,11},{10,... | collective-permute-start | bytes 1572872 | tf_op jit(solution)/shard_map/ppermute | solution.py:35
  34.2 31.8 %collective-permute-start.6 = (bf16[128,2048]{1,0:T(8,128)(2,1)S(1)}, bf16[128,2048]{1,0:T(8,128)(2,1)S(1)}, u32[]{:S(2)}, u32[]{:S(2)}) collective-permute-start(bf16[128,2048]{1,0:T(8,128)(2,1)S(1)} %get-tuple-element.76.refs_4_), channel_id=1, source_target_pairs={{0,6},{1,7},{2,0},{3,1},{4,2},{5,3},{6,4},{7,5},{8,14},{9,15},{10,... | collective-permute-start | bytes 1572872 | tf_op jit(solution)/shard_map/ppermute | solution.py:35
  36.2 43.1 %collective-permute-start.10 = (bf16[128,2048]{1,0:T(8,128)(2,1)S(1)}, bf16[128,2048]{1,0:T(8,128)(2,1)}, u32[]{:S(2)}, u32[]{:S(2)}) collective-permute-start(bf16[128,2048]{1,0:T(8,128)(2,1)S(1)} %collective-permute-done.3.refs_5_), channel_id=1, source_target_pairs={{0,2},{1,3},{2,4},{3,5},{4,6},{5,7},{6,0},{7,1},{8,10},{9,11},{10,... | collective-permute-start | bytes 1572872 | tf_op jit(solution)/shard_map/ppermute | solution.py:35
  36.2 46.9 %collective-permute-start.11 = (bf16[128,2048]{1,0:T(8,128)(2,1)S(1)}, bf16[128,2048]{1,0:T(8,128)(2,1)}, u32[]{:S(2)}, u32[]{:S(2)}) collective-permute-start(bf16[128,2048]{1,0:T(8,128)(2,1)S(1)} %collective-permute-done.4.refs_10_), channel_id=1, source_target_pairs={{0,6},{1,7},{2,0},{3,1},{4,2},{5,3},{6,4},{7,5},{8,14},{9,15},{10,... | collective-permute-start | bytes 1572872 | tf_op jit(solution)/shard_map/ppermute | solution.py:35
  38.9 2.1 %collective-permute-start = (f32[2,128]{1,0:T(2,128)S(1)}, f32[2,128]{1,0:T(2,128)S(1)}, u32[]{:S(2)}, u32[]{:S(2)}) collective-permute-start(f32[2,128]{1,0:T(2,128)S(1)} %get-tuple-element.40.squares), channel_id=1, source_target_pairs={{0,1},{1,0},{2,3},{3,2},{4,5},{5,4},{6,7},{7,6},{8,9},{9,8},{10,11... | collective-permute-start | bytes 3080 | tf_op jit(solution)/shard_map/ppermute | solution.py:35
  41.0 18.6 %collective-permute-start.7 = (f32[4,128]{1,0:T(4,128)S(1)}, f32[4,128]{1,0:T(4,128)S(1)}, u32[]{:S(2)}, u32[]{:S(2)}) collective-permute-start(f32[4,128]{1,0:T(4,128)S(1)} %shard_map.65.refs_0_), channel_id=1, source_target_pairs={{0,2},{1,3},{2,4},{3,5},{4,6},{5,7},{6,0},{7,1},{8,10},{9,11},{10,... | collective-permute-start | bytes 6152 | tf_op jit(solution)/shard_map/ppermute | solution.py:35
  59.6 3.9 %collective-permute-start.8 = (f32[4,128]{1,0:T(4,128)S(1)}, f32[4,128]{1,0:T(4,128)S(1)}, u32[]{:S(2)}, u32[]{:S(2)}) collective-permute-start(f32[4,128]{1,0:T(4,128)S(1)} %shard_map.65.refs_0_), channel_id=1, source_target_pairs={{0,4},{1,5},{2,6},{3,7},{4,0},{5,1},{6,2},{7,3},{8,12},{9,13},{10,... | collective-permute-start | bytes 6152 | tf_op jit(solution)/shard_map/ppermute | solution.py:35
  63.6 2.4 %collective-permute-start.9 = (f32[4,128]{1,0:T(4,128)S(1)}, f32[4,128]{1,0:T(4,128)S(1)}, u32[]{:S(2)}, u32[]{:S(2)}) collective-permute-start(f32[4,128]{1,0:T(4,128)S(1)} %shard_map.65.refs_0_), channel_id=1, source_target_pairs={{0,6},{1,7},{2,0},{3,1},{4,2},{5,3},{6,4},{7,5},{8,14},{9,15},{10,... | collective-permute-start | bytes 6152 | tf_op jit(solution)/shard_map/ppermute | solution.py:35
  67.8 8.5 %collective-permute-start.12 = (bf16[512,256]{1,0:T(8,128)(2,1)S(1)}, bf16[512,256]{1,0:T(8,128)(2,1)S(1)}, u32[]{:S(2)}, u32[]{:S(2)}) collective-permute-start(bf16[512,256]{1,0:T(8,128)(2,1)S(1)} %slice.26.own), channel_id=1, source_target_pairs={{0,8},{1,9},{2,10},{3,11},{4,12},{5,13},{6,14},{7,15},{8,16},{9,17... | collective-permute-start | bytes 786440 | tf_op jit(solution)/shard_map/ppermute | solution.py:35
  70.2 6.1 %collective-permute-start.13 = (bf16[512,256]{1,0:T(8,128)(2,1)S(1)}, bf16[512,256]{1,0:T(8,128)(2,1)S(1)}, u32[]{:S(2)}, u32[]{:S(2)}) collective-permute-start(bf16[512,256]{1,0:T(8,128)(2,1)S(1)} %slice.26.own), channel_id=1, source_target_pairs={{0,24},{1,25},{2,26},{3,27},{4,28},{5,29},{6,30},{7,31},{8,0},{9,1... | collective-permute-start | bytes 786440 | tf_op jit(solution)/shard_map/ppermute | solution.py:35
  76.3 20.4 %collective-permute-start.17 = (bf16[512,512]{1,0:T(8,128)(2,1)S(1)}, bf16[512,512]{1,0:T(8,128)(2,1)S(1)}, u32[]{:S(2)}, u32[]{:S(2)}) collective-permute-start(bf16[512,512]{1,0:T(8,128)(2,1)S(1)} %slice.27.own), channel_id=1, source_target_pairs={{0,8},{1,9},{2,10},{3,11},{4,12},{5,13},{6,14},{7,15},{8,16},{9,17... | collective-permute-start | bytes 1572872 | tf_op jit(solution)/shard_map/ppermute | solution.py:35
  77.5 20.4 %collective-permute-start.18 = (bf16[512,512]{1,0:T(8,128)(2,1)S(1)}, bf16[512,512]{1,0:T(8,128)(2,1)S(1)}, u32[]{:S(2)}, u32[]{:S(2)}) collective-permute-start(bf16[512,512]{1,0:T(8,128)(2,1)S(1)} %slice.27.own), channel_id=1, source_target_pairs={{0,24},{1,25},{2,26},{3,27},{4,28},{5,29},{6,30},{7,31},{8,0},{9,1... | collective-permute-start | bytes 1572872 | tf_op jit(solution)/shard_map/ppermute | solution.py:35
  79.1 10.9 %collective-permute-start.14 = (bf16[256,256]{1,0:T(8,128)(2,1)S(1)}, bf16[256,256]{1,0:T(8,128)(2,1)S(1)}, u32[]{:S(2)}, u32[]{:S(2)}) collective-permute-start(bf16[256,256]{1,0:T(8,128)(2,1)S(1)} %slice.32), channel_id=1, source_target_pairs={{0,8},{1,9},{2,10},{3,11},{4,12},{5,13},{6,14},{7,15},{8,16},{9,17... | collective-permute-start | bytes 393224 | tf_op jit(solution)/shard_map/ppermute | solution.py:35
  79.4 10.6 %collective-permute-start.15 = (bf16[256,256]{1,0:T(8,128)(2,1)S(1)}, bf16[256,256]{1,0:T(8,128)(2,1)S(1)}, u32[]{:S(2)}, u32[]{:S(2)}) collective-permute-start(bf16[256,256]{1,0:T(8,128)(2,1)S(1)} %slice.33), channel_id=1, source_target_pairs={{0,24},{1,25},{2,26},{3,27},{4,28},{5,29},{6,30},{7,31},{8,0},{9,1... | collective-permute-start | bytes 393224 | tf_op jit(solution)/shard_map/ppermute | solution.py:35
  91.8 7.8 %collective-permute-start.16 = (f32[512,256]{1,0:T(8,128)S(1)}, f32[512,256]{1,0:T(8,128)S(1)}, u32[]{:S(2)}, u32[]{:S(2)}) collective-permute-start(f32[512,256]{1,0:T(8,128)S(1)} %get-tuple-element.57), channel_id=1, source_target_pairs={{0,1},{1,0},{2,3},{3,2},{4,5},{5,4},{6,7},{7,6},{8,9},{9,8},{10,11... | collective-permute-start | bytes 1572872 | tf_op jit(solution)/shard_map/ppermute | solution.py:35
  96.7 9.2 %collective-permute-start.19 = (bf16[256,512]{1,0:T(8,128)(2,1)S(1)}, bf16[256,512]{1,0:T(8,128)(2,1)S(1)}, u32[]{:S(2)}, u32[]{:S(2)}) collective-permute-start(bf16[256,512]{1,0:T(8,128)(2,1)S(1)} %slice.34), channel_id=1, source_target_pairs={{0,8},{1,9},{2,10},{3,11},{4,12},{5,13},{6,14},{7,15},{8,16},{9,17... | collective-permute-start | bytes 786440 | tf_op jit(solution)/shard_map/ppermute | solution.py:35
  97.9 8.2 %collective-permute-start.20 = (bf16[256,512]{1,0:T(8,128)(2,1)S(1)}, bf16[256,512]{1,0:T(8,128)(2,1)S(1)}, u32[]{:S(2)}, u32[]{:S(2)}) collective-permute-start(bf16[256,512]{1,0:T(8,128)(2,1)S(1)} %slice.35), channel_id=1, source_target_pairs={{0,24},{1,25},{2,26},{3,27},{4,28},{5,29},{6,30},{7,31},{8,0},{9,1... | collective-permute-start | bytes 786440 | tf_op jit(solution)/shard_map/ppermute | solution.py:35
  100.5 10.7 %collective-permute-start.22 = (bf16[1040,128]{1,0:T(8,128)(2,1)S(1)}, bf16[1040,128]{1,0:T(8,128)(2,1)S(1)}, u32[]{:S(2)}, u32[]{:S(2)}) collective-permute-start(bf16[1040,128]{1,0:T(8,128)(2,1)S(1)} %shard_map.69.refs_4_), channel_id=1, source_target_pairs={{0,32},{1,33},{2,34},{3,35},{4,36},{5,37},{6,38},{7,39},{8,40},{9,... | collective-permute-start | bytes 798728 | tf_op jit(solution)/shard_map/ppermute | solution.py:35
  101.9 12.6 %collective-permute-start.23 = (bf16[1040,128]{1,0:T(8,128)(2,1)S(1)}, bf16[1040,128]{1,0:T(8,128)(2,1)S(1)}, u32[]{:S(2)}, u32[]{:S(2)}) collective-permute-start(bf16[1040,128]{1,0:T(8,128)(2,1)S(1)} %shard_map.69.refs_4_), channel_id=1, source_target_pairs={{0,24},{1,25},{2,26},{3,27},{4,28},{5,29},{6,30},{7,31},{8,32},{9,... | collective-permute-start | bytes 798728 | tf_op jit(solution)/shard_map/ppermute | solution.py:35
  103.4 18.4 %collective-permute-start.24 = (bf16[1040,128]{1,0:T(8,128)(2,1)S(1)}, bf16[1040,128]{1,0:T(8,128)(2,1)S(1)}, u32[]{:S(2)}, u32[]{:S(2)}) collective-permute-start(bf16[1040,128]{1,0:T(8,128)(2,1)S(1)} %shard_map.69.refs_4_), channel_id=1, source_target_pairs={{0,16},{1,17},{2,18},{3,19},{4,20},{5,21},{6,22},{7,23},{8,24},{9,... | collective-permute-start | bytes 798728 | tf_op jit(solution)/shard_map/ppermute | solution.py:35
  105.9 21.5 %collective-permute-start.25 = (bf16[1040,128]{1,0:T(8,128)(2,1)S(1)}, bf16[1040,128]{1,0:T(8,128)(2,1)S(1)}, u32[]{:S(2)}, u32[]{:S(2)}) collective-permute-start(bf16[1040,128]{1,0:T(8,128)(2,1)S(1)} %shard_map.69.refs_4_), channel_id=1, source_target_pairs={{0,8},{1,9},{2,10},{3,11},{4,12},{5,13},{6,14},{7,15},{8,16},{9,17... | collective-permute-start | bytes 798728 | tf_op jit(solution)/shard_map/ppermute | solution.py:35
  109.2 19.7 %collective-permute-start.21 = (f32[512,512]{1,0:T(8,128)S(1)}, f32[512,512]{1,0:T(8,128)S(1)}, u32[]{:S(2)}, u32[]{:S(2)}) collective-permute-start(f32[512,512]{1,0:T(8,128)S(1)} %get-tuple-element.63), channel_id=1, source_target_pairs={{0,1},{1,0},{2,3},{3,2},{4,5},{5,4},{6,7},{7,6},{8,9},{9,8},{10,11... | collective-permute-start | bytes 3145736 | tf_op jit(solution)/shard_map/ppermute | solution.py:35
  131.4 7.9 %collective-permute-start.26 = (bf16[128,512]{1,0:T(8,128)(2,1)S(1)}, bf16[128,512]{1,0:T(8,128)(2,1)S(1)}, u32[]{:S(2)}, u32[]{:S(2)}) collective-permute-start(bf16[128,512]{1,0:T(8,128)(2,1)S(1)} %get-tuple-element.67), channel_id=1, source_target_pairs={{0,0},{1,2},{2,4},{3,6},{4,1},{5,3},{6,5},{7,7},{8,8},{9,10},{10,1... | collective-permute-start | bytes 393224 | tf_op jit(solution)/shard_map/ppermute | solution.py:35
  135.0 5.5 %collective-permute-start.27 = (bf16[128,512]{1,0:T(8,128)(2,1)S(1)}, bf16[128,512]{1,0:T(8,128)(2,1)S(1)}, u32[]{:S(2)}, u32[]{:S(2)}) collective-permute-start(bf16[128,512]{1,0:T(8,128)(2,1)S(1)} %get-tuple-element.68), channel_id=1, source_target_pairs={{0,2},{1,0},{2,6},{3,4},{4,3},{5,1},{6,7},{7,5},{8,10},{9,8},{10,1... | collective-permute-start | bytes 393224 | tf_op jit(solution)/shard_map/ppermute | solution.py:35
  140.5 5.8 %collective-permute-start.28 = (bf16[128,512]{1,0:T(8,128)(2,1)S(1)}, bf16[128,512]{1,0:T(8,128)(2,1)S(1)}, u32[]{:S(2)}, u32[]{:S(2)}) collective-permute-start(bf16[128,512]{1,0:T(8,128)(2,1)S(1)} %get-tuple-element.73), channel_id=1, source_target_pairs={{0,4},{1,6},{2,0},{3,2},{4,5},{5,7},{6,1},{7,3},{8,12},{9,14},{10,... | collective-permute-start | bytes 393224 | tf_op jit(solution)/shard_map/ppermute | solution.py:35
  143.7 6.9 %collective-permute-start.29 = (bf16[128,512]{1,0:T(8,128)(2,1)S(1)}, bf16[128,512]{1,0:T(8,128)(2,1)S(1)}, u32[]{:S(2)}, u32[]{:S(2)}) collective-permute-start(bf16[128,512]{1,0:T(8,128)(2,1)S(1)} %get-tuple-element.74), channel_id=1, source_target_pairs={{0,6},{1,4},{2,2},{3,0},{4,7},{5,5},{6,3},{7,1},{8,14},{9,12},{10,... | collective-permute-start | bytes 393224 | tf_op jit(solution)/shard_map/ppermute | solution.py:35
  (7 other events, 46.3 us)
where the time goes:
time: 153 us; the launch traced here: 152 us
  waiting for transfers between devices  63 us (41%)
  starting transfers between devices  61 us (40%)
  Pallas kernels  17 us (11%)
  local copies, waits for them, and re-layouts  9.72 us (6%)
    ppermute x30, waiting for transfers between devices, permute(): return lax.ppermute(value, AXES, pairs)  63 us
    ppermute x30, starting transfers between devices, permute(): return lax.ppermute(value, AXES, pairs)  51.3 us
    pallas_call x12, Pallas kernels, call(): pl.pallas_call(kernel, out_shape=shapes, in_specs=[SMEM] * smem + [VMEM]...  17 us
    all_to_all x1, starting transfers between devices, copies(): lax.all_to_all(jnp.broadcast_to(value[None], (count, *value.shape)), axis...  9.7 us
    unnamed x16, local copies, waits for them, and re-layouts  5.33 us
  transfers between devices with their start and end apart: 31, of which 16 were waited for; matrix products, arithmetic and copies ran while one was open for 2% of the time, Pallas kernels for 8%

commit v1 on v0

--- a/solution.py
+++ b/solution.py
@@ -1,5 +1,3 @@
-import functools
-
 import jax
 import jax.numpy as jnp
 from jax import lax
@@ -83,8 +81,9 @@
 
 def tell_kernel(squares, others, docs, out):
     scale = lax.rsqrt((squares[...] + others[...]) * (1.0 / WIDTH) + EPS)
-    out[0:2, :] = docs[...].astype(F32)
-    out[2:4, :] = scale
+    for n in range(NX):
+        out[n, 0:2, :] = docs[...].astype(F32)
+        out[n, 2:4, :] = scale
 
 
 def merge_kernel(idx, first, second, out):
@@ -94,15 +93,15 @@
     out[32:, :] = jnp.where(odd, top, low).astype(BF)
 
 
-def norm_kernel(idx, gain, *refs):
-    told, hidden, x_all = refs[:4], refs[4:12], refs[12]
+def norm_kernel(idx, told, gain, *refs):
+    hidden, x_all = refs[:8], refs[8]
     x, c = idx[2], idx[3]
     g = gain[:, pl.ds(pl.multiple_of(c * HALF, HALF), HALF)].astype(F32)
     for n, ref in enumerate(hidden):
         s, d = n // 4, (0, -1, 1, 2)[n % 4]
         chip = lax.rem(x + d + NX, NX)
         base = jnp.where(c == s, 0, 512) + chip * 128
-        scale = jnp.broadcast_to(told[-d % NX][2 + s : 3 + s, :], (HD, HD)).T
+        scale = jnp.broadcast_to(told[chip, 2 + s : 3 + s, :], (HD, HD)).T
         for t in range(4):
             rows = slice(t * 32, t * 32 + 32)
             wide = ref[rows, :].astype(F32) * scale[rows, :1] * g
@@ -137,20 +136,15 @@
     return value * cosine + pltpu.roll(value, 64, 1) * sine
 
 
-def rotate_kv_kernel(idx, keep, got, cos, sin, *refs):
-    told, kv = refs[:4], refs[4]
+def rotate_kv_kernel(idx, keep, got, cos, sin, told, kv):
     for i in range(4):
         rows = slice(i * 128, i * 128 + 128)
         value = keep[rows, :] + got[rows, :]
         at = i * 256
         kv[at : at + 128, :] = turned(value[:, :128], cos[rows, :], sin[rows, :]).astype(BF)
         kv[at + 128 : at + 256, :] = value[:, 128:].T.astype(BF)
-    docs = jnp.zeros((16, HD), F32)
-    row = lax.broadcasted_iota(jnp.int32, (16, HD), 0)
-    for n in range(NX):
-        piece = jnp.where(idx[3] == 0, told[n][0:1, :], told[n][1:2, :])
-        docs = jnp.where(row == lax.rem(idx[2] - n + NX, NX), piece, docs)
-    kv[1024:1040, :] = docs.astype(BF)
+    docs = jnp.where(idx[3] == 0, told[:, 0, :], told[:, 1, :])
+    kv[1024:1040, :] = jnp.concatenate([docs, jnp.zeros((12, HD), F32)], axis=0).astype(BF)
 
 
 def rotate_q_kernel(keep, got, cos, sin, query):
@@ -228,8 +222,9 @@
         start[i] = jnp.concatenate([row] * 4, axis=1)
 
 
-def attend_kernel(part, idx, query, kv, start, out0, out1, scores, acc):
-    attend(idx, query, start, kv, scores, acc, (out0, out1), part)
+def attend_kernel(idx, query, kv, start, out0, out1, out2, out3, scores, acc):
+    attend(idx, query, start, kv, scores, acc, (out0, out1), 0)
+    attend(idx, query, start, kv, scores, acc, (out2, out3), 1)
 
 
 def place_kernel(idx, *refs):
@@ -286,18 +281,17 @@
     others = permute(squares, lambda z, y, x, c: (z, y, x, 1 - c))
     told = call(
         tell_kernel,
-        shape((4, HD), F32),
+        shape((NX, 4, HD), F32),
         (squares, others, doc_ids),
         cost=cost(0, 1 << 14),
         smem=0,
     )
-    told1, told2, told3 = (along_x(told, n) for n in (1, 2, 3))
+    told = lax.all_to_all(told, "x", 0, 0, tiled=True)
     first, second, right_a, left_b = tie(first, second, right_a, left_b)
     far_a, far_b = along_x(right_a, 1), along_x(left_b, -1)
     rows = call(merge_kernel, shape((64, COLS), BF), (where, first, second), cost=cost(0, 1 << 18))
     w_z = copies(rows, "z", NZ).reshape(512, COLS)
-    w_z, right_b, left_a, told1, told2, told3 = tie(w_z, right_b, left_a, told1, told2, told3)
-    told = (told, told1, told2, told3)
+    w_z, right_b, left_a, told = tie(w_z, right_b, left_a, told)
     around = []
     for cols in (slice(512, COLS), slice(0, 512)):
         own = w_z[:, cols]
@@ -309,7 +303,7 @@
     x_all = call(
         norm_kernel,
         shape((1024, HALF), BF),
-        (where, norm_gain.reshape(1, WIDTH), *told)
+        (where, told, norm_gain.reshape(1, WIDTH))
         + (seq_a, right_a, left_a, far_a, seq_b, right_b, left_b, far_b),
         cost=cost(1 << 22, 8 << 20),
     )
@@ -331,7 +325,7 @@
     own = call(
         rotate_kv_kernel,
         shape((ROWS, HD), BF),
-        (where, keep, got, cos, sin, *told),
+        (where, keep, got, cos, sin, told),
         cost=cost(1 << 20, 2 << 20),
     )
     x_all, own = tie(x_all, own)
@@ -362,24 +356,17 @@
         cost(1 << 36, 4 << 20),
     )
     block = shape((128, 512), BF)
-
-    def blocks(part, flops):
-        return call(
-            functools.partial(attend_kernel, part),
-            (block, block),
-            (where, query, kv, start),
-            (pltpu.VMEM((2560, 1024), F32), pltpu.VMEM((HD, 1024), F32)),
-            cost(flops, 4 << 20),
-            mib=24,
-        )
-
-    out0, out1 = blocks(0, 1 << 30)
-    out0, out1 = permute(out0, back(0)), permute(out1, back(1))
-    out2, out3 = blocks(1, 1 << 33)
-    out0, out1, out2, out3 = tie(out0, out1, out2, out3)
-    out2, out3 = permute(out2, back(2)), permute(out3, back(3))
+    outs = call(
+        attend_kernel,
+        (block,) * 4,
+        (where, query, kv, start),
+        (pltpu.VMEM((2560, 1024), F32), pltpu.VMEM((HD, 1024), F32)),
+        cost(1 << 31, 4 << 20),
+        mib=24,
+    )
+    outs = [permute(out, back(k)) for k, out in enumerate(outs)]
     return call(
-        place_kernel, shape((2, 128, 1024), BF), (where, out0, out1, out2, out3), cost=cost(0, 1 << 20)
+        place_kernel, shape((2, 128, 1024), BF), (where, *outs), cost=cost(0, 1 << 20)
     )
 
 

time: 153 us -> 141 us (0.922)
  the two profiles are of different devices: /device:TPU:1 before, /device:TPU:64 now
where the time goes in v1:
time: 141 us; the launch traced here: 140 us
  starting transfers between devices  56 us (40%)
  waiting for transfers between devices  49.8 us (35%)
  Pallas kernels  22.1 us (16%)
  local copies, waits for them, and re-layouts  10.4 us (7%)
    ppermute x27, waiting for transfers between devices, permute(): return lax.ppermute(value, AXES, pairs)  43.9 us
    ppermute x27, starting transfers between devices, permute(): return lax.ppermute(value, AXES, pairs)  42.4 us
    pallas_call x11, Pallas kernels, call(): pl.pallas_call(kernel, out_shape=shapes, in_specs=[SMEM] * smem + [VMEM]...  22.1 us
    all_to_all x1, starting transfers between devices, copies(): lax.all_to_all(jnp.broadcast_to(value[None], (count, *value.shape)), axis...  9.36 us
    unnamed x16, local copies, waits for them, and re-layouts  6.01 us
    all_to_all x1, waiting for transfers between devices, local(): told = lax.all_to_all(told, 'x', 0, 0, tiled=True)  4.71 us
    all_to_all x1, starting transfers between devices, local(): told = lax.all_to_all(told, 'x', 0, 0, tiled=True)  4.2 us
  transfers between devices with their start and end apart: 29, of which 14 were waited for; matrix products, arithmetic and copies ran while one was open for 2% of the time, Pallas kernels for 8%

profile of v1, /device:TPU:64, one launch (start us, length us, event | category | flops | bytes accessed | tf_op | source)
XLA Modules:
  0.0 139.6 jit_solution(3855882006500466710)
XLA Ops:
  1.3 1.6 %collective-permute-start.2 = (bf16[128,2048]{1,0:T(8,128)(2,1)S(1)}, bf16[128,2048]{1,0:T(8,128)(2,1)S(1)}, u32[]{:S(2)}, u32[]{:S(2)}) collective-permute-start(bf16[128,2048]{1,0:T(8,128)(2,1)S(1)} %get-tuple-element.64.refs_0_), channel_id=1, source_target_pairs={{0,2},{1,3},{2,4},{3,5},{4,6},{5,7},{6,0},{7,1},{8,10},{9,11},{10,... | collective-permute-start | bytes 1572872 | tf_op jit(solution)/shard_map/ppermute | solution.py:33
  2.9 1.7 %collective-permute-start.3 = (bf16[128,2048]{1,0:T(8,128)(2,1)S(1)}, bf16[128,2048]{1,0:T(8,128)(2,1)S(1)}, u32[]{:S(2)}, u32[]{:S(2)}) collective-permute-start(bf16[128,2048]{1,0:T(8,128)(2,1)S(1)} %get-tuple-element.63.refs_4_), channel_id=1, source_target_pairs={{0,6},{1,7},{2,0},{3,1},{4,2},{5,3},{6,4},{7,5},{8,14},{9,15},{10,... | collective-permute-start | bytes 1572872 | tf_op jit(solution)/shard_map/ppermute | solution.py:33
  9.0 6.4 %collective-permute-start = (bf16[32,768]{1,0:T(8,128)(2,1)S(1)}, bf16[32,768]{1,0:T(8,128)(2,1)S(1)}, u32[]{:S(2)}, u32[]{:S(2)}) collective-permute-start(bf16[32,768]{1,0:T(8,128)(2,1)S(1)} %get-tuple-element.34), channel_id=1, source_target_pairs={{0,0},{1,4},{2,2},{3,6},{4,8},{5,12},{6,10},{7,14},{8,16},{9,20},{... | collective-permute-start | bytes 147464 | tf_op jit(solution)/shard_map/ppermute | solution.py:33
  15.6 1.5 %collective-permute-start.6 = (f32[2,128]{1,0:T(2,128)S(1)}, f32[2,128]{1,0:T(2,128)S(1)}, u32[]{:S(2)}, u32[]{:S(2)}) collective-permute-start(f32[2,128]{1,0:T(2,128)S(1)} %get-tuple-element.38.squares), channel_id=1, source_target_pairs={{0,1},{1,0},{2,3},{3,2},{4,5},{5,4},{6,7},{7,6},{8,9},{9,8},{10,11... | collective-permute-start | bytes 3080 | tf_op jit(solution)/shard_map/ppermute | solution.py:33
  19.1 4.2 %all-to-all-start.1 = ((f32[4,4,128]{2,1,0:T(4,128)}), f32[4,4,128]{2,1,0:T(4,128)S(1)}, u32[]{:S(2)}, u32[]{:S(2)}) async-start(f32[4,4,128]{2,1,0:T(4,128)} %shard_map.66), calls=%async_computation.1 | async-start | bytes 16384 | tf_op jit(solution)/shard_map/all_to_all | solution.py:289
  23.9 4.7 %all-to-all-done.1.told = f32[4,4,128]{2,1,0:T(4,128)S(1)} async-done(((f32[4,4,128]{2,1,0:T(4,128)}), f32[4,4,128]{2,1,0:T(4,128)S(1)}, u32[]{:S(2)}, u32[]{:S(2)}) %all-to-all-start.1) | async-done | bytes 8224 | tf_op jit(solution)/shard_map/all_to_all | solution.py:289
  29.6 9.4 %all-to-all-start = ((bf16[8,64,768]{2,1,0:T(8,128)(2,1)}), bf16[8,64,768]{2,1,0:T(8,128)(2,1)}, u32[]{:S(2)}, u32[]{:S(2)}) async-start(bf16[8,64,768]{2,1,0:T(8,128)(2,1)} %broadcast_in_dim.2), calls=%async_computation | async-start | bytes 1572864 | tf_op jit(solution)/shard_map/all_to_all | solution.py:259
  39.5 2.7 %collective-permute-start.5 = (bf16[128,2048]{1,0:T(8,128)(2,1)S(1)}, bf16[128,2048]{1,0:T(8,128)(2,1)S(1)}, u32[]{:S(2)}, u32[]{:S(2)}) collective-permute-start(bf16[128,2048]{1,0:T(8,128)(2,1)S(1)} %get-tuple-element.64.refs_0_), channel_id=1, source_target_pairs={{0,6},{1,7},{2,0},{3,1},{4,2},{5,3},{6,4},{7,5},{8,14},{9,15},{10,... | collective-permute-start | bytes 1572872 | tf_op jit(solution)/shard_map/ppermute | solution.py:33
  42.2 3.2 %collective-permute-start.8 = (bf16[128,2048]{1,0:T(8,128)(2,1)S(1)}, bf16[128,2048]{1,0:T(8,128)(2,1)}, u32[]{:S(2)}, u32[]{:S(2)}) collective-permute-start(bf16[128,2048]{1,0:T(8,128)(2,1)S(1)} %collective-permute-done.3.refs_6_), channel_id=1, source_target_pairs={{0,6},{1,7},{2,0},{3,1},{4,2},{5,3},{6,4},{7,5},{8,14},{9,15},{10,... | collective-permute-start | bytes 1572872 | tf_op jit(solution)/shard_map/ppermute | solution.py:33
  45.4 9.6 %collective-permute-done.4.refs_5_ = bf16[128,2048]{1,0:T(8,128)(2,1)S(1)} collective-permute-done((bf16[128,2048]{1,0:T(8,128)(2,1)S(1)}, bf16[128,2048]{1,0:T(8,128)(2,1)S(1)}, u32[]{:S(2)}, u32[]{:S(2)}) %collective-permute-start.4) | collective-permute-done | bytes 524320 | tf_op jit(solution)/shard_map/ppermute | solution.py:33
  58.0 2.0 %collective-permute-start.9 = (bf16[512,256]{1,0:T(8,128)(2,1)S(1)}, bf16[512,256]{1,0:T(8,128)(2,1)S(1)}, u32[]{:S(2)}, u32[]{:S(2)}) collective-permute-start(bf16[512,256]{1,0:T(8,128)(2,1)S(1)} %slice.26.own), channel_id=1, source_target_pairs={{0,8},{1,9},{2,10},{3,11},{4,12},{5,13},{6,14},{7,15},{8,16},{9,17... | collective-permute-start | bytes 786440 | tf_op jit(solution)/shard_map/ppermute | solution.py:33
  62.4 3.2 %collective-permute-done.9.up = bf16[512,256]{1,0:T(8,128)(2,1)S(1)} collective-permute-done((bf16[512,256]{1,0:T(8,128)(2,1)S(1)}, bf16[512,256]{1,0:T(8,128)(2,1)S(1)}, u32[]{:S(2)}, u32[]{:S(2)}) %collective-permute-start.9) | collective-permute-done | bytes 262176 | tf_op jit(solution)/shard_map/ppermute | solution.py:33
  66.5 3.2 %collective-permute-start.15 = (bf16[512,512]{1,0:T(8,128)(2,1)S(1)}, bf16[512,512]{1,0:T(8,128)(2,1)S(1)}, u32[]{:S(2)}, u32[]{:S(2)}) collective-permute-start(bf16[512,512]{1,0:T(8,128)(2,1)S(1)} %slice.27.own), channel_id=1, source_target_pairs={{0,24},{1,25},{2,26},{3,27},{4,28},{5,29},{6,30},{7,31},{8,0},{9,1... | collective-permute-start | bytes 1572872 | tf_op jit(solution)/shard_map/ppermute | solution.py:33
  69.9 3.5 %collective-permute-start.12 = (bf16[256,256]{1,0:T(8,128)(2,1)S(1)}, bf16[256,256]{1,0:T(8,128)(2,1)S(1)}, u32[]{:S(2)}, u32[]{:S(2)}) collective-permute-start(bf16[256,256]{1,0:T(8,128)(2,1)S(1)} %slice.33), channel_id=1, source_target_pairs={{0,24},{1,25},{2,26},{3,27},{4,28},{5,29},{6,30},{7,31},{8,0},{9,1... | collective-permute-start | bytes 393224 | tf_op jit(solution)/shard_map/ppermute | solution.py:33
  75.5 2.4 %shard_map.67.x_all = bf16[1024,2048]{1,0:T(8,128)(2,1)S(1)} custom-call(s32[4]{0:T(128)S(1)} %pad_add_fusion.idx, f32[4,4,128]{2,1,0:T(4,128)S(1)} %all-to-all-done.1.told, bf16[1,4096]{1,0:T(2,128)(2,1)S(1)} %reshape.19.gain, bf16[128,2048]{1,0:T(8,128)(2,1)S(1)} %get-tuple-element.64.refs_0_, bf16[128,2048]{1,0:T(8,128)(2,1)S(1)} %collective-permute-done.2.refs_1_, ...), custom_call_target="tpu_custom_call" | custom-call | flops 4194304 | bytes 8388608 | tf_op jit(solution)/shard_map/pallas_call | solution.py:239
  77.8 3.4 %collective-permute-done.11.far_up = bf16[256,256]{1,0:T(8,128)(2,1)S(1)} collective-permute-done((bf16[256,256]{1,0:T(8,128)(2,1)S(1)}, bf16[256,256]{1,0:T(8,128)(2,1)S(1)}, u32[]{:S(2)}, u32[]{:S(2)}) %collective-permute-start.11) | collective-permute-done | bytes 131104 | tf_op jit(solution)/shard_map/ppermute | solution.py:33
  81.2 1.9 %shard_map.68 = (f32[512,256]{1,0:T(8,128)S(1)}, f32[512,256]{1,0:T(8,128)S(1)}) custom-call(s32[4]{0:T(128)S(1)} %pad_add_fusion.idx, bf16[1024,2048]{1,0:T(8,128)(2,1)S(1)} %shard_map.67.x_all, bf16[512,256]{1,0:T(8,128)(2,1)S(1)} %slice.26.own, bf16[512,256]{1,0:T(8,128)(2,1)S(1)} %collective-permute-done.9.up, ...), custom_call_target="tpu_custom_call" | custom-call | flops 1073741824 | bytes 10485760 | tf_op jit(solution)/shard_map/pallas_call | solution.py:239
  83.6 3.0 %collective-permute-start.17 = (bf16[256,512]{1,0:T(8,128)(2,1)S(1)}, bf16[256,512]{1,0:T(8,128)(2,1)S(1)}, u32[]{:S(2)}, u32[]{:S(2)}) collective-permute-start(bf16[256,512]{1,0:T(8,128)(2,1)S(1)} %slice.35), channel_id=1, source_target_pairs={{0,24},{1,25},{2,26},{3,27},{4,28},{5,29},{6,30},{7,31},{8,0},{9,1... | collective-permute-start | bytes 786440 | tf_op jit(solution)/shard_map/ppermute | solution.py:33
  88.2 1.7 %collective-permute-start.20 = (bf16[1040,128]{1,0:T(8,128)(2,1)S(1)}, bf16[1040,128]{1,0:T(8,128)(2,1)S(1)}, u32[]{:S(2)}, u32[]{:S(2)}) collective-permute-start(bf16[1040,128]{1,0:T(8,128)(2,1)S(1)} %shard_map.69.refs_4_), channel_id=1, source_target_pairs={{0,24},{1,25},{2,26},{3,27},{4,28},{5,29},{6,30},{7,31},{8,32},{9,... | collective-permute-start | bytes 798728 | tf_op jit(solution)/shard_map/ppermute | solution.py:33
  90.6 2.6 %collective-permute-done.16.far_up = bf16[256,512]{1,0:T(8,128)(2,1)S(1)} collective-permute-done((bf16[256,512]{1,0:T(8,128)(2,1)S(1)}, bf16[256,512]{1,0:T(8,128)(2,1)S(1)}, u32[]{:S(2)}, u32[]{:S(2)}) %collective-permute-start.16) | collective-permute-done | bytes 262176 | tf_op jit(solution)/shard_map/ppermute | solution.py:33
  93.2 3.6 %collective-permute-done.17.far_down = bf16[256,512]{1,0:T(8,128)(2,1)S(1)} collective-permute-done((bf16[256,512]{1,0:T(8,128)(2,1)S(1)}, bf16[256,512]{1,0:T(8,128)(2,1)S(1)}, u32[]{:S(2)}, u32[]{:S(2)}) %collective-permute-start.17) | collective-permute-done | bytes 262176 | tf_op jit(solution)/shard_map/ppermute | solution.py:33
  96.8 3.1 %shard_map.70 = (f32[512,512]{1,0:T(8,128)S(1)}, f32[512,512]{1,0:T(8,128)S(1)}) custom-call(s32[4]{0:T(128)S(1)} %pad_add_fusion.idx, bf16[1024,2048]{1,0:T(8,128)(2,1)S(1)} %shard_map.67.x_all, bf16[512,512]{1,0:T(8,128)(2,1)S(1)} %slice.27.own, bf16[512,512]{1,0:T(8,128)(2,1)S(1)} %collective-permute-done.14.up, ...), custom_call_target="tpu_custom_call" | custom-call | flops 2147483648 | bytes 10485760 | tf_op jit(solution)/shard_map/pallas_call | solution.py:239
  100.2 3.8 %collective-permute-done.20.refs_1_ = bf16[1040,128]{1,0:T(8,128)(2,1)S(1)} collective-permute-done((bf16[1040,128]{1,0:T(8,128)(2,1)S(1)}, bf16[1040,128]{1,0:T(8,128)(2,1)S(1)}, u32[]{:S(2)}, u32[]{:S(2)}) %collective-permute-start.20) | collective-permute-done | bytes 266272 | tf_op jit(solution)/shard_map/ppermute | solution.py:33
  104.0 5.9 %collective-permute-done.21.refs_2_ = bf16[1040,128]{1,0:T(8,128)(2,1)S(1)} collective-permute-done((bf16[1040,128]{1,0:T(8,128)(2,1)S(1)}, bf16[1040,128]{1,0:T(8,128)(2,1)S(1)}, u32[]{:S(2)}, u32[]{:S(2)}) %collective-permute-start.21) | collective-permute-done | bytes 266272 | tf_op jit(solution)/shard_map/ppermute | solution.py:33
  109.8 5.7 %collective-permute-done.22.refs_3_ = bf16[1040,128]{1,0:T(8,128)(2,1)S(1)} collective-permute-done((bf16[1040,128]{1,0:T(8,128)(2,1)S(1)}, bf16[1040,128]{1,0:T(8,128)(2,1)S(1)}, u32[]{:S(2)}, u32[]{:S(2)}) %collective-permute-start.22) | collective-permute-done | bytes 266272 | tf_op jit(solution)/shard_map/ppermute | solution.py:33
  115.6 1.4 %shard_map.72 = (bf16[20,2,128,128]{3,2,1,0:T(8,128)(2,1)S(1)}, s32[4,1,512]{2,1,0:T(1,128)S(1)}) custom-call(s32[4]{0:T(128)S(1)} %pad_add_fusion.idx, bf16[1040,128]{1,0:T(8,128)(2,1)S(1)} %collective-permute-done.19.refs_0_, bf16[1040,128]{1,0:T(8,128)(2,1)S(1)} %collective-permute-done.20.refs_1_, bf16[1040,128]{1,0:T(8,128)(2,1)S(1)} %collective-permute-done.21.refs_2_, ...), custom_call_target="tpu_custom_call" | custom-call | flops 68719476736 | bytes 4194304 | tf_op jit(solution)/shard_map/pallas_call | solution.py:239
  117.9 8.2 %shard_map.73 = (bf16[128,512]{1,0:T(8,128)(2,1)S(1)}, bf16[128,512]{1,0:T(8,128)(2,1)S(1)}, bf16[128,512]{1,0:T(8,128)(2,1)S(1)}, bf16[128,512]{1,0:T(8,128)(2,1)S(1)}) custom-call(s32[4]{0:T(128)S(1)} %pad_add_fusion.idx, bf16[4,512,128]{2,1,0:T(8,128)(2,1)S(1)} %shard_map.71.query, bf16[20,2,128,128]{3,2,1,0:T(8,128)(2,1)S(1)} %get-tuple-element.57.kv, ...), custom_call_target="tpu_custom_call" | custom-call | flops 2147483648 | bytes 4194304 | tf_op jit(solution)/shard_map/pallas_call | solution.py:239
  126.8 2.6 %collective-permute-start.24 = (bf16[128,512]{1,0:T(8,128)(2,1)S(1)}, bf16[128,512]{1,0:T(8,128)(2,1)S(1)}, u32[]{:S(2)}, u32[]{:S(2)}) collective-permute-start(bf16[128,512]{1,0:T(8,128)(2,1)S(1)} %get-tuple-element.60), channel_id=1, source_target_pairs={{0,2},{1,0},{2,6},{3,4},{4,3},{5,1},{6,7},{7,5},{8,10},{9,8},{10,1... | collective-permute-start | bytes 393224 | tf_op jit(solution)/shard_map/ppermute | solution.py:33
  129.5 2.5 %collective-permute-start.25 = (bf16[128,512]{1,0:T(8,128)(2,1)S(1)}, bf16[128,512]{1,0:T(8,128)(2,1)S(1)}, u32[]{:S(2)}, u32[]{:S(2)}) collective-permute-start(bf16[128,512]{1,0:T(8,128)(2,1)S(1)} %get-tuple-element.61), channel_id=1, source_target_pairs={{0,4},{1,6},{2,0},{3,2},{4,5},{5,7},{6,1},{7,3},{8,12},{9,14},{10,... | collective-permute-start | bytes 393224 | tf_op jit(solution)/shard_map/ppermute | solution.py:33
  132.0 1.9 %collective-permute-start.26 = (bf16[128,512]{1,0:T(8,128)(2,1)S(1)}, bf16[128,512]{1,0:T(8,128)(2,1)S(1)}, u32[]{:S(2)}, u32[]{:S(2)}) collective-permute-start(bf16[128,512]{1,0:T(8,128)(2,1)S(1)} %get-tuple-element.62), channel_id=1, source_target_pairs={{0,6},{1,4},{2,2},{3,0},{4,7},{5,5},{6,3},{7,1},{8,14},{9,12},{10,... | collective-permute-start | bytes 393224 | tf_op jit(solution)/shard_map/ppermute | solution.py:33
  133.9 1.4 collective-permute-done.25.refs_2_
  135.3 2.9 %collective-permute-done.26.refs_3_ = bf16[128,512]{1,0:T(8,128)(2,1)S(1)} collective-permute-done((bf16[128,512]{1,0:T(8,128)(2,1)S(1)}, bf16[128,512]{1,0:T(8,128)(2,1)S(1)}, u32[]{:S(2)}, u32[]{:S(2)}) %collective-permute-start.26) | collective-permute-done | bytes 131104 | tf_op jit(solution)/shard_map/ppermute | solution.py:33
  (66 shorter events, 24.5 us)
Async XLA Ops:
  0.0 74.4 %copy-start.7 = (bf16[4096]{0:T(1024)(128)(2,1)S(1)}, bf16[4096]{0:T(1024)(128)(2,1)}, u32[]{:S(2)}) copy-start(bf16[4096]{0:T(1024)(128)(2,1)} %param.7) | copy-start | bytes 24580
  1.3 22.0 %collective-permute-start.2 = (bf16[128,2048]{1,0:T(8,128)(2,1)S(1)}, bf16[128,2048]{1,0:T(8,128)(2,1)S(1)}, u32[]{:S(2)}, u32[]{:S(2)}) collective-permute-start(bf16[128,2048]{1,0:T(8,128)(2,1)S(1)} %get-tuple-element.64.refs_0_), channel_id=1, source_target_pairs={{0,2},{1,3},{2,4},{3,5},{4,6},{5,7},{6,0},{7,1},{8,10},{9,11},{10,... | collective-permute-start | bytes 1572872 | tf_op jit(solution)/shard_map/ppermute | solution.py:33
  2.9 20.5 %collective-permute-start.3 = (bf16[128,2048]{1,0:T(8,128)(2,1)S(1)}, bf16[128,2048]{1,0:T(8,128)(2,1)S(1)}, u32[]{:S(2)}, u32[]{:S(2)}) collective-permute-start(bf16[128,2048]{1,0:T(8,128)(2,1)S(1)} %get-tuple-element.63.refs_4_), channel_id=1, source_target_pairs={{0,6},{1,7},{2,0},{3,1},{4,2},{5,3},{6,4},{7,5},{8,14},{9,15},{10,... | collective-permute-start | bytes 1572872 | tf_op jit(solution)/shard_map/ppermute | solution.py:33
  4.7 1.2 copy-start
  9.0 14.3 %collective-permute-start = (bf16[32,768]{1,0:T(8,128)(2,1)S(1)}, bf16[32,768]{1,0:T(8,128)(2,1)S(1)}, u32[]{:S(2)}, u32[]{:S(2)}) collective-permute-start(bf16[32,768]{1,0:T(8,128)(2,1)S(1)} %get-tuple-element.34), channel_id=1, source_target_pairs={{0,0},{1,4},{2,2},{3,6},{4,8},{5,12},{6,10},{7,14},{8,16},{9,20},{... | collective-permute-start | bytes 147464 | tf_op jit(solution)/shard_map/ppermute | solution.py:33
  15.5 7.9 %collective-permute-start.1 = (bf16[32,768]{1,0:T(8,128)(2,1)S(1)}, bf16[32,768]{1,0:T(8,128)(2,1)S(1)}, u32[]{:S(2)}, u32[]{:S(2)}) collective-permute-start(bf16[32,768]{1,0:T(8,128)(2,1)S(1)} %get-tuple-element.35), channel_id=1, source_target_pairs={{0,2},{1,6},{2,0},{3,4},{4,10},{5,14},{6,8},{7,12},{8,18},{9,22},{... | collective-permute-start | bytes 147464 | tf_op jit(solution)/shard_map/ppermute | solution.py:33
  15.6 2.3 %collective-permute-start.6 = (f32[2,128]{1,0:T(2,128)S(1)}, f32[2,128]{1,0:T(2,128)S(1)}, u32[]{:S(2)}, u32[]{:S(2)}) collective-permute-start(f32[2,128]{1,0:T(2,128)S(1)} %get-tuple-element.38.squares), channel_id=1, source_target_pairs={{0,1},{1,0},{2,3},{3,2},{4,5},{5,4},{6,7},{7,6},{8,9},{9,8},{10,11... | collective-permute-start | bytes 3080 | tf_op jit(solution)/shard_map/ppermute | solution.py:33
  19.1 9.5 %all-to-all-start.1 = ((f32[4,4,128]{2,1,0:T(4,128)}), f32[4,4,128]{2,1,0:T(4,128)S(1)}, u32[]{:S(2)}, u32[]{:S(2)}) async-start(f32[4,4,128]{2,1,0:T(4,128)} %shard_map.66), calls=%async_computation.1 | async-start | bytes 16384 | tf_op jit(solution)/shard_map/all_to_all | solution.py:289
  29.6 27.4 %all-to-all-start = ((bf16[8,64,768]{2,1,0:T(8,128)(2,1)}), bf16[8,64,768]{2,1,0:T(8,128)(2,1)}, u32[]{:S(2)}, u32[]{:S(2)}) async-start(bf16[8,64,768]{2,1,0:T(8,128)(2,1)} %broadcast_in_dim.2), calls=%async_computation | async-start | bytes 1572864 | tf_op jit(solution)/shard_map/all_to_all | solution.py:259
  38.9 16.1 %collective-permute-start.4 = (bf16[128,2048]{1,0:T(8,128)(2,1)S(1)}, bf16[128,2048]{1,0:T(8,128)(2,1)S(1)}, u32[]{:S(2)}, u32[]{:S(2)}) collective-permute-start(bf16[128,2048]{1,0:T(8,128)(2,1)S(1)} %get-tuple-element.63.refs_4_), channel_id=1, source_target_pairs={{0,2},{1,3},{2,4},{3,5},{4,6},{5,7},{6,0},{7,1},{8,10},{9,11},{10,... | collective-permute-start | bytes 1572872 | tf_op jit(solution)/shard_map/ppermute | solution.py:33
  39.5 15.5 %collective-permute-start.5 = (bf16[128,2048]{1,0:T(8,128)(2,1)S(1)}, bf16[128,2048]{1,0:T(8,128)(2,1)S(1)}, u32[]{:S(2)}, u32[]{:S(2)}) collective-permute-start(bf16[128,2048]{1,0:T(8,128)(2,1)S(1)} %get-tuple-element.64.refs_0_), channel_id=1, source_target_pairs={{0,6},{1,7},{2,0},{3,1},{4,2},{5,3},{6,4},{7,5},{8,14},{9,15},{10,... | collective-permute-start | bytes 1572872 | tf_op jit(solution)/shard_map/ppermute | solution.py:33
  42.2 27.7 %collective-permute-start.7 = (bf16[128,2048]{1,0:T(8,128)(2,1)S(1)}, bf16[128,2048]{1,0:T(8,128)(2,1)}, u32[]{:S(2)}, u32[]{:S(2)}) collective-permute-start(bf16[128,2048]{1,0:T(8,128)(2,1)S(1)} %collective-permute-done.2.refs_1_), channel_id=1, source_target_pairs={{0,2},{1,3},{2,4},{3,5},{4,6},{5,7},{6,0},{7,1},{8,10},{9,11},{10,... | collective-permute-start | bytes 1572872 | tf_op jit(solution)/shard_map/ppermute | solution.py:33
  42.2 32.2 %collective-permute-start.8 = (bf16[128,2048]{1,0:T(8,128)(2,1)S(1)}, bf16[128,2048]{1,0:T(8,128)(2,1)}, u32[]{:S(2)}, u32[]{:S(2)}) collective-permute-start(bf16[128,2048]{1,0:T(8,128)(2,1)S(1)} %collective-permute-done.3.refs_6_), channel_id=1, source_target_pairs={{0,6},{1,7},{2,0},{3,1},{4,2},{5,3},{6,4},{7,5},{8,14},{9,15},{10,... | collective-permute-start | bytes 1572872 | tf_op jit(solution)/shard_map/ppermute | solution.py:33
  58.0 7.7 %collective-permute-start.9 = (bf16[512,256]{1,0:T(8,128)(2,1)S(1)}, bf16[512,256]{1,0:T(8,128)(2,1)S(1)}, u32[]{:S(2)}, u32[]{:S(2)}) collective-permute-start(bf16[512,256]{1,0:T(8,128)(2,1)S(1)} %slice.26.own), channel_id=1, source_target_pairs={{0,8},{1,9},{2,10},{3,11},{4,12},{5,13},{6,14},{7,15},{8,16},{9,17... | collective-permute-start | bytes 786440 | tf_op jit(solution)/shard_map/ppermute | solution.py:33
  59.9 6.6 %collective-permute-start.10 = (bf16[512,256]{1,0:T(8,128)(2,1)S(1)}, bf16[512,256]{1,0:T(8,128)(2,1)S(1)}, u32[]{:S(2)}, u32[]{:S(2)}) collective-permute-start(bf16[512,256]{1,0:T(8,128)(2,1)S(1)} %slice.26.own), channel_id=1, source_target_pairs={{0,24},{1,25},{2,26},{3,27},{4,28},{5,29},{6,30},{7,31},{8,0},{9,1... | collective-permute-start | bytes 786440 | tf_op jit(solution)/shard_map/ppermute | solution.py:33
  66.5 16.6 %collective-permute-start.14 = (bf16[512,512]{1,0:T(8,128)(2,1)S(1)}, bf16[512,512]{1,0:T(8,128)(2,1)S(1)}, u32[]{:S(2)}, u32[]{:S(2)}) collective-permute-start(bf16[512,512]{1,0:T(8,128)(2,1)S(1)} %slice.27.own), channel_id=1, source_target_pairs={{0,8},{1,9},{2,10},{3,11},{4,12},{5,13},{6,14},{7,15},{8,16},{9,17... | collective-permute-start | bytes 1572872 | tf_op jit(solution)/shard_map/ppermute | solution.py:33
  66.5 17.0 %collective-permute-start.15 = (bf16[512,512]{1,0:T(8,128)(2,1)S(1)}, bf16[512,512]{1,0:T(8,128)(2,1)S(1)}, u32[]{:S(2)}, u32[]{:S(2)}) collective-permute-start(bf16[512,512]{1,0:T(8,128)(2,1)S(1)} %slice.27.own), channel_id=1, source_target_pairs={{0,24},{1,25},{2,26},{3,27},{4,28},{5,29},{6,30},{7,31},{8,0},{9,1... | collective-permute-start | bytes 1572872 | tf_op jit(solution)/shard_map/ppermute | solution.py:33
  69.8 11.4 %collective-permute-start.11 = (bf16[256,256]{1,0:T(8,128)(2,1)S(1)}, bf16[256,256]{1,0:T(8,128)(2,1)S(1)}, u32[]{:S(2)}, u32[]{:S(2)}) collective-permute-start(bf16[256,256]{1,0:T(8,128)(2,1)S(1)} %slice.32), channel_id=1, source_target_pairs={{0,8},{1,9},{2,10},{3,11},{4,12},{5,13},{6,14},{7,15},{8,16},{9,17... | collective-permute-start | bytes 393224 | tf_op jit(solution)/shard_map/ppermute | solution.py:33
  69.9 11.3 %collective-permute-start.12 = (bf16[256,256]{1,0:T(8,128)(2,1)S(1)}, bf16[256,256]{1,0:T(8,128)(2,1)S(1)}, u32[]{:S(2)}, u32[]{:S(2)}) collective-permute-start(bf16[256,256]{1,0:T(8,128)(2,1)S(1)} %slice.33), channel_id=1, source_target_pairs={{0,24},{1,25},{2,26},{3,27},{4,28},{5,29},{6,30},{7,31},{8,0},{9,1... | collective-permute-start | bytes 393224 | tf_op jit(solution)/shard_map/ppermute | solution.py:33
  74.4 1.0 copy-start.2
  83.0 3.6 %collective-permute-start.13 = (f32[512,256]{1,0:T(8,128)S(1)}, f32[512,256]{1,0:T(8,128)S(1)}, u32[]{:S(2)}, u32[]{:S(2)}) collective-permute-start(f32[512,256]{1,0:T(8,128)S(1)} %get-tuple-element.49), channel_id=1, source_target_pairs={{0,1},{1,0},{2,3},{3,2},{4,5},{5,4},{6,7},{7,6},{8,9},{9,8},{10,11... | collective-permute-start | bytes 1572872 | tf_op jit(solution)/shard_map/ppermute | solution.py:33
  83.2 10.0 %collective-permute-start.16 = (bf16[256,512]{1,0:T(8,128)(2,1)S(1)}, bf16[256,512]{1,0:T(8,128)(2,1)S(1)}, u32[]{:S(2)}, u32[]{:S(2)}) collective-permute-start(bf16[256,512]{1,0:T(8,128)(2,1)S(1)} %slice.34), channel_id=1, source_target_pairs={{0,8},{1,9},{2,10},{3,11},{4,12},{5,13},{6,14},{7,15},{8,16},{9,17... | collective-permute-start | bytes 786440 | tf_op jit(solution)/shard_map/ppermute | solution.py:33
  83.6 13.2 %collective-permute-start.17 = (bf16[256,512]{1,0:T(8,128)(2,1)S(1)}, bf16[256,512]{1,0:T(8,128)(2,1)S(1)}, u32[]{:S(2)}, u32[]{:S(2)}) collective-permute-start(bf16[256,512]{1,0:T(8,128)(2,1)S(1)} %slice.35), channel_id=1, source_target_pairs={{0,24},{1,25},{2,26},{3,27},{4,28},{5,29},{6,30},{7,31},{8,0},{9,1... | collective-permute-start | bytes 786440 | tf_op jit(solution)/shard_map/ppermute | solution.py:33
  87.5 12.7 %collective-permute-start.19 = (bf16[1040,128]{1,0:T(8,128)(2,1)S(1)}, bf16[1040,128]{1,0:T(8,128)(2,1)S(1)}, u32[]{:S(2)}, u32[]{:S(2)}) collective-permute-start(bf16[1040,128]{1,0:T(8,128)(2,1)S(1)} %shard_map.69.refs_4_), channel_id=1, source_target_pairs={{0,32},{1,33},{2,34},{3,35},{4,36},{5,37},{6,38},{7,39},{8,40},{9,... | collective-permute-start | bytes 798728 | tf_op jit(solution)/shard_map/ppermute | solution.py:33
  88.2 15.8 %collective-permute-start.20 = (bf16[1040,128]{1,0:T(8,128)(2,1)S(1)}, bf16[1040,128]{1,0:T(8,128)(2,1)S(1)}, u32[]{:S(2)}, u32[]{:S(2)}) collective-permute-start(bf16[1040,128]{1,0:T(8,128)(2,1)S(1)} %shard_map.69.refs_4_), channel_id=1, source_target_pairs={{0,24},{1,25},{2,26},{3,27},{4,28},{5,29},{6,30},{7,31},{8,32},{9,... | collective-permute-start | bytes 798728 | tf_op jit(solution)/shard_map/ppermute | solution.py:33
  89.9 19.9 %collective-permute-start.21 = (bf16[1040,128]{1,0:T(8,128)(2,1)S(1)}, bf16[1040,128]{1,0:T(8,128)(2,1)S(1)}, u32[]{:S(2)}, u32[]{:S(2)}) collective-permute-start(bf16[1040,128]{1,0:T(8,128)(2,1)S(1)} %shard_map.69.refs_4_), channel_id=1, source_target_pairs={{0,16},{1,17},{2,18},{3,19},{4,20},{5,21},{6,22},{7,23},{8,24},{9,... | collective-permute-start | bytes 798728 | tf_op jit(solution)/shard_map/ppermute | solution.py:33
  93.2 22.4 %collective-permute-start.22 = (bf16[1040,128]{1,0:T(8,128)(2,1)S(1)}, bf16[1040,128]{1,0:T(8,128)(2,1)S(1)}, u32[]{:S(2)}, u32[]{:S(2)}) collective-permute-start(bf16[1040,128]{1,0:T(8,128)(2,1)S(1)} %shard_map.69.refs_4_), channel_id=1, source_target_pairs={{0,8},{1,9},{2,10},{3,11},{4,12},{5,13},{6,14},{7,15},{8,16},{9,17... | collective-permute-start | bytes 798728 | tf_op jit(solution)/shard_map/ppermute | solution.py:33
  99.9 17.2 %collective-permute-start.18 = (f32[512,512]{1,0:T(8,128)S(1)}, f32[512,512]{1,0:T(8,128)S(1)}, u32[]{:S(2)}, u32[]{:S(2)}) collective-permute-start(f32[512,512]{1,0:T(8,128)S(1)} %get-tuple-element.55), channel_id=1, source_target_pairs={{0,1},{1,0},{2,3},{3,2},{4,5},{5,4},{6,7},{7,6},{8,9},{9,8},{10,11... | collective-permute-start | bytes 3145736 | tf_op jit(solution)/shard_map/ppermute | solution.py:33
  126.2 7.7 %collective-permute-start.23 = (bf16[128,512]{1,0:T(8,128)(2,1)S(1)}, bf16[128,512]{1,0:T(8,128)(2,1)S(1)}, u32[]{:S(2)}, u32[]{:S(2)}) collective-permute-start(bf16[128,512]{1,0:T(8,128)(2,1)S(1)} %get-tuple-element.59), channel_id=1, source_target_pairs={{0,0},{1,2},{2,4},{3,6},{4,1},{5,3},{6,5},{7,7},{8,8},{9,10},{10,1... | collective-permute-start | bytes 393224 | tf_op jit(solution)/shard_map/ppermute | solution.py:33
  126.8 7.1 %collective-permute-start.24 = (bf16[128,512]{1,0:T(8,128)(2,1)S(1)}, bf16[128,512]{1,0:T(8,128)(2,1)S(1)}, u32[]{:S(2)}, u32[]{:S(2)}) collective-permute-start(bf16[128,512]{1,0:T(8,128)(2,1)S(1)} %get-tuple-element.60), channel_id=1, source_target_pairs={{0,2},{1,0},{2,6},{3,4},{4,3},{5,1},{6,7},{7,5},{8,10},{9,8},{10,1... | collective-permute-start | bytes 393224 | tf_op jit(solution)/shard_map/ppermute | solution.py:33
  129.5 5.8 %collective-permute-start.25 = (bf16[128,512]{1,0:T(8,128)(2,1)S(1)}, bf16[128,512]{1,0:T(8,128)(2,1)S(1)}, u32[]{:S(2)}, u32[]{:S(2)}) collective-permute-start(bf16[128,512]{1,0:T(8,128)(2,1)S(1)} %get-tuple-element.61), channel_id=1, source_target_pairs={{0,4},{1,6},{2,0},{3,2},{4,5},{5,7},{6,1},{7,3},{8,12},{9,14},{10,... | collective-permute-start | bytes 393224 | tf_op jit(solution)/shard_map/ppermute | solution.py:33
  132.0 6.3 %collective-permute-start.26 = (bf16[128,512]{1,0:T(8,128)(2,1)S(1)}, bf16[128,512]{1,0:T(8,128)(2,1)S(1)}, u32[]{:S(2)}, u32[]{:S(2)}) collective-permute-start(bf16[128,512]{1,0:T(8,128)(2,1)S(1)} %get-tuple-element.62), channel_id=1, source_target_pairs={{0,6},{1,4},{2,2},{3,0},{4,7},{5,5},{6,3},{7,1},{8,14},{9,12},{10,... | collective-permute-start | bytes 393224 | tf_op jit(solution)/shard_map/ppermute | solution.py:33
  (5 other events, 3.7 us)

commit v2 on v1

--- a/solution.py
+++ b/solution.py
@@ -65,7 +65,7 @@
 ROWS = 8 * HD + 16
 
 
-def begin_kernel(idx, hidden, query, key, value, first, second, squares):
+def pack_kernel(idx, query, key, value, first, second):
     x = idx[2]
     for by, out in ((0, first), (1, second)):
         b = lax.rem(x + by, 2)
@@ -73,17 +73,26 @@
         out[:, 512:640] = key[:, pl.ds(pl.multiple_of(b * 128, 128), 128)]
         out[:, 640:] = value[:, pl.ds(pl.multiple_of(b * 128, 128), 128)]
 
+
+def squares_kernel(hidden, squares):
     for s in range(2):
         wide = hidden[s].astype(F32)
         total = jnp.sum(wide * wide, axis=-1, keepdims=True)
-        squares[s : s + 1, :] = jnp.broadcast_to(total, (HD, HD)).T[:1, :]
-
-
-def tell_kernel(squares, others, docs, out):
-    scale = lax.rsqrt((squares[...] + others[...]) * (1.0 / WIDTH) + EPS)
-    for n in range(NX):
-        out[n, 0:2, :] = docs[...].astype(F32)
-        out[n, 2:4, :] = scale
+        squares[s * 128 : s * 128 + 128, :] = jnp.broadcast_to(total, (HD, HD))
+
+
+def norm_kernel(idx, hidden, squares, others, docs, gain, seq_a, seq_b):
+    g = gain[:, pl.ds(pl.multiple_of(idx[3] * HALF, HALF), HALF)].astype(F32)
+    for s, out in ((0, seq_a), (1, seq_b)):
+        for t in range(4):
+            rows = slice(t * 32, t * 32 + 32)
+            both = slice(s * 128 + t * 32, s * 128 + t * 32 + 32)
+            scale = lax.rsqrt((squares[both, :] + others[both, :]) * (1.0 / WIDTH) + EPS)
+            wide = hidden[s, rows, :].astype(F32)
+            out[rows, :] = (wide * scale[:, :1] * g).astype(BF)
+    extra = jnp.concatenate([docs[...].astype(F32), jnp.zeros((14, HD), F32)], axis=0)
+    seq_a[128:144, :HD] = extra.astype(BF)
+    seq_a[128:144, HD:] = jnp.zeros((16, HALF - HD), BF)
 
 
 def merge_kernel(idx, first, second, out):
@@ -93,19 +102,21 @@
     out[32:, :] = jnp.where(odd, top, low).astype(BF)
 
 
-def norm_kernel(idx, told, gain, *refs):
-    hidden, x_all = refs[:8], refs[8]
+def stack_kernel(idx, *refs):
+    hidden, (x_all, docs) = refs[:8], refs[8:]
     x, c = idx[2], idx[3]
-    g = gain[:, pl.ds(pl.multiple_of(c * HALF, HALF), HALF)].astype(F32)
+    row = lax.broadcasted_iota(jnp.int32, (16, HD), 0)
+    found = jnp.zeros((16, HD), F32)
     for n, ref in enumerate(hidden):
         s, d = n // 4, (0, -1, 1, 2)[n % 4]
         chip = lax.rem(x + d + NX, NX)
         base = jnp.where(c == s, 0, 512) + chip * 128
-        scale = jnp.broadcast_to(told[chip, 2 + s : 3 + s, :], (HD, HD)).T
-        for t in range(4):
-            rows = slice(t * 32, t * 32 + 32)
-            wide = ref[rows, :].astype(F32) * scale[rows, :1] * g
-            x_all[pl.ds(pl.multiple_of(base + t * 32, 32), 32), :] = wide.astype(BF)
+        x_all[pl.ds(pl.multiple_of(base, 128), 128), :] = ref[:128, :]
+        if s == 0:
+            tile = ref[128:144, :HD].astype(F32)
+            mine = jnp.where(c == 0, tile[0:1, :], tile[1:2, :])
+            found = jnp.where(row == chip, mine, found)
+    docs[...] = found.astype(BF)
 
 
 def multiply(x_all, w_all, keep, send):
@@ -136,15 +147,14 @@
     return value * cosine + pltpu.roll(value, 64, 1) * sine
 
 
-def rotate_kv_kernel(idx, keep, got, cos, sin, told, kv):
+def rotate_kv_kernel(keep, got, cos, sin, docs, kv):
     for i in range(4):
         rows = slice(i * 128, i * 128 + 128)
         value = keep[rows, :] + got[rows, :]
         at = i * 256
         kv[at : at + 128, :] = turned(value[:, :128], cos[rows, :], sin[rows, :]).astype(BF)
         kv[at + 128 : at + 256, :] = value[:, 128:].T.astype(BF)
-    docs = jnp.where(idx[3] == 0, told[:, 0, :], told[:, 1, :])
-    kv[1024:1040, :] = jnp.concatenate([docs, jnp.zeros((12, HD), F32)], axis=0).astype(BF)
+    kv[1024:1040, :] = docs[...]
 
 
 def rotate_q_kernel(keep, got, cos, sin, query):
@@ -175,14 +185,21 @@
     def top(s):
         return jnp.max(s.reshape(32, 8, 1024), axis=0)
 
-    def scan(p, best):
-        s = jnp.where(sub >= first - 256 * p, score(p), -1e30)
+    def keep(p, s, best):
         scores[pl.ds(pl.multiple_of(p * 256, 256), 256), :] = s
         return jnp.maximum(best, top(s))
 
+    def masked(p, best):
+        return keep(p, jnp.where(sub >= first - 256 * p, score(p), -1e30), best)
+
+    def whole(p, best):
+        return keep(p, score(p), best)
+
     s = jnp.where((sub >= first - 256 * last) & (sub <= lane), score(last), -1e30)
     scores[pl.ds(pl.multiple_of(256 * last, 256), 256), :] = s
-    best = lax.fori_loop(low, last, scan, top(s))
+    inside = jnp.clip(lax.div(jnp.max(first) + 255, 256), low, last)
+    best = lax.fori_loop(low, inside, masked, top(s))
+    best = lax.fori_loop(inside, last, whole, best)
     best = jnp.max(best, axis=0, keepdims=True)
     acc[...] = jnp.zeros((HD, 1024), F32)
 
@@ -266,46 +283,46 @@
     shape = jax.ShapeDtypeStruct
     where = jnp.stack([z, y, x, c]).astype(jnp.int32)
 
-    seq_a, seq_b = hidden_in[0], hidden_in[1]
+    piece = shape((32, COLS), BF)
+    first, second = call(
+        pack_kernel, (piece, piece), (where, w_query, w_key, w_value), cost=cost(0, 1 << 18)
+    )
+    first, second = permute(first, spread(0)), permute(second, spread(1))
+    squares = call(
+        squares_kernel,
+        shape((256, HD), F32),
+        (hidden_in,),
+        cost=cost(1 << 20, 2 << 20),
+        smem=0,
+    )
+    others = permute(squares, lambda z, y, x, c: (z, y, x, 1 - c))
+
+    seq_a, seq_b = call(
+        norm_kernel,
+        (shape((144, HALF), BF), shape((128, HALF), BF)),
+        (where, hidden_in, squares, others, doc_ids, norm_gain.reshape(1, WIDTH)),
+        cost=cost(1 << 20, 3 << 20),
+    )
+    first, second, seq_a, seq_b = tie(first, second, seq_a, seq_b)
     right_a, left_b = along_x(seq_a, 1), along_x(seq_b, -1)
     right_b, left_a = along_x(seq_b, 1), along_x(seq_a, -1)
-
-    piece = shape((32, COLS), BF)
-    first, second, squares = call(
-        begin_kernel,
-        (piece, piece, shape((2, HD), F32)),
-        (where, hidden_in, w_query, w_key, w_value),
-        cost=cost(1 << 20, 2 << 20),
-    )
-    first, second = permute(first, spread(0)), permute(second, spread(1))
-    others = permute(squares, lambda z, y, x, c: (z, y, x, 1 - c))
-    told = call(
-        tell_kernel,
-        shape((NX, 4, HD), F32),
-        (squares, others, doc_ids),
-        cost=cost(0, 1 << 14),
-        smem=0,
-    )
-    told = lax.all_to_all(told, "x", 0, 0, tiled=True)
-    first, second, right_a, left_b = tie(first, second, right_a, left_b)
-    far_a, far_b = along_x(right_a, 1), along_x(left_b, -1)
     rows = call(merge_kernel, shape((64, COLS), BF), (where, first, second), cost=cost(0, 1 << 18))
     w_z = copies(rows, "z", NZ).reshape(512, COLS)
-    w_z, right_b, left_a, told = tie(w_z, right_b, left_a, told)
-    around = []
-    for cols in (slice(512, COLS), slice(0, 512)):
-        own = w_z[:, cols]
-        if around:
-            own, up, down = tie(own, *around[0][1:3])
-            around[0] = (around[0][0], up, down, *around[0][3:])
-        up, down = along_y(own, 1), along_y(own, -1)
-        around.append((own, up, down, along_y(up[:256], 1), along_y(down[256:], -1)))
-    x_all = call(
-        norm_kernel,
-        shape((1024, HALF), BF),
-        (where, told, norm_gain.reshape(1, WIDTH))
-        + (seq_a, right_a, left_a, far_a, seq_b, right_b, left_b, far_b),
-        cost=cost(1 << 22, 8 << 20),
+    w_z, right_a, left_b = tie(w_z, right_a, left_b)
+    far_a, far_b = along_x(right_a, 1), along_x(left_b, -1)
+
+    kv0, q0 = w_z[:, 512:], w_z[:, :512]
+    kv_up, kv_down = along_y(kv0, 1), along_y(kv0, -1)
+    kv_up, kv_down, right_b, left_a = tie(kv_up, kv_down, right_b, left_a)
+    kv_far_up, kv_far_down = along_y(kv_up[:256], 1), along_y(kv_down[256:], -1)
+    q0, kv_far_up, kv_far_down = tie(q0, kv_far_up, kv_far_down)
+    q_up, q_down = along_y(q0, 1), along_y(q0, -1)
+    q_far_up, q_far_down = along_y(q_up[:256], 1), along_y(q_down[256:], -1)
+    x_all, docs = call(
+        stack_kernel,
+        (shape((1024, HALF), BF), shape((16, HD), BF)),
+        (where, seq_a, right_a, left_a, far_a, seq_b, right_b, left_b, far_b),
+        cost=cost(0, 8 << 20),
     )
 
     position = (512 * (z * NY + y) + jnp.arange(512, dtype=jnp.int32)).astype(F32)
@@ -317,7 +334,7 @@
     keep, send = call(
         project_kernel,
         (shape((512, 256), F32), shape((512, 256), F32)),
-        (where, x_all, *around[0]),
+        (where, x_all, kv0, kv_up, kv_down, kv_far_up, kv_far_down),
         (pltpu.VMEM((NZ, 256, 256), BF),),
         cost(2 * 1024 * HALF * 256, 10 << 20),
     )
@@ -325,8 +342,9 @@
     own = call(
         rotate_kv_kernel,
         shape((ROWS, HD), BF),
-        (where, keep, got, cos, sin, told),
+        (keep, got, cos, sin, docs),
         cost=cost(1 << 20, 2 << 20),
+        smem=0,
     )
     x_all, own = tie(x_all, own)
     earlier = [
@@ -336,9 +354,9 @@
     keep, send = call(
         project_kernel,
         (shape((512, 512), F32), shape((512, 512), F32)),
-        (where, x_all, *around[1]),
+        (where, x_all, q0, q_up, q_down, q_far_up, q_far_down),
         (pltpu.VMEM((NZ, 256, 512), BF),),
-        cost(2 * 1024 * HALF * 512, 10 << 20),
+        cost(0, 0),
     )
     got = permute(send, lambda z, y, x, c: (z, y, x, 1 - c))
     query = call(

time: 141 us -> 141 us (level)
  the two profiles are of different devices: /device:TPU:64 before, /device:TPU:32 now
where the time goes in v2:
time: 141 us; the launch traced here: 142 us
  starting transfers between devices  54.2 us (38%)
  waiting for transfers between devices  52.2 us (37%)
  Pallas kernels  24.6 us (17%)
  local copies, waits for them, and re-layouts  9.77 us (7%)
    ppermute x27, waiting for transfers between devices, permute(): return lax.ppermute(value, AXES, pairs)  47.9 us
    ppermute x27, starting transfers between devices, permute(): return lax.ppermute(value, AXES, pairs)  45.1 us
    pallas_call x12, Pallas kernels, call(): pl.pallas_call(kernel, out_shape=shapes, in_specs=[SMEM] * smem + [VMEM]...  24.6 us
    all_to_all x1, starting transfers between devices, copies(): lax.all_to_all(jnp.broadcast_to(value[None], (count, *value.shape)), axis...  9.14 us
    unnamed x14, local copies, waits for them, and re-layouts  6.3 us
    all_to_all x1, waiting for transfers between devices, copies(): lax.all_to_all(jnp.broadcast_to(value[None], (count, *value.shape)), axis...  4.24 us
  transfers between devices with their start and end apart: 28, of which 12 were waited for; matrix products, arithmetic and copies ran while one was open for 3% of the time, Pallas kernels for 8%

profile of v2, /device:TPU:32, one launch (start us, length us, event | category | flops | bytes accessed | tf_op | source)
XLA Modules:
  0.0 142.1 jit_solution(2551717210582416270)
XLA Ops:
  4.5 3.8 %collective-permute-start = (bf16[32,768]{1,0:T(8,128)(2,1)S(1)}, bf16[32,768]{1,0:T(8,128)(2,1)S(1)}, u32[]{:S(2)}, u32[]{:S(2)}) collective-permute-start(bf16[32,768]{1,0:T(8,128)(2,1)S(1)} %get-tuple-element.40), channel_id=1, source_target_pairs={{0,0},{1,4},{2,2},{3,6},{4,8},{5,12},{6,10},{7,14},{8,16},{9,20},{... | collective-permute-start | bytes 147464 | tf_op jit(solution)/shard_map/ppermute | solution.py:33
  8.3 5.5 %collective-permute-start.1 = (bf16[32,768]{1,0:T(8,128)(2,1)S(1)}, bf16[32,768]{1,0:T(8,128)(2,1)S(1)}, u32[]{:S(2)}, u32[]{:S(2)}) collective-permute-start(bf16[32,768]{1,0:T(8,128)(2,1)S(1)} %get-tuple-element.41), channel_id=1, source_target_pairs={{0,2},{1,6},{2,0},{3,4},{4,10},{5,14},{6,8},{7,12},{8,18},{9,22},{... | collective-permute-start | bytes 147464 | tf_op jit(solution)/shard_map/ppermute | solution.py:33
  16.5 1.6 %shard_map.66 = (bf16[144,2048]{1,0:T(8,128)(2,1)S(1)}, bf16[128,2048]{1,0:T(8,128)(2,1)}) custom-call(s32[4]{0:T(128)S(1)} %pad_add_fusion.idx, bf16[2,128,2048]{2,1,0:T(8,128)(2,1)S(1)} %copy-done.1, f32[256,128]{1,0:T(8,128)S(1)} %shard_map.65.squares, f32[256,128]{1,0:T(8,128)S(1)} %collective-permute-done.2.others, s32[2,128]{1,0:T(2,128)S(1)} %copy-done.5, ...), custom_call_target="tpu_custom_call" | custom-call | flops 1048576 | bytes 3145728 | tf_op jit(solution)/shard_map/pallas_call | solution.py:256
  19.6 9.1 %all-to-all-start = ((bf16[8,64,768]{2,1,0:T(8,128)(2,1)}), bf16[8,64,768]{2,1,0:T(8,128)(2,1)S(1)}, u32[]{:S(2)}, u32[]{:S(2)}) async-start(bf16[8,64,768]{2,1,0:T(8,128)(2,1)} %broadcast_in_dim.2), calls=%async_computation | async-start | bytes 1572864 | tf_op jit(solution)/shard_map/all_to_all | solution.py:276
  28.8 1.4 %collective-permute-start.3 = (bf16[144,2048]{1,0:T(8,128)(2,1)S(1)}, bf16[144,2048]{1,0:T(8,128)(2,1)S(1)}, u32[]{:S(2)}, u32[]{:S(2)}) collective-permute-start(bf16[144,2048]{1,0:T(8,128)(2,1)S(1)} %get-tuple-element.44.refs_0_), channel_id=1, source_target_pairs={{0,2},{1,3},{2,4},{3,5},{4,6},{5,7},{6,0},{7,1},{8,10},{9,11},{10,... | collective-permute-start | bytes 1769480 | tf_op jit(solution)/shard_map/ppermute | solution.py:33
  30.2 2.7 %collective-permute-start.4 = (bf16[128,2048]{1,0:T(8,128)(2,1)}, bf16[128,2048]{1,0:T(8,128)(2,1)}, u32[]{:S(2)}, u32[]{:S(2)}) collective-permute-start(bf16[128,2048]{1,0:T(8,128)(2,1)} %get-tuple-element.47.refs_4_), channel_id=1, source_target_pairs={{0,6},{1,7},{2,0},{3,1},{4,2},{5,3},{6,4},{7,5},{8,14},{9,15},{10,... | collective-permute-start | bytes 1572872 | tf_op jit(solution)/shard_map/ppermute | solution.py:33
  32.9 2.0 %collective-permute-start.8 = (bf16[144,2048]{1,0:T(8,128)(2,1)S(1)}, bf16[144,2048]{1,0:T(8,128)(2,1)S(1)}, u32[]{:S(2)}, u32[]{:S(2)}) collective-permute-start(bf16[144,2048]{1,0:T(8,128)(2,1)S(1)} %get-tuple-element.44.refs_0_), channel_id=1, source_target_pairs={{0,6},{1,7},{2,0},{3,1},{4,2},{5,3},{6,4},{7,5},{8,14},{9,15},{10,... | collective-permute-start | bytes 1769480 | tf_op jit(solution)/shard_map/ppermute | solution.py:33
  34.9 10.7 %collective-permute-done.4.refs_6_ = bf16[128,2048]{1,0:T(8,128)(2,1)} collective-permute-done((bf16[128,2048]{1,0:T(8,128)(2,1)}, bf16[128,2048]{1,0:T(8,128)(2,1)}, u32[]{:S(2)}, u32[]{:S(2)}) %collective-permute-start.4) | collective-permute-done | bytes 524320 | tf_op jit(solution)/shard_map/ppermute | solution.py:33
  45.6 1.5 %collective-permute-done.3.refs_1_ = bf16[144,2048]{1,0:T(8,128)(2,1)S(1)} collective-permute-done((bf16[144,2048]{1,0:T(8,128)(2,1)S(1)}, bf16[144,2048]{1,0:T(8,128)(2,1)S(1)}, u32[]{:S(2)}, u32[]{:S(2)}) %collective-permute-start.3) | collective-permute-done | bytes 589856 | tf_op jit(solution)/shard_map/ppermute | solution.py:33
  47.2 4.2 %all-to-all-done = bf16[8,64,768]{2,1,0:T(8,128)(2,1)S(1)} async-done(((bf16[8,64,768]{2,1,0:T(8,128)(2,1)}), bf16[8,64,768]{2,1,0:T(8,128)(2,1)S(1)}, u32[]{:S(2)}, u32[]{:S(2)}) %all-to-all-start) | async-done | bytes 786464 | tf_op jit(solution)/shard_map/all_to_all | solution.py:276
  52.3 2.2 %collective-permute-start.5 = (bf16[512,256]{1,0:T(8,128)(2,1)S(1)}, bf16[512,256]{1,0:T(8,128)(2,1)S(1)}, u32[]{:S(2)}, u32[]{:S(2)}) collective-permute-start(bf16[512,256]{1,0:T(8,128)(2,1)S(1)} %slice.18.own), channel_id=1, source_target_pairs={{0,8},{1,9},{2,10},{3,11},{4,12},{5,13},{6,14},{7,15},{8,16},{9,17... | collective-permute-start | bytes 786440 | tf_op jit(solution)/shard_map/ppermute | solution.py:33
  54.5 2.8 %collective-permute-start.6 = (bf16[512,256]{1,0:T(8,128)(2,1)S(1)}, bf16[512,256]{1,0:T(8,128)(2,1)S(1)}, u32[]{:S(2)}, u32[]{:S(2)}) collective-permute-start(bf16[512,256]{1,0:T(8,128)(2,1)S(1)} %slice.18.own), channel_id=1, source_target_pairs={{0,24},{1,25},{2,26},{3,27},{4,28},{5,29},{6,30},{7,31},{8,0},{9,1... | collective-permute-start | bytes 786440 | tf_op jit(solution)/shard_map/ppermute | solution.py:33
  57.3 3.2 %collective-permute-start.10 = (bf16[128,2048]{1,0:T(8,128)(2,1)}, bf16[128,2048]{1,0:T(8,128)(2,1)}, u32[]{:S(2)}, u32[]{:S(2)}) collective-permute-start(bf16[128,2048]{1,0:T(8,128)(2,1)} %collective-permute-done.4.refs_6_), channel_id=1, source_target_pairs={{0,6},{1,7},{2,0},{3,1},{4,2},{5,3},{6,4},{7,5},{8,14},{9,15},{10,... | collective-permute-start | bytes 1572872 | tf_op jit(solution)/shard_map/ppermute | solution.py:33
  60.6 3.0 %collective-permute-done.5.up = bf16[512,256]{1,0:T(8,128)(2,1)S(1)} collective-permute-done((bf16[512,256]{1,0:T(8,128)(2,1)S(1)}, bf16[512,256]{1,0:T(8,128)(2,1)S(1)}, u32[]{:S(2)}, u32[]{:S(2)}) %collective-permute-start.5) | collective-permute-done | bytes 262176 | tf_op jit(solution)/shard_map/ppermute | solution.py:33
  65.5 2.1 %collective-permute-start.12 = (bf16[256,256]{1,0:T(8,128)(2,1)}, bf16[256,256]{1,0:T(8,128)(2,1)S(1)}, u32[]{:S(2)}, u32[]{:S(2)}) collective-permute-start(bf16[256,256]{1,0:T(8,128)(2,1)} %slice.21), channel_id=1, source_target_pairs={{0,24},{1,25},{2,26},{3,27},{4,28},{5,29},{6,30},{7,31},{8,0},{9,1... | collective-permute-start | bytes 393224 | tf_op jit(solution)/shard_map/ppermute | solution.py:33
  70.7 1.7 %collective-permute-start.14 = (bf16[512,512]{1,0:T(8,128)(2,1)S(1)}, bf16[512,512]{1,0:T(8,128)(2,1)S(1)}, u32[]{:S(2)}, u32[]{:S(2)}) collective-permute-start(bf16[512,512]{1,0:T(8,128)(2,1)S(1)} %slice.19.own), channel_id=1, source_target_pairs={{0,8},{1,9},{2,10},{3,11},{4,12},{5,13},{6,14},{7,15},{8,16},{9,17... | collective-permute-start | bytes 1572872 | tf_op jit(solution)/shard_map/ppermute | solution.py:33
  73.4 1.8 %shard_map.68 = (bf16[1024,2048]{1,0:T(8,128)(2,1)S(1)}, bf16[16,128]{1,0:T(8,128)(2,1)S(1)}) custom-call(s32[4]{0:T(128)S(1)} %pad_add_fusion.idx, bf16[144,2048]{1,0:T(8,128)(2,1)S(1)} %get-tuple-element.44.refs_0_, bf16[144,2048]{1,0:T(8,128)(2,1)S(1)} %collective-permute-done.3.refs_1_, bf16[144,2048]{1,0:T(8,128)(2,1)S(1)} %collective-permute-done.8.refs_2_, ...), custom_call_target="tpu_custom_call" | custom-call | bytes 8388608 | tf_op jit(solution)/shard_map/pallas_call | solution.py:256
  75.2 1.8 %shard_map.69 = (f32[512,256]{1,0:T(8,128)S(1)}, f32[512,256]{1,0:T(8,128)S(1)}) custom-call(s32[4]{0:T(128)S(1)} %pad_add_fusion.idx, bf16[1024,2048]{1,0:T(8,128)(2,1)S(1)} %get-tuple-element.64.x_all, bf16[512,256]{1,0:T(8,128)(2,1)S(1)} %slice.18.own, bf16[512,256]{1,0:T(8,128)(2,1)S(1)} %collective-permute-done.5.up, ...), custom_call_target="tpu_custom_call" | custom-call | flops 1073741824 | bytes 10485760 | tf_op jit(solution)/shard_map/pallas_call | solution.py:256
  77.2 2.1 %collective-permute-start.15 = (bf16[512,512]{1,0:T(8,128)(2,1)S(1)}, bf16[512,512]{1,0:T(8,128)(2,1)S(1)}, u32[]{:S(2)}, u32[]{:S(2)}) collective-permute-start(bf16[512,512]{1,0:T(8,128)(2,1)S(1)} %slice.19.own), channel_id=1, source_target_pairs={{0,24},{1,25},{2,26},{3,27},{4,28},{5,29},{6,30},{7,31},{8,0},{9,1... | collective-permute-start | bytes 1572872 | tf_op jit(solution)/shard_map/ppermute | solution.py:33
  79.3 4.9 %collective-permute-done.14.up = bf16[512,512]{1,0:T(8,128)(2,1)S(1)} collective-permute-done((bf16[512,512]{1,0:T(8,128)(2,1)S(1)}, bf16[512,512]{1,0:T(8,128)(2,1)S(1)}, u32[]{:S(2)}, u32[]{:S(2)}) %collective-permute-start.14) | collective-permute-done | bytes 524320 | tf_op jit(solution)/shard_map/ppermute | solution.py:33
  84.8 3.3 %collective-permute-start.20 = (bf16[1040,128]{1,0:T(8,128)(2,1)S(1)}, bf16[1040,128]{1,0:T(8,128)(2,1)S(1)}, u32[]{:S(2)}, u32[]{:S(2)}) collective-permute-start(bf16[1040,128]{1,0:T(8,128)(2,1)S(1)} %shard_map.70.refs_4_), channel_id=1, source_target_pairs={{0,24},{1,25},{2,26},{3,27},{4,28},{5,29},{6,30},{7,31},{8,32},{9,... | collective-permute-start | bytes 798728 | tf_op jit(solution)/shard_map/ppermute | solution.py:33
  88.2 9.5 %collective-permute-done.15.down = bf16[512,512]{1,0:T(8,128)(2,1)S(1)} collective-permute-done((bf16[512,512]{1,0:T(8,128)(2,1)S(1)}, bf16[512,512]{1,0:T(8,128)(2,1)S(1)}, u32[]{:S(2)}, u32[]{:S(2)}) %collective-permute-start.15) | collective-permute-done | bytes 524320 | tf_op jit(solution)/shard_map/ppermute | solution.py:33
  97.8 10.8 %collective-permute-done.17.far_down = bf16[256,512]{1,0:T(8,128)(2,1)S(1)} collective-permute-done((bf16[256,512]{1,0:T(8,128)(2,1)S(1)}, bf16[256,512]{1,0:T(8,128)(2,1)S(1)}, u32[]{:S(2)}, u32[]{:S(2)}) %collective-permute-start.17) | collective-permute-done | bytes 262176 | tf_op jit(solution)/shard_map/ppermute | solution.py:33
  108.6 3.0 %shard_map.71 = (f32[512,512]{1,0:T(8,128)S(1)}, f32[512,512]{1,0:T(8,128)S(1)}) custom-call(s32[4]{0:T(128)S(1)} %pad_add_fusion.idx, bf16[1024,2048]{1,0:T(8,128)(2,1)S(1)} %get-tuple-element.64.x_all, bf16[512,512]{1,0:T(8,128)(2,1)S(1)} %slice.19.own, bf16[512,512]{1,0:T(8,128)(2,1)S(1)} %collective-permute-done.14.up, ...), custom_call_target="tpu_custom_call" | custom-call | tf_op jit(solution)/shard_map/pallas_call | solution.py:256
  112.0 1.4 %shard_map.73 = (bf16[20,2,128,128]{3,2,1,0:T(8,128)(2,1)S(1)}, s32[4,1,512]{2,1,0:T(1,128)S(1)}) custom-call(s32[4]{0:T(128)S(1)} %pad_add_fusion.idx, bf16[1040,128]{1,0:T(8,128)(2,1)S(1)} %collective-permute-done.19.refs_0_, bf16[1040,128]{1,0:T(8,128)(2,1)S(1)} %collective-permute-done.20.refs_1_, bf16[1040,128]{1,0:T(8,128)(2,1)S(1)} %collective-permute-done.21.refs_2_, ...), custom_call_target="tpu_custom_call" | custom-call | flops 68719476736 | bytes 4194304 | tf_op jit(solution)/shard_map/pallas_call | solution.py:256
  115.5 10.7 %shard_map.74 = (bf16[128,512]{1,0:T(8,128)(2,1)S(1)}, bf16[128,512]{1,0:T(8,128)(2,1)S(1)}, bf16[128,512]{1,0:T(8,128)(2,1)S(1)}, bf16[128,512]{1,0:T(8,128)(2,1)S(1)}) custom-call(s32[4]{0:T(128)S(1)} %pad_add_fusion.idx, bf16[4,512,128]{2,1,0:T(8,128)(2,1)S(1)} %shard_map.72.query, bf16[20,2,128,128]{3,2,1,0:T(8,128)(2,1)S(1)} %get-tuple-element.69.kv, ...), custom_call_target="tpu_custom_call" | custom-call | flops 2147483648 | bytes 4194304 | tf_op jit(solution)/shard_map/pallas_call | solution.py:256
  126.9 1.6 %collective-permute-start.24 = (bf16[128,512]{1,0:T(8,128)(2,1)S(1)}, bf16[128,512]{1,0:T(8,128)(2,1)S(1)}, u32[]{:S(2)}, u32[]{:S(2)}) collective-permute-start(bf16[128,512]{1,0:T(8,128)(2,1)S(1)} %get-tuple-element.72), channel_id=1, source_target_pairs={{0,2},{1,0},{2,6},{3,4},{4,3},{5,1},{6,7},{7,5},{8,10},{9,8},{10,1... | collective-permute-start | bytes 393224 | tf_op jit(solution)/shard_map/ppermute | solution.py:33
  128.6 5.9 %collective-permute-start.25 = (bf16[128,512]{1,0:T(8,128)(2,1)S(1)}, bf16[128,512]{1,0:T(8,128)(2,1)S(1)}, u32[]{:S(2)}, u32[]{:S(2)}) collective-permute-start(bf16[128,512]{1,0:T(8,128)(2,1)S(1)} %get-tuple-element.73), channel_id=1, source_target_pairs={{0,4},{1,6},{2,0},{3,2},{4,5},{5,7},{6,1},{7,3},{8,12},{9,14},{10,... | collective-permute-start | bytes 393224 | tf_op jit(solution)/shard_map/ppermute | solution.py:33
  134.5 1.9 %collective-permute-start.26 = (bf16[128,512]{1,0:T(8,128)(2,1)S(1)}, bf16[128,512]{1,0:T(8,128)(2,1)S(1)}, u32[]{:S(2)}, u32[]{:S(2)}) collective-permute-start(bf16[128,512]{1,0:T(8,128)(2,1)S(1)} %get-tuple-element.74), channel_id=1, source_target_pairs={{0,6},{1,4},{2,2},{3,0},{4,7},{5,5},{6,3},{7,1},{8,14},{9,12},{10,... | collective-permute-start | bytes 393224 | tf_op jit(solution)/shard_map/ppermute | solution.py:33
  136.4 1.4 collective-permute-done.25.refs_2_
  137.8 2.9 %collective-permute-done.26.refs_3_ = bf16[128,512]{1,0:T(8,128)(2,1)S(1)} collective-permute-done((bf16[128,512]{1,0:T(8,128)(2,1)S(1)}, bf16[128,512]{1,0:T(8,128)(2,1)S(1)}, u32[]{:S(2)}, u32[]{:S(2)}) %collective-permute-start.26) | collective-permute-done | bytes 131104 | tf_op jit(solution)/shard_map/ppermute | solution.py:33
  140.7 1.4 shard_map.75
  (62 shorter events, 19.4 us)
Async XLA Ops:
  0.0 1.2 copy-start
  1.5 13.0 %collective-permute-start.2 = (f32[256,128]{1,0:T(8,128)S(1)}, f32[256,128]{1,0:T(8,128)S(1)}, u32[]{:S(2)}, u32[]{:S(2)}) collective-permute-start(f32[256,128]{1,0:T(8,128)S(1)} %shard_map.65.squares), channel_id=1, source_target_pairs={{0,1},{1,0},{2,3},{3,2},{4,5},{5,4},{6,7},{7,6},{8,9},{9,8},{10,11... | collective-permute-start | bytes 393224 | tf_op jit(solution)/shard_map/ppermute | solution.py:33
  1.7 0.8 copy-start.2
  4.5 13.6 %collective-permute-start = (bf16[32,768]{1,0:T(8,128)(2,1)S(1)}, bf16[32,768]{1,0:T(8,128)(2,1)S(1)}, u32[]{:S(2)}, u32[]{:S(2)}) collective-permute-start(bf16[32,768]{1,0:T(8,128)(2,1)S(1)} %get-tuple-element.40), channel_id=1, source_target_pairs={{0,0},{1,4},{2,2},{3,6},{4,8},{5,12},{6,10},{7,14},{8,16},{9,20},{... | collective-permute-start | bytes 147464 | tf_op jit(solution)/shard_map/ppermute | solution.py:33
  8.3 9.8 %collective-permute-start.1 = (bf16[32,768]{1,0:T(8,128)(2,1)S(1)}, bf16[32,768]{1,0:T(8,128)(2,1)S(1)}, u32[]{:S(2)}, u32[]{:S(2)}) collective-permute-start(bf16[32,768]{1,0:T(8,128)(2,1)S(1)} %get-tuple-element.41), channel_id=1, source_target_pairs={{0,2},{1,6},{2,0},{3,4},{4,10},{5,14},{6,8},{7,12},{8,18},{9,22},{... | collective-permute-start | bytes 147464 | tf_op jit(solution)/shard_map/ppermute | solution.py:33
  14.5 1.2 copy-start.1
  19.6 31.8 %all-to-all-start = ((bf16[8,64,768]{2,1,0:T(8,128)(2,1)}), bf16[8,64,768]{2,1,0:T(8,128)(2,1)S(1)}, u32[]{:S(2)}, u32[]{:S(2)}) async-start(bf16[8,64,768]{2,1,0:T(8,128)(2,1)} %broadcast_in_dim.2), calls=%async_computation | async-start | bytes 1572864 | tf_op jit(solution)/shard_map/all_to_all | solution.py:276
  28.8 18.4 %collective-permute-start.3 = (bf16[144,2048]{1,0:T(8,128)(2,1)S(1)}, bf16[144,2048]{1,0:T(8,128)(2,1)S(1)}, u32[]{:S(2)}, u32[]{:S(2)}) collective-permute-start(bf16[144,2048]{1,0:T(8,128)(2,1)S(1)} %get-tuple-element.44.refs_0_), channel_id=1, source_target_pairs={{0,2},{1,3},{2,4},{3,5},{4,6},{5,7},{6,0},{7,1},{8,10},{9,11},{10,... | collective-permute-start | bytes 1769480 | tf_op jit(solution)/shard_map/ppermute | solution.py:33
  30.2 15.4 %collective-permute-start.4 = (bf16[128,2048]{1,0:T(8,128)(2,1)}, bf16[128,2048]{1,0:T(8,128)(2,1)}, u32[]{:S(2)}, u32[]{:S(2)}) collective-permute-start(bf16[128,2048]{1,0:T(8,128)(2,1)} %get-tuple-element.47.refs_4_), channel_id=1, source_target_pairs={{0,6},{1,7},{2,0},{3,1},{4,2},{5,3},{6,4},{7,5},{8,14},{9,15},{10,... | collective-permute-start | bytes 1572872 | tf_op jit(solution)/shard_map/ppermute | solution.py:33
  32.9 27.7 %collective-permute-start.8 = (bf16[144,2048]{1,0:T(8,128)(2,1)S(1)}, bf16[144,2048]{1,0:T(8,128)(2,1)S(1)}, u32[]{:S(2)}, u32[]{:S(2)}) collective-permute-start(bf16[144,2048]{1,0:T(8,128)(2,1)S(1)} %get-tuple-element.44.refs_0_), channel_id=1, source_target_pairs={{0,6},{1,7},{2,0},{3,1},{4,2},{5,3},{6,4},{7,5},{8,14},{9,15},{10,... | collective-permute-start | bytes 1769480 | tf_op jit(solution)/shard_map/ppermute | solution.py:33
  34.9 22.4 %collective-permute-start.7 = (bf16[128,2048]{1,0:T(8,128)(2,1)}, bf16[128,2048]{1,0:T(8,128)(2,1)}, u32[]{:S(2)}, u32[]{:S(2)}) collective-permute-start(bf16[128,2048]{1,0:T(8,128)(2,1)} %get-tuple-element.47.refs_4_), channel_id=1, source_target_pairs={{0,2},{1,3},{2,4},{3,5},{4,6},{5,7},{6,0},{7,1},{8,10},{9,11},{10,... | collective-permute-start | bytes 1572872 | tf_op jit(solution)/shard_map/ppermute | solution.py:33
  51.4 0.9 copy-start.6
  52.3 11.3 %collective-permute-start.5 = (bf16[512,256]{1,0:T(8,128)(2,1)S(1)}, bf16[512,256]{1,0:T(8,128)(2,1)S(1)}, u32[]{:S(2)}, u32[]{:S(2)}) collective-permute-start(bf16[512,256]{1,0:T(8,128)(2,1)S(1)} %slice.18.own), channel_id=1, source_target_pairs={{0,8},{1,9},{2,10},{3,11},{4,12},{5,13},{6,14},{7,15},{8,16},{9,17... | collective-permute-start | bytes 786440 | tf_op jit(solution)/shard_map/ppermute | solution.py:33
  54.5 9.1 %collective-permute-start.6 = (bf16[512,256]{1,0:T(8,128)(2,1)S(1)}, bf16[512,256]{1,0:T(8,128)(2,1)S(1)}, u32[]{:S(2)}, u32[]{:S(2)}) collective-permute-start(bf16[512,256]{1,0:T(8,128)(2,1)S(1)} %slice.18.own), channel_id=1, source_target_pairs={{0,24},{1,25},{2,26},{3,27},{4,28},{5,29},{6,30},{7,31},{8,0},{9,1... | collective-permute-start | bytes 786440 | tf_op jit(solution)/shard_map/ppermute | solution.py:33
  57.3 16.1 %collective-permute-start.9 = (bf16[144,2048]{1,0:T(8,128)(2,1)S(1)}, bf16[144,2048]{1,0:T(8,128)(2,1)S(1)}, u32[]{:S(2)}, u32[]{:S(2)}) collective-permute-start(bf16[144,2048]{1,0:T(8,128)(2,1)S(1)} %collective-permute-done.3.refs_1_), channel_id=1, source_target_pairs={{0,2},{1,3},{2,4},{3,5},{4,6},{5,7},{6,0},{7,1},{8,10},{9,11},{10,... | collective-permute-start | bytes 1769480 | tf_op jit(solution)/shard_map/ppermute | solution.py:33
  57.3 16.0 %collective-permute-start.10 = (bf16[128,2048]{1,0:T(8,128)(2,1)}, bf16[128,2048]{1,0:T(8,128)(2,1)}, u32[]{:S(2)}, u32[]{:S(2)}) collective-permute-start(bf16[128,2048]{1,0:T(8,128)(2,1)} %collective-permute-done.4.refs_6_), channel_id=1, source_target_pairs={{0,6},{1,7},{2,0},{3,1},{4,2},{5,3},{6,4},{7,5},{8,14},{9,15},{10,... | collective-permute-start | bytes 1572872 | tf_op jit(solution)/shard_map/ppermute | solution.py:33
  63.6 6.3 %collective-permute-start.11 = (bf16[256,256]{1,0:T(8,128)(2,1)S(1)}, bf16[256,256]{1,0:T(8,128)(2,1)S(1)}, u32[]{:S(2)}, u32[]{:S(2)}) collective-permute-start(bf16[256,256]{1,0:T(8,128)(2,1)S(1)} %slice.20), channel_id=1, source_target_pairs={{0,8},{1,9},{2,10},{3,11},{4,12},{5,13},{6,14},{7,15},{8,16},{9,17... | collective-permute-start | bytes 393224 | tf_op jit(solution)/shard_map/ppermute | solution.py:33
  65.5 5.2 %collective-permute-start.12 = (bf16[256,256]{1,0:T(8,128)(2,1)}, bf16[256,256]{1,0:T(8,128)(2,1)S(1)}, u32[]{:S(2)}, u32[]{:S(2)}) collective-permute-start(bf16[256,256]{1,0:T(8,128)(2,1)} %slice.21), channel_id=1, source_target_pairs={{0,24},{1,25},{2,26},{3,27},{4,28},{5,29},{6,30},{7,31},{8,0},{9,1... | collective-permute-start | bytes 393224 | tf_op jit(solution)/shard_map/ppermute | solution.py:33
  70.7 13.6 %collective-permute-start.14 = (bf16[512,512]{1,0:T(8,128)(2,1)S(1)}, bf16[512,512]{1,0:T(8,128)(2,1)S(1)}, u32[]{:S(2)}, u32[]{:S(2)}) collective-permute-start(bf16[512,512]{1,0:T(8,128)(2,1)S(1)} %slice.19.own), channel_id=1, source_target_pairs={{0,8},{1,9},{2,10},{3,11},{4,12},{5,13},{6,14},{7,15},{8,16},{9,17... | collective-permute-start | bytes 1572872 | tf_op jit(solution)/shard_map/ppermute | solution.py:33
  77.1 7.3 %collective-permute-start.13 = (f32[512,256]{1,0:T(8,128)S(1)}, f32[512,256]{1,0:T(8,128)S(1)}, u32[]{:S(2)}, u32[]{:S(2)}) collective-permute-start(f32[512,256]{1,0:T(8,128)S(1)} %get-tuple-element.60), channel_id=1, source_target_pairs={{0,1},{1,0},{2,3},{3,2},{4,5},{5,4},{6,7},{7,6},{8,9},{9,8},{10,11... | collective-permute-start | bytes 1572872 | tf_op jit(solution)/shard_map/ppermute | solution.py:33
  77.2 20.5 %collective-permute-start.15 = (bf16[512,512]{1,0:T(8,128)(2,1)S(1)}, bf16[512,512]{1,0:T(8,128)(2,1)S(1)}, u32[]{:S(2)}, u32[]{:S(2)}) collective-permute-start(bf16[512,512]{1,0:T(8,128)(2,1)S(1)} %slice.19.own), channel_id=1, source_target_pairs={{0,24},{1,25},{2,26},{3,27},{4,28},{5,29},{6,30},{7,31},{8,0},{9,1... | collective-permute-start | bytes 1572872 | tf_op jit(solution)/shard_map/ppermute | solution.py:33
  84.3 13.4 %collective-permute-start.16 = (bf16[256,512]{1,0:T(8,128)(2,1)S(1)}, bf16[256,512]{1,0:T(8,128)(2,1)S(1)}, u32[]{:S(2)}, u32[]{:S(2)}) collective-permute-start(bf16[256,512]{1,0:T(8,128)(2,1)S(1)} %slice.24), channel_id=1, source_target_pairs={{0,8},{1,9},{2,10},{3,11},{4,12},{5,13},{6,14},{7,15},{8,16},{9,17... | collective-permute-start | bytes 786440 | tf_op jit(solution)/shard_map/ppermute | solution.py:33
  84.7 27.2 %collective-permute-start.19 = (bf16[1040,128]{1,0:T(8,128)(2,1)S(1)}, bf16[1040,128]{1,0:T(8,128)(2,1)S(1)}, u32[]{:S(2)}, u32[]{:S(2)}) collective-permute-start(bf16[1040,128]{1,0:T(8,128)(2,1)S(1)} %shard_map.70.refs_4_), channel_id=1, source_target_pairs={{0,32},{1,33},{2,34},{3,35},{4,36},{5,37},{6,38},{7,39},{8,40},{9,... | collective-permute-start | bytes 798728 | tf_op jit(solution)/shard_map/ppermute | solution.py:33
  84.8 27.1 %collective-permute-start.20 = (bf16[1040,128]{1,0:T(8,128)(2,1)S(1)}, bf16[1040,128]{1,0:T(8,128)(2,1)S(1)}, u32[]{:S(2)}, u32[]{:S(2)}) collective-permute-start(bf16[1040,128]{1,0:T(8,128)(2,1)S(1)} %shard_map.70.refs_4_), channel_id=1, source_target_pairs={{0,24},{1,25},{2,26},{3,27},{4,28},{5,29},{6,30},{7,31},{8,32},{9,... | collective-permute-start | bytes 798728 | tf_op jit(solution)/shard_map/ppermute | solution.py:33
  88.1 23.8 %collective-permute-start.21 = (bf16[1040,128]{1,0:T(8,128)(2,1)S(1)}, bf16[1040,128]{1,0:T(8,128)(2,1)S(1)}, u32[]{:S(2)}, u32[]{:S(2)}) collective-permute-start(bf16[1040,128]{1,0:T(8,128)(2,1)S(1)} %shard_map.70.refs_4_), channel_id=1, source_target_pairs={{0,16},{1,17},{2,18},{3,19},{4,20},{5,21},{6,22},{7,23},{8,24},{9,... | collective-permute-start | bytes 798728 | tf_op jit(solution)/shard_map/ppermute | solution.py:33
  97.7 14.3 %collective-permute-start.22 = (bf16[1040,128]{1,0:T(8,128)(2,1)S(1)}, bf16[1040,128]{1,0:T(8,128)(2,1)S(1)}, u32[]{:S(2)}, u32[]{:S(2)}) collective-permute-start(bf16[1040,128]{1,0:T(8,128)(2,1)S(1)} %shard_map.70.refs_4_), channel_id=1, source_target_pairs={{0,8},{1,9},{2,10},{3,11},{4,12},{5,13},{6,14},{7,15},{8,16},{9,17... | collective-permute-start | bytes 798728 | tf_op jit(solution)/shard_map/ppermute | solution.py:33
  97.7 10.9 %collective-permute-start.17 = (bf16[256,512]{1,0:T(8,128)(2,1)S(1)}, bf16[256,512]{1,0:T(8,128)(2,1)S(1)}, u32[]{:S(2)}, u32[]{:S(2)}) collective-permute-start(bf16[256,512]{1,0:T(8,128)(2,1)S(1)} %slice.25), channel_id=1, source_target_pairs={{0,24},{1,25},{2,26},{3,27},{4,28},{5,29},{6,30},{7,31},{8,0},{9,1... | collective-permute-start | bytes 786440 | tf_op jit(solution)/shard_map/ppermute | solution.py:33
  111.6 3.0 %collective-permute-start.18 = (f32[512,512]{1,0:T(8,128)S(1)}, f32[512,512]{1,0:T(8,128)S(1)}, u32[]{:S(2)}, u32[]{:S(2)}) collective-permute-start(f32[512,512]{1,0:T(8,128)S(1)} %get-tuple-element.67), channel_id=1, source_target_pairs={{0,1},{1,0},{2,3},{3,2},{4,5},{5,4},{6,7},{7,6},{8,9},{9,8},{10,11... | collective-permute-start | bytes 3145736 | tf_op jit(solution)/shard_map/ppermute | solution.py:33
  126.3 10.1 %collective-permute-start.23 = (bf16[128,512]{1,0:T(8,128)(2,1)S(1)}, bf16[128,512]{1,0:T(8,128)(2,1)S(1)}, u32[]{:S(2)}, u32[]{:S(2)}) collective-permute-start(bf16[128,512]{1,0:T(8,128)(2,1)S(1)} %get-tuple-element.71), channel_id=1, source_target_pairs={{0,0},{1,2},{2,4},{3,6},{4,1},{5,3},{6,5},{7,7},{8,8},{9,10},{10,1... | collective-permute-start | bytes 393224 | tf_op jit(solution)/shard_map/ppermute | solution.py:33
  126.9 9.4 %collective-permute-start.24 = (bf16[128,512]{1,0:T(8,128)(2,1)S(1)}, bf16[128,512]{1,0:T(8,128)(2,1)S(1)}, u32[]{:S(2)}, u32[]{:S(2)}) collective-permute-start(bf16[128,512]{1,0:T(8,128)(2,1)S(1)} %get-tuple-element.72), channel_id=1, source_target_pairs={{0,2},{1,0},{2,6},{3,4},{4,3},{5,1},{6,7},{7,5},{8,10},{9,8},{10,1... | collective-permute-start | bytes 393224 | tf_op jit(solution)/shard_map/ppermute | solution.py:33
  128.6 9.2 %collective-permute-start.25 = (bf16[128,512]{1,0:T(8,128)(2,1)S(1)}, bf16[128,512]{1,0:T(8,128)(2,1)S(1)}, u32[]{:S(2)}, u32[]{:S(2)}) collective-permute-start(bf16[128,512]{1,0:T(8,128)(2,1)S(1)} %get-tuple-element.73), channel_id=1, source_target_pairs={{0,4},{1,6},{2,0},{3,2},{4,5},{5,7},{6,1},{7,3},{8,12},{9,14},{10,... | collective-permute-start | bytes 393224 | tf_op jit(solution)/shard_map/ppermute | solution.py:33
  134.5 6.3 %collective-permute-start.26 = (bf16[128,512]{1,0:T(8,128)(2,1)S(1)}, bf16[128,512]{1,0:T(8,128)(2,1)S(1)}, u32[]{:S(2)}, u32[]{:S(2)}) collective-permute-start(bf16[128,512]{1,0:T(8,128)(2,1)S(1)} %get-tuple-element.74), channel_id=1, source_target_pairs={{0,6},{1,4},{2,2},{3,0},{4,7},{5,5},{6,3},{7,1},{8,14},{9,12},{10,... | collective-permute-start | bytes 393224 | tf_op jit(solution)/shard_map/ppermute | solution.py:33
  (3 other events, 2.1 us)

commit v3 on v2

--- a/solution.py
+++ b/solution.py
@@ -132,13 +132,12 @@
         )
 
 
-def project_kernel(idx, x_all, own, up, down, far_up, far_down, keep, send, w_all):
-    columns = own.shape[1]
-    for ref, d, first in ((own, 0, 0), (up, -1, 0), (down, 1, 0), (far_up, 2, 0), (far_down, 2, 4)):
+def project_kernel(idx, x_all, own, up, down, far, keep, send, w_all):
+    for ref, d in ((own, 0), (up, -1), (down, 1), (far, 2)):
         shift = pl.multiple_of(lax.rem(idx[1] + d + NY, NY) * 64, 64)
-        for z in range(ref.shape[0] // 64):
-            w_all[first + z, pl.ds(shift, 64), :] = ref[z * 64 : z * 64 + 64, :]
-    multiply(x_all, w_all[...].reshape(HALF, columns), keep, send)
+        for z in range(NZ):
+            w_all[z, pl.ds(shift, 64), :] = ref[z * 64 : z * 64 + 64, :]
+    multiply(x_all, w_all[...].reshape(HALF, own.shape[1]), keep, send)
 
 
 def turned(value, cos, sin):
@@ -313,11 +312,10 @@
 
     kv0, q0 = w_z[:, 512:], w_z[:, :512]
     kv_up, kv_down = along_y(kv0, 1), along_y(kv0, -1)
-    kv_up, kv_down, right_b, left_a = tie(kv_up, kv_down, right_b, left_a)
-    kv_far_up, kv_far_down = along_y(kv_up[:256], 1), along_y(kv_down[256:], -1)
-    q0, kv_far_up, kv_far_down = tie(q0, kv_far_up, kv_far_down)
+    kv_up, kv_down, right_b, left_a, q0 = tie(kv_up, kv_down, right_b, left_a, q0)
+    kv_far = along_y(kv_up, 1)
     q_up, q_down = along_y(q0, 1), along_y(q0, -1)
-    q_far_up, q_far_down = along_y(q_up[:256], 1), along_y(q_down[256:], -1)
+    q_far = along_y(q_down, -1)
     x_all, docs = call(
         stack_kernel,
         (shape((1024, HALF), BF), shape((16, HD), BF)),
@@ -334,7 +332,7 @@
     keep, send = call(
         project_kernel,
         (shape((512, 256), F32), shape((512, 256), F32)),
-        (where, x_all, kv0, kv_up, kv_down, kv_far_up, kv_far_down),
+        (where, x_all, kv0, kv_up, kv_down, kv_far),
         (pltpu.VMEM((NZ, 256, 256), BF),),
         cost(2 * 1024 * HALF * 256, 10 << 20),
     )
@@ -354,9 +352,9 @@
     keep, send = call(
         project_kernel,
         (shape((512, 512), F32), shape((512, 512), F32)),
-        (where, x_all, q0, q_up, q_down, q_far_up, q_far_down),
+        (where, x_all, q0, q_up, q_down, q_far),
         (pltpu.VMEM((NZ, 256, 512), BF),),
-        cost(0, 0),
+        cost(2 * 1024 * HALF * 512, 10 << 20),
     )
     got = permute(send, lambda z, y, x, c: (z, y, x, 1 - c))
     query = call(

time: 141 us -> 136 us (0.965)
  the two profiles are of different devices: /device:TPU:32 before, /device:TPU:48 now
where the time goes in v3:
time: 136 us; the launch traced here: 135 us
  starting transfers between devices  54.8 us (40%)
  waiting for transfers between devices  46.4 us (34%)
  Pallas kernels  21.4 us (16%)
  local copies, waits for them, and re-layouts  10.9 us (8%)
    ppermute x25, starting transfers between devices, permute(): return lax.ppermute(value, AXES, pairs)  46.2 us
    ppermute x25, waiting for transfers between devices, permute(): return lax.ppermute(value, AXES, pairs)  41.9 us
    pallas_call x12, Pallas kernels, call(): pl.pallas_call(kernel, out_shape=shapes, in_specs=[SMEM] * smem + [VMEM]...  21.4 us
    all_to_all x1, starting transfers between devices, copies(): lax.all_to_all(jnp.broadcast_to(value[None], (count, *value.shape)), axis...  8.57 us
    unnamed x18, local copies, waits for them, and re-layouts  8.13 us
    all_to_all x1, waiting for transfers between devices, copies(): lax.all_to_all(jnp.broadcast_to(value[None], (count, *value.shape)), axis...  4.55 us
  transfers between devices with their start and end apart: 26, of which 12 were waited for; matrix products, arithmetic and copies ran while one was open for 2% of the time, Pallas kernels for 7%

profile of v3, /device:TPU:48, one launch (start us, length us, event | category | flops | bytes accessed | tf_op | source)
XLA Modules:
  0.0 134.9 jit_solution(10281490788014850242)
XLA Ops:
  0.0 1.2 copy-done
  4.5 5.0 %collective-permute-start = (bf16[32,768]{1,0:T(8,128)(2,1)S(1)}, bf16[32,768]{1,0:T(8,128)(2,1)S(1)}, u32[]{:S(2)}, u32[]{:S(2)}) collective-permute-start(bf16[32,768]{1,0:T(8,128)(2,1)S(1)} %get-tuple-element.38), channel_id=1, source_target_pairs={{0,0},{1,4},{2,2},{3,6},{4,8},{5,12},{6,10},{7,14},{8,16},{9,20},{... | collective-permute-start | bytes 147464 | tf_op jit(solution)/shard_map/ppermute | solution.py:33
  9.5 5.0 %collective-permute-start.1 = (bf16[32,768]{1,0:T(8,128)(2,1)S(1)}, bf16[32,768]{1,0:T(8,128)(2,1)S(1)}, u32[]{:S(2)}, u32[]{:S(2)}) collective-permute-start(bf16[32,768]{1,0:T(8,128)(2,1)S(1)} %get-tuple-element.39), channel_id=1, source_target_pairs={{0,2},{1,6},{2,0},{3,4},{4,10},{5,14},{6,8},{7,12},{8,18},{9,22},{... | collective-permute-start | bytes 147464 | tf_op jit(solution)/shard_map/ppermute | solution.py:33
  15.2 1.2 copy-done.1
  19.5 8.6 %all-to-all-start = ((bf16[8,64,768]{2,1,0:T(8,128)(2,1)}), bf16[8,64,768]{2,1,0:T(8,128)(2,1)S(1)}, u32[]{:S(2)}, u32[]{:S(2)}) async-start(bf16[8,64,768]{2,1,0:T(8,128)(2,1)} %broadcast_in_dim.2), calls=%async_computation | async-start | bytes 1572864 | tf_op jit(solution)/shard_map/all_to_all | solution.py:275
  28.5 2.8 %collective-permute-start.4 = (bf16[128,2048]{1,0:T(8,128)(2,1)S(1)}, bf16[128,2048]{1,0:T(8,128)(2,1)S(1)}, u32[]{:S(2)}, u32[]{:S(2)}) collective-permute-start(bf16[128,2048]{1,0:T(8,128)(2,1)S(1)} %get-tuple-element.45.refs_4_), channel_id=1, source_target_pairs={{0,6},{1,7},{2,0},{3,1},{4,2},{5,3},{6,4},{7,5},{8,14},{9,15},{10,... | collective-permute-start | bytes 1572872 | tf_op jit(solution)/shard_map/ppermute | solution.py:33
  33.4 10.4 %collective-permute-done.4.refs_6_ = bf16[128,2048]{1,0:T(8,128)(2,1)S(1)} collective-permute-done((bf16[128,2048]{1,0:T(8,128)(2,1)S(1)}, bf16[128,2048]{1,0:T(8,128)(2,1)S(1)}, u32[]{:S(2)}, u32[]{:S(2)}) %collective-permute-start.4) | collective-permute-done | bytes 524320 | tf_op jit(solution)/shard_map/ppermute | solution.py:33
  45.6 4.5 %all-to-all-done = bf16[8,64,768]{2,1,0:T(8,128)(2,1)S(1)} async-done(((bf16[8,64,768]{2,1,0:T(8,128)(2,1)}), bf16[8,64,768]{2,1,0:T(8,128)(2,1)S(1)}, u32[]{:S(2)}, u32[]{:S(2)}) %all-to-all-start) | async-done | bytes 786464 | tf_op jit(solution)/shard_map/all_to_all | solution.py:275
  51.0 4.5 %collective-permute-start.5 = (bf16[512,256]{1,0:T(8,128)(2,1)S(1)}, bf16[512,256]{1,0:T(8,128)(2,1)S(1)}, u32[]{:S(2)}, u32[]{:S(2)}) collective-permute-start(bf16[512,256]{1,0:T(8,128)(2,1)S(1)} %slice.6.own), channel_id=1, source_target_pairs={{0,8},{1,9},{2,10},{3,11},{4,12},{5,13},{6,14},{7,15},{8,16},{9,17... | collective-permute-start | bytes 786440 | tf_op jit(solution)/shard_map/ppermute | solution.py:33
  55.5 3.2 %collective-permute-start.10 = (bf16[128,2048]{1,0:T(8,128)(2,1)}, bf16[128,2048]{1,0:T(8,128)(2,1)}, u32[]{:S(2)}, u32[]{:S(2)}) collective-permute-start(bf16[128,2048]{1,0:T(8,128)(2,1)} %copy-done.2), channel_id=1, source_target_pairs={{0,6},{1,7},{2,0},{3,1},{4,2},{5,3},{6,4},{7,5},{8,14},{9,15},{10,... | collective-permute-start | bytes 1572872 | tf_op jit(solution)/shard_map/ppermute | solution.py:33
  59.8 1.3 collective-permute-done.5.up
  61.1 2.3 %collective-permute-done.6.down = bf16[512,256]{1,0:T(8,128)(2,1)} collective-permute-done((bf16[512,256]{1,0:T(8,128)(2,1)S(1)}, bf16[512,256]{1,0:T(8,128)(2,1)}, u32[]{:S(2)}, u32[]{:S(2)}) %collective-permute-start.6) | collective-permute-done | bytes 262176 | tf_op jit(solution)/shard_map/ppermute | solution.py:33
  63.7 1.7 %collective-permute-start.11 = (bf16[512,256]{1,0:T(8,128)(2,1)S(1)}, bf16[512,256]{1,0:T(8,128)(2,1)S(1)}, u32[]{:S(2)}, u32[]{:S(2)}) collective-permute-start(bf16[512,256]{1,0:T(8,128)(2,1)S(1)} %collective-permute-done.5.up), channel_id=1, source_target_pairs={{0,8},{1,9},{2,10},{3,11},{4,12},{5,13},{6,14},{7,15},{8,16},{9,17... | collective-permute-start | bytes 786440 | tf_op jit(solution)/shard_map/ppermute | solution.py:33
  66.4 3.3 %collective-permute-done.10.refs_7_ = bf16[128,2048]{1,0:T(8,128)(2,1)} collective-permute-done((bf16[128,2048]{1,0:T(8,128)(2,1)}, bf16[128,2048]{1,0:T(8,128)(2,1)}, u32[]{:S(2)}, u32[]{:S(2)}) %collective-permute-start.10) | collective-permute-done | bytes 524320 | tf_op jit(solution)/shard_map/ppermute | solution.py:33
  69.7 1.8 %collective-permute-done.9.refs_3_ = bf16[144,2048]{1,0:T(8,128)(2,1)S(1)} collective-permute-done((bf16[144,2048]{1,0:T(8,128)(2,1)S(1)}, bf16[144,2048]{1,0:T(8,128)(2,1)S(1)}, u32[]{:S(2)}, u32[]{:S(2)}) %collective-permute-start.9) | collective-permute-done | bytes 589856 | tf_op jit(solution)/shard_map/ppermute | solution.py:33
  72.6 1.5 %shard_map.68 = (bf16[1024,2048]{1,0:T(8,128)(2,1)S(1)}, bf16[16,128]{1,0:T(8,128)(2,1)S(1)}) custom-call(s32[4]{0:T(128)S(1)} %pad_add_fusion.idx, bf16[144,2048]{1,0:T(8,128)(2,1)S(1)} %get-tuple-element.42.refs_0_, bf16[144,2048]{1,0:T(8,128)(2,1)S(1)} %collective-permute-done.3.refs_1_, bf16[144,2048]{1,0:T(8,128)(2,1)S(1)} %collective-permute-done.8.refs_2_, ...), custom_call_target="tpu_custom_call" | custom-call | bytes 8388608 | tf_op jit(solution)/shard_map/pallas_call | solution.py:255
  74.1 2.3 %shard_map.69 = (f32[512,256]{1,0:T(8,128)S(1)}, f32[512,256]{1,0:T(8,128)S(1)}) custom-call(s32[4]{0:T(128)S(1)} %pad_add_fusion.idx, bf16[1024,2048]{1,0:T(8,128)(2,1)S(1)} %get-tuple-element.60.x_all, bf16[512,256]{1,0:T(8,128)(2,1)S(1)} %slice.6.own, bf16[512,256]{1,0:T(8,128)(2,1)S(1)} %collective-permute-done.5.up, ...), custom_call_target="tpu_custom_call" | custom-call | flops 1073741824 | bytes 10485760 | tf_op jit(solution)/shard_map/pallas_call | solution.py:255
  76.5 2.3 %collective-permute-start.13 = (bf16[512,512]{1,0:T(8,128)(2,1)S(1)}, bf16[512,512]{1,0:T(8,128)(2,1)S(1)}, u32[]{:S(2)}, u32[]{:S(2)}) collective-permute-start(bf16[512,512]{1,0:T(8,128)(2,1)S(1)} %slice.7.own), channel_id=1, source_target_pairs={{0,8},{1,9},{2,10},{3,11},{4,12},{5,13},{6,14},{7,15},{8,16},{9,17... | collective-permute-start | bytes 1572872 | tf_op jit(solution)/shard_map/ppermute | solution.py:33
  79.1 1.5 %collective-permute-start.17 = (bf16[1040,128]{1,0:T(8,128)(2,1)S(1)}, bf16[1040,128]{1,0:T(8,128)(2,1)S(1)}, u32[]{:S(2)}, u32[]{:S(2)}) collective-permute-start(bf16[1040,128]{1,0:T(8,128)(2,1)S(1)} %shard_map.70.refs_4_), channel_id=1, source_target_pairs={{0,32},{1,33},{2,34},{3,35},{4,36},{5,37},{6,38},{7,39},{8,40},{9,... | collective-permute-start | bytes 798728 | tf_op jit(solution)/shard_map/ppermute | solution.py:33
  81.8 3.9 %collective-permute-start.19 = (bf16[1040,128]{1,0:T(8,128)(2,1)S(1)}, bf16[1040,128]{1,0:T(8,128)(2,1)S(1)}, u32[]{:S(2)}, u32[]{:S(2)}) collective-permute-start(bf16[1040,128]{1,0:T(8,128)(2,1)S(1)} %shard_map.70.refs_4_), channel_id=1, source_target_pairs={{0,16},{1,17},{2,18},{3,19},{4,20},{5,21},{6,22},{7,23},{8,24},{9,... | collective-permute-start | bytes 798728 | tf_op jit(solution)/shard_map/ppermute | solution.py:33
  85.6 5.2 %collective-permute-done.13.up = bf16[512,512]{1,0:T(8,128)(2,1)S(1)} collective-permute-done((bf16[512,512]{1,0:T(8,128)(2,1)S(1)}, bf16[512,512]{1,0:T(8,128)(2,1)S(1)}, u32[]{:S(2)}, u32[]{:S(2)}) %collective-permute-start.13) | collective-permute-done | bytes 524320 | tf_op jit(solution)/shard_map/ppermute | solution.py:33
  90.8 2.2 %collective-permute-start.20 = (bf16[1040,128]{1,0:T(8,128)(2,1)S(1)}, bf16[1040,128]{1,0:T(8,128)(2,1)S(1)}, u32[]{:S(2)}, u32[]{:S(2)}) collective-permute-start(bf16[1040,128]{1,0:T(8,128)(2,1)S(1)} %shard_map.70.refs_4_), channel_id=1, source_target_pairs={{0,8},{1,9},{2,10},{3,11},{4,12},{5,13},{6,14},{7,15},{8,16},{9,17... | collective-permute-start | bytes 798728 | tf_op jit(solution)/shard_map/ppermute | solution.py:33
  93.0 11.1 %collective-permute-done.15.far = bf16[512,512]{1,0:T(8,128)(2,1)S(1)} collective-permute-done((bf16[512,512]{1,0:T(8,128)(2,1)S(1)}, bf16[512,512]{1,0:T(8,128)(2,1)S(1)}, u32[]{:S(2)}, u32[]{:S(2)}) %collective-permute-start.15) | collective-permute-done | bytes 524320 | tf_op jit(solution)/shard_map/ppermute | solution.py:33
  104.1 3.1 %shard_map.71 = (f32[512,512]{1,0:T(8,128)S(1)}, f32[512,512]{1,0:T(8,128)S(1)}) custom-call(s32[4]{0:T(128)S(1)} %pad_add_fusion.idx, bf16[1024,2048]{1,0:T(8,128)(2,1)S(1)} %get-tuple-element.60.x_all, bf16[512,512]{1,0:T(8,128)(2,1)S(1)} %slice.7.own, bf16[512,512]{1,0:T(8,128)(2,1)S(1)} %collective-permute-done.13.up, ...), custom_call_target="tpu_custom_call" | custom-call | flops 2147483648 | bytes 10485760 | tf_op jit(solution)/shard_map/pallas_call | solution.py:255
  107.6 1.4 %shard_map.73 = (bf16[20,2,128,128]{3,2,1,0:T(8,128)(2,1)S(1)}, s32[4,1,512]{2,1,0:T(1,128)S(1)}) custom-call(s32[4]{0:T(128)S(1)} %pad_add_fusion.idx, bf16[1040,128]{1,0:T(8,128)(2,1)S(1)} %collective-permute-done.17.refs_0_, bf16[1040,128]{1,0:T(8,128)(2,1)S(1)} %collective-permute-done.18.refs_1_, bf16[1040,128]{1,0:T(8,128)(2,1)S(1)} %collective-permute-done.19.refs_2_, ...), custom_call_target="tpu_custom_call" | custom-call | flops 68719476736 | bytes 4194304 | tf_op jit(solution)/shard_map/pallas_call | solution.py:255
  109.0 1.2 collective-permute-done.16.got
  111.1 8.2 %shard_map.74 = (bf16[128,512]{1,0:T(8,128)(2,1)S(1)}, bf16[128,512]{1,0:T(8,128)(2,1)S(1)}, bf16[128,512]{1,0:T(8,128)(2,1)S(1)}, bf16[128,512]{1,0:T(8,128)(2,1)S(1)}) custom-call(s32[4]{0:T(128)S(1)} %pad_add_fusion.idx, bf16[4,512,128]{2,1,0:T(8,128)(2,1)S(1)} %shard_map.72.query, bf16[20,2,128,128]{3,2,1,0:T(8,128)(2,1)S(1)} %get-tuple-element.65.kv, ...), custom_call_target="tpu_custom_call" | custom-call | flops 2147483648 | bytes 4194304 | tf_op jit(solution)/shard_map/pallas_call | solution.py:255
  119.9 1.2 collective-permute-start.22
  121.2 6.0 %collective-permute-start.23 = (bf16[128,512]{1,0:T(8,128)(2,1)S(1)}, bf16[128,512]{1,0:T(8,128)(2,1)S(1)}, u32[]{:S(2)}, u32[]{:S(2)}) collective-permute-start(bf16[128,512]{1,0:T(8,128)(2,1)S(1)} %get-tuple-element.69), channel_id=1, source_target_pairs={{0,4},{1,6},{2,0},{3,2},{4,5},{5,7},{6,1},{7,3},{8,12},{9,14},{10,... | collective-permute-start | bytes 393224 | tf_op jit(solution)/shard_map/ppermute | solution.py:33
  127.2 1.9 %collective-permute-start.24 = (bf16[128,512]{1,0:T(8,128)(2,1)S(1)}, bf16[128,512]{1,0:T(8,128)(2,1)S(1)}, u32[]{:S(2)}, u32[]{:S(2)}) collective-permute-start(bf16[128,512]{1,0:T(8,128)(2,1)S(1)} %get-tuple-element.70), channel_id=1, source_target_pairs={{0,6},{1,4},{2,2},{3,0},{4,7},{5,5},{6,3},{7,1},{8,14},{9,12},{10,... | collective-permute-start | bytes 393224 | tf_op jit(solution)/shard_map/ppermute | solution.py:33
  129.7 3.8 %collective-permute-done.24.refs_3_ = bf16[128,512]{1,0:T(8,128)(2,1)S(1)} collective-permute-done((bf16[128,512]{1,0:T(8,128)(2,1)S(1)}, bf16[128,512]{1,0:T(8,128)(2,1)S(1)}, u32[]{:S(2)}, u32[]{:S(2)}) %collective-permute-start.24) | collective-permute-done | bytes 131104 | tf_op jit(solution)/shard_map/ppermute | solution.py:33
  133.5 1.4 %shard_map.75 = bf16[2,128,1024]{2,1,0:T(8,128)(2,1)} custom-call(s32[4]{0:T(128)S(1)} %pad_add_fusion.idx, bf16[128,512]{1,0:T(8,128)(2,1)S(1)} %collective-permute-done.21.refs_0_, bf16[128,512]{1,0:T(8,128)(2,1)S(1)} %collective-permute-done.22.refs_1_, bf16[128,512]{1,0:T(8,128)(2,1)S(1)} %collective-permute-done.23.refs_2_, ...), custom_call_target="tpu_custom_call" | custom-call | bytes 1048576 | tf_op jit(solution)/shard_map/pallas_call | solution.py:255
  (58 shorter events, 19.7 us)
Async XLA Ops:
  0.0 1.2 copy-start
  1.5 13.7 %collective-permute-start.2 = (f32[256,128]{1,0:T(8,128)S(1)}, f32[256,128]{1,0:T(8,128)S(1)}, u32[]{:S(2)}, u32[]{:S(2)}) collective-permute-start(f32[256,128]{1,0:T(8,128)S(1)} %shard_map.65.squares), channel_id=1, source_target_pairs={{0,1},{1,0},{2,3},{3,2},{4,5},{5,4},{6,7},{7,6},{8,9},{9,8},{10,11... | collective-permute-start | bytes 393224 | tf_op jit(solution)/shard_map/ppermute | solution.py:33
  1.7 0.8 copy-start.4
  4.5 13.5 %collective-permute-start = (bf16[32,768]{1,0:T(8,128)(2,1)S(1)}, bf16[32,768]{1,0:T(8,128)(2,1)S(1)}, u32[]{:S(2)}, u32[]{:S(2)}) collective-permute-start(bf16[32,768]{1,0:T(8,128)(2,1)S(1)} %get-tuple-element.38), channel_id=1, source_target_pairs={{0,0},{1,4},{2,2},{3,6},{4,8},{5,12},{6,10},{7,14},{8,16},{9,20},{... | collective-permute-start | bytes 147464 | tf_op jit(solution)/shard_map/ppermute | solution.py:33
  9.5 8.5 %collective-permute-start.1 = (bf16[32,768]{1,0:T(8,128)(2,1)S(1)}, bf16[32,768]{1,0:T(8,128)(2,1)S(1)}, u32[]{:S(2)}, u32[]{:S(2)}) collective-permute-start(bf16[32,768]{1,0:T(8,128)(2,1)S(1)} %get-tuple-element.39), channel_id=1, source_target_pairs={{0,2},{1,6},{2,0},{3,4},{4,10},{5,14},{6,8},{7,12},{8,18},{9,22},{... | collective-permute-start | bytes 147464 | tf_op jit(solution)/shard_map/ppermute | solution.py:33
  15.2 1.2 copy-start.1
  19.5 30.6 %all-to-all-start = ((bf16[8,64,768]{2,1,0:T(8,128)(2,1)}), bf16[8,64,768]{2,1,0:T(8,128)(2,1)S(1)}, u32[]{:S(2)}, u32[]{:S(2)}) async-start(bf16[8,64,768]{2,1,0:T(8,128)(2,1)} %broadcast_in_dim.2), calls=%async_computation | async-start | bytes 1572864 | tf_op jit(solution)/shard_map/all_to_all | solution.py:275
  28.1 17.5 %collective-permute-start.3 = (bf16[144,2048]{1,0:T(8,128)(2,1)S(1)}, bf16[144,2048]{1,0:T(8,128)(2,1)S(1)}, u32[]{:S(2)}, u32[]{:S(2)}) collective-permute-start(bf16[144,2048]{1,0:T(8,128)(2,1)S(1)} %get-tuple-element.42.refs_0_), channel_id=1, source_target_pairs={{0,2},{1,3},{2,4},{3,5},{4,6},{5,7},{6,0},{7,1},{8,10},{9,11},{10,... | collective-permute-start | bytes 1769480 | tf_op jit(solution)/shard_map/ppermute | solution.py:33
  28.5 15.2 %collective-permute-start.4 = (bf16[128,2048]{1,0:T(8,128)(2,1)S(1)}, bf16[128,2048]{1,0:T(8,128)(2,1)S(1)}, u32[]{:S(2)}, u32[]{:S(2)}) collective-permute-start(bf16[128,2048]{1,0:T(8,128)(2,1)S(1)} %get-tuple-element.45.refs_4_), channel_id=1, source_target_pairs={{0,6},{1,7},{2,0},{3,1},{4,2},{5,3},{6,4},{7,5},{8,14},{9,15},{10,... | collective-permute-start | bytes 1572872 | tf_op jit(solution)/shard_map/ppermute | solution.py:33
  31.3 28.5 %collective-permute-start.8 = (bf16[144,2048]{1,0:T(8,128)(2,1)S(1)}, bf16[144,2048]{1,0:T(8,128)(2,1)S(1)}, u32[]{:S(2)}, u32[]{:S(2)}) collective-permute-start(bf16[144,2048]{1,0:T(8,128)(2,1)S(1)} %get-tuple-element.42.refs_0_), channel_id=1, source_target_pairs={{0,6},{1,7},{2,0},{3,1},{4,2},{5,3},{6,4},{7,5},{8,14},{9,15},{10,... | collective-permute-start | bytes 1769480 | tf_op jit(solution)/shard_map/ppermute | solution.py:33
  32.4 23.1 %collective-permute-start.7 = (bf16[128,2048]{1,0:T(8,128)(2,1)S(1)}, bf16[128,2048]{1,0:T(8,128)(2,1)}, u32[]{:S(2)}, u32[]{:S(2)}) collective-permute-start(bf16[128,2048]{1,0:T(8,128)(2,1)S(1)} %get-tuple-element.45.refs_4_), channel_id=1, source_target_pairs={{0,2},{1,3},{2,4},{3,5},{4,6},{5,7},{6,0},{7,1},{8,10},{9,11},{10,... | collective-permute-start | bytes 1572872 | tf_op jit(solution)/shard_map/ppermute | solution.py:33
  43.7 0.8 copy-start.2
  50.1 0.9 copy-start.8
  51.0 10.1 %collective-permute-start.5 = (bf16[512,256]{1,0:T(8,128)(2,1)S(1)}, bf16[512,256]{1,0:T(8,128)(2,1)S(1)}, u32[]{:S(2)}, u32[]{:S(2)}) collective-permute-start(bf16[512,256]{1,0:T(8,128)(2,1)S(1)} %slice.6.own), channel_id=1, source_target_pairs={{0,8},{1,9},{2,10},{3,11},{4,12},{5,13},{6,14},{7,15},{8,16},{9,17... | collective-permute-start | bytes 786440 | tf_op jit(solution)/shard_map/ppermute | solution.py:33
  55.5 7.9 %collective-permute-start.6 = (bf16[512,256]{1,0:T(8,128)(2,1)S(1)}, bf16[512,256]{1,0:T(8,128)(2,1)}, u32[]{:S(2)}, u32[]{:S(2)}) collective-permute-start(bf16[512,256]{1,0:T(8,128)(2,1)S(1)} %slice.6.own), channel_id=1, source_target_pairs={{0,24},{1,25},{2,26},{3,27},{4,28},{5,29},{6,30},{7,31},{8,0},{9,1... | collective-permute-start | bytes 786440 | tf_op jit(solution)/shard_map/ppermute | solution.py:33
  55.5 16.0 %collective-permute-start.9 = (bf16[144,2048]{1,0:T(8,128)(2,1)S(1)}, bf16[144,2048]{1,0:T(8,128)(2,1)S(1)}, u32[]{:S(2)}, u32[]{:S(2)}) collective-permute-start(bf16[144,2048]{1,0:T(8,128)(2,1)S(1)} %collective-permute-done.3.refs_1_), channel_id=1, source_target_pairs={{0,2},{1,3},{2,4},{3,5},{4,6},{5,7},{6,0},{7,1},{8,10},{9,11},{10,... | collective-permute-start | bytes 1769480 | tf_op jit(solution)/shard_map/ppermute | solution.py:33
  55.5 14.2 %collective-permute-start.10 = (bf16[128,2048]{1,0:T(8,128)(2,1)}, bf16[128,2048]{1,0:T(8,128)(2,1)}, u32[]{:S(2)}, u32[]{:S(2)}) collective-permute-start(bf16[128,2048]{1,0:T(8,128)(2,1)} %copy-done.2), channel_id=1, source_target_pairs={{0,6},{1,7},{2,0},{3,1},{4,2},{5,3},{6,4},{7,5},{8,14},{9,15},{10,... | collective-permute-start | bytes 1572872 | tf_op jit(solution)/shard_map/ppermute | solution.py:33
  63.4 15.3 %collective-permute-start.14 = (bf16[512,512]{1,0:T(8,128)(2,1)S(1)}, bf16[512,512]{1,0:T(8,128)(2,1)S(1)}, u32[]{:S(2)}, u32[]{:S(2)}) collective-permute-start(bf16[512,512]{1,0:T(8,128)(2,1)S(1)} %slice.7.own), channel_id=1, source_target_pairs={{0,24},{1,25},{2,26},{3,27},{4,28},{5,29},{6,30},{7,31},{8,0},{9,1... | collective-permute-start | bytes 1572872 | tf_op jit(solution)/shard_map/ppermute | solution.py:33
  63.7 10.4 %collective-permute-start.11 = (bf16[512,256]{1,0:T(8,128)(2,1)S(1)}, bf16[512,256]{1,0:T(8,128)(2,1)S(1)}, u32[]{:S(2)}, u32[]{:S(2)}) collective-permute-start(bf16[512,256]{1,0:T(8,128)(2,1)S(1)} %collective-permute-done.5.up), channel_id=1, source_target_pairs={{0,8},{1,9},{2,10},{3,11},{4,12},{5,13},{6,14},{7,15},{8,16},{9,17... | collective-permute-start | bytes 786440 | tf_op jit(solution)/shard_map/ppermute | solution.py:33
  71.5 1.0 copy-start.3
  76.4 2.4 %collective-permute-start.12 = (f32[512,256]{1,0:T(8,128)S(1)}, f32[512,256]{1,0:T(8,128)S(1)}, u32[]{:S(2)}, u32[]{:S(2)}) collective-permute-start(f32[512,256]{1,0:T(8,128)S(1)} %get-tuple-element.56), channel_id=1, source_target_pairs={{0,1},{1,0},{2,3},{3,2},{4,5},{5,4},{6,7},{7,6},{8,9},{9,8},{10,11... | collective-permute-start | bytes 1572872 | tf_op jit(solution)/shard_map/ppermute | solution.py:33
  76.5 14.3 %collective-permute-start.13 = (bf16[512,512]{1,0:T(8,128)(2,1)S(1)}, bf16[512,512]{1,0:T(8,128)(2,1)S(1)}, u32[]{:S(2)}, u32[]{:S(2)}) collective-permute-start(bf16[512,512]{1,0:T(8,128)(2,1)S(1)} %slice.7.own), channel_id=1, source_target_pairs={{0,8},{1,9},{2,10},{3,11},{4,12},{5,13},{6,14},{7,15},{8,16},{9,17... | collective-permute-start | bytes 1572872 | tf_op jit(solution)/shard_map/ppermute | solution.py:33
  78.7 25.4 %collective-permute-start.15 = (bf16[512,512]{1,0:T(8,128)(2,1)S(1)}, bf16[512,512]{1,0:T(8,128)(2,1)S(1)}, u32[]{:S(2)}, u32[]{:S(2)}) collective-permute-start(bf16[512,512]{1,0:T(8,128)(2,1)S(1)} %collective-permute-done.14.down), channel_id=1, source_target_pairs={{0,24},{1,25},{2,26},{3,27},{4,28},{5,29},{6,30},{7,31},{8,0},{9,1... | collective-permute-start | bytes 1572872 | tf_op jit(solution)/shard_map/ppermute | solution.py:33
  79.1 28.4 %collective-permute-start.17 = (bf16[1040,128]{1,0:T(8,128)(2,1)S(1)}, bf16[1040,128]{1,0:T(8,128)(2,1)S(1)}, u32[]{:S(2)}, u32[]{:S(2)}) collective-permute-start(bf16[1040,128]{1,0:T(8,128)(2,1)S(1)} %shard_map.70.refs_4_), channel_id=1, source_target_pairs={{0,32},{1,33},{2,34},{3,35},{4,36},{5,37},{6,38},{7,39},{8,40},{9,... | collective-permute-start | bytes 798728 | tf_op jit(solution)/shard_map/ppermute | solution.py:33
  80.7 26.9 %collective-permute-start.18 = (bf16[1040,128]{1,0:T(8,128)(2,1)S(1)}, bf16[1040,128]{1,0:T(8,128)(2,1)S(1)}, u32[]{:S(2)}, u32[]{:S(2)}) collective-permute-start(bf16[1040,128]{1,0:T(8,128)(2,1)S(1)} %shard_map.70.refs_4_), channel_id=1, source_target_pairs={{0,24},{1,25},{2,26},{3,27},{4,28},{5,29},{6,30},{7,31},{8,32},{9,... | collective-permute-start | bytes 798728 | tf_op jit(solution)/shard_map/ppermute | solution.py:33
  81.8 25.8 %collective-permute-start.19 = (bf16[1040,128]{1,0:T(8,128)(2,1)S(1)}, bf16[1040,128]{1,0:T(8,128)(2,1)S(1)}, u32[]{:S(2)}, u32[]{:S(2)}) collective-permute-start(bf16[1040,128]{1,0:T(8,128)(2,1)S(1)} %shard_map.70.refs_4_), channel_id=1, source_target_pairs={{0,16},{1,17},{2,18},{3,19},{4,20},{5,21},{6,22},{7,23},{8,24},{9,... | collective-permute-start | bytes 798728 | tf_op jit(solution)/shard_map/ppermute | solution.py:33
  90.8 16.7 %collective-permute-start.20 = (bf16[1040,128]{1,0:T(8,128)(2,1)S(1)}, bf16[1040,128]{1,0:T(8,128)(2,1)S(1)}, u32[]{:S(2)}, u32[]{:S(2)}) collective-permute-start(bf16[1040,128]{1,0:T(8,128)(2,1)S(1)} %shard_map.70.refs_4_), channel_id=1, source_target_pairs={{0,8},{1,9},{2,10},{3,11},{4,12},{5,13},{6,14},{7,15},{8,16},{9,17... | collective-permute-start | bytes 798728 | tf_op jit(solution)/shard_map/ppermute | solution.py:33
  107.2 3.0 %collective-permute-start.16 = (f32[512,512]{1,0:T(8,128)S(1)}, f32[512,512]{1,0:T(8,128)S(1)}, u32[]{:S(2)}, u32[]{:S(2)}) collective-permute-start(f32[512,512]{1,0:T(8,128)S(1)} %get-tuple-element.63), channel_id=1, source_target_pairs={{0,1},{1,0},{2,3},{3,2},{4,5},{5,4},{6,7},{7,6},{8,9},{9,8},{10,11... | collective-permute-start | bytes 3145736 | tf_op jit(solution)/shard_map/ppermute | solution.py:33
  119.3 9.9 %collective-permute-start.21 = (bf16[128,512]{1,0:T(8,128)(2,1)S(1)}, bf16[128,512]{1,0:T(8,128)(2,1)S(1)}, u32[]{:S(2)}, u32[]{:S(2)}) collective-permute-start(bf16[128,512]{1,0:T(8,128)(2,1)S(1)} %get-tuple-element.67), channel_id=1, source_target_pairs={{0,0},{1,2},{2,4},{3,6},{4,1},{5,3},{6,5},{7,7},{8,8},{9,10},{10,1... | collective-permute-start | bytes 393224 | tf_op jit(solution)/shard_map/ppermute | solution.py:33
  119.9 9.2 %collective-permute-start.22 = (bf16[128,512]{1,0:T(8,128)(2,1)S(1)}, bf16[128,512]{1,0:T(8,128)(2,1)S(1)}, u32[]{:S(2)}, u32[]{:S(2)}) collective-permute-start(bf16[128,512]{1,0:T(8,128)(2,1)S(1)} %get-tuple-element.68), channel_id=1, source_target_pairs={{0,2},{1,0},{2,6},{3,4},{4,3},{5,1},{6,7},{7,5},{8,10},{9,8},{10,1... | collective-permute-start | bytes 393224 | tf_op jit(solution)/shard_map/ppermute | solution.py:33
  121.2 8.6 %collective-permute-start.23 = (bf16[128,512]{1,0:T(8,128)(2,1)S(1)}, bf16[128,512]{1,0:T(8,128)(2,1)S(1)}, u32[]{:S(2)}, u32[]{:S(2)}) collective-permute-start(bf16[128,512]{1,0:T(8,128)(2,1)S(1)} %get-tuple-element.69), channel_id=1, source_target_pairs={{0,4},{1,6},{2,0},{3,2},{4,5},{5,7},{6,1},{7,3},{8,12},{9,14},{10,... | collective-permute-start | bytes 393224 | tf_op jit(solution)/shard_map/ppermute | solution.py:33
  127.2 6.3 %collective-permute-start.24 = (bf16[128,512]{1,0:T(8,128)(2,1)S(1)}, bf16[128,512]{1,0:T(8,128)(2,1)S(1)}, u32[]{:S(2)}, u32[]{:S(2)}) collective-permute-start(bf16[128,512]{1,0:T(8,128)(2,1)S(1)} %get-tuple-element.70), channel_id=1, source_target_pairs={{0,6},{1,4},{2,2},{3,0},{4,7},{5,5},{6,3},{7,1},{8,14},{9,12},{10,... | collective-permute-start | bytes 393224 | tf_op jit(solution)/shard_map/ppermute | solution.py:33
  (3 other events, 2.1 us)

commit v4 on v3

--- a/solution.py
+++ b/solution.py
@@ -315,7 +315,6 @@
     kv_up, kv_down, right_b, left_a, q0 = tie(kv_up, kv_down, right_b, left_a, q0)
     kv_far = along_y(kv_up, 1)
     q_up, q_down = along_y(q0, 1), along_y(q0, -1)
-    q_far = along_y(q_down, -1)
     x_all, docs = call(
         stack_kernel,
         (shape((1024, HALF), BF), shape((16, HD), BF)),
@@ -337,6 +336,8 @@
         cost(2 * 1024 * HALF * 256, 10 << 20),
     )
     got = permute(send, lambda z, y, x, c: (z, y, x, 1 - c))
+    got, q_up, q_down = tie(got, q_up, q_down)
+    q_far = along_y(q_down, -1)
     own = call(
         rotate_kv_kernel,
         shape((ROWS, HD), BF),

time: 136 us -> 136 us (level)
  the two profiles are of different devices: /device:TPU:48 before, /device:TPU:128 now
where the time goes in v4:
time: 136 us; the launch traced here: 135 us
  waiting for transfers between devices  49.8 us (37%)
  starting transfers between devices  48.7 us (36%)
  Pallas kernels  23.9 us (18%)
  local copies, waits for them, and re-layouts  10.9 us (8%)
    ppermute x25, waiting for transfers between devices, permute(): return lax.ppermute(value, AXES, pairs)  49.5 us
    ppermute x25, starting transfers between devices, permute(): return lax.ppermute(value, AXES, pairs)  37.4 us
    pallas_call x12, Pallas kernels, call(): pl.pallas_call(kernel, out_shape=shapes, in_specs=[SMEM] * smem + [VMEM]...  23.9 us
    all_to_all x1, starting transfers between devices, copies(): lax.all_to_all(jnp.broadcast_to(value[None], (count, *value.shape)), axis...  11.2 us
    unnamed x18, local copies, waits for them, and re-layouts  8.13 us
  transfers between devices with their start and end apart: 26, of which 14 were waited for; matrix products, arithmetic and copies ran while one was open for 2% of the time, Pallas kernels for 7%

profile of v4, /device:TPU:128, one launch (start us, length us, event | category | flops | bytes accessed | tf_op | source)
XLA Modules:
  0.0 134.6 jit_solution(8755103926961502586)
XLA Ops:
  0.0 1.2 copy-done
  4.5 2.5 %collective-permute-start = (bf16[32,768]{1,0:T(8,128)(2,1)S(1)}, bf16[32,768]{1,0:T(8,128)(2,1)S(1)}, u32[]{:S(2)}, u32[]{:S(2)}) collective-permute-start(bf16[32,768]{1,0:T(8,128)(2,1)S(1)} %get-tuple-element.41), channel_id=1, source_target_pairs={{0,0},{1,4},{2,2},{3,6},{4,8},{5,12},{6,10},{7,14},{8,16},{9,20},{... | collective-permute-start | bytes 147464 | tf_op jit(solution)/shard_map/ppermute | solution.py:33
  8.7 1.2 copy-done.1
  12.6 2.0 %collective-permute-done.1.second = bf16[32,768]{1,0:T(8,128)(2,1)S(1)} collective-permute-done((bf16[32,768]{1,0:T(8,128)(2,1)S(1)}, bf16[32,768]{1,0:T(8,128)(2,1)S(1)}, u32[]{:S(2)}, u32[]{:S(2)}) %collective-permute-start.1) | collective-permute-done | bytes 49184 | tf_op jit(solution)/shard_map/ppermute | solution.py:33
  16.2 11.2 %all-to-all-start = ((bf16[8,64,768]{2,1,0:T(8,128)(2,1)}), bf16[8,64,768]{2,1,0:T(8,128)(2,1)S(1)}, u32[]{:S(2)}, u32[]{:S(2)}) async-start(bf16[8,64,768]{2,1,0:T(8,128)(2,1)} %broadcast_in_dim.2), calls=%async_computation | async-start | bytes 1572864 | tf_op jit(solution)/shard_map/all_to_all | solution.py:275
  27.4 1.4 %collective-permute-start.3 = (bf16[144,2048]{1,0:T(8,128)(2,1)S(1)}, bf16[144,2048]{1,0:T(8,128)(2,1)S(1)}, u32[]{:S(2)}, u32[]{:S(2)}) collective-permute-start(bf16[144,2048]{1,0:T(8,128)(2,1)S(1)} %get-tuple-element.45.refs_0_), channel_id=1, source_target_pairs={{0,2},{1,3},{2,4},{3,5},{4,6},{5,7},{6,0},{7,1},{8,10},{9,11},{10,... | collective-permute-start | bytes 1769480 | tf_op jit(solution)/shard_map/ppermute | solution.py:33
  28.8 2.7 %collective-permute-start.4 = (bf16[128,2048]{1,0:T(8,128)(2,1)S(1)}, bf16[128,2048]{1,0:T(8,128)(2,1)S(1)}, u32[]{:S(2)}, u32[]{:S(2)}) collective-permute-start(bf16[128,2048]{1,0:T(8,128)(2,1)S(1)} %get-tuple-element.48.refs_4_), channel_id=1, source_target_pairs={{0,6},{1,7},{2,0},{3,1},{4,2},{5,3},{6,4},{7,5},{8,14},{9,15},{10,... | collective-permute-start | bytes 1572872 | tf_op jit(solution)/shard_map/ppermute | solution.py:33
  31.6 3.2 %collective-permute-start.8 = (bf16[144,2048]{1,0:T(8,128)(2,1)S(1)}, bf16[144,2048]{1,0:T(8,128)(2,1)S(1)}, u32[]{:S(2)}, u32[]{:S(2)}) collective-permute-start(bf16[144,2048]{1,0:T(8,128)(2,1)S(1)} %get-tuple-element.45.refs_0_), channel_id=1, source_target_pairs={{0,6},{1,7},{2,0},{3,1},{4,2},{5,3},{6,4},{7,5},{8,14},{9,15},{10,... | collective-permute-start | bytes 1769480 | tf_op jit(solution)/shard_map/ppermute | solution.py:33
  34.8 9.1 %collective-permute-done.4.refs_6_ = bf16[128,2048]{1,0:T(8,128)(2,1)S(1)} collective-permute-done((bf16[128,2048]{1,0:T(8,128)(2,1)S(1)}, bf16[128,2048]{1,0:T(8,128)(2,1)S(1)}, u32[]{:S(2)}, u32[]{:S(2)}) %collective-permute-start.4) | collective-permute-done | bytes 524320 | tf_op jit(solution)/shard_map/ppermute | solution.py:33
  47.0 2.4 %collective-permute-start.5 = (bf16[512,256]{1,0:T(8,128)(2,1)S(1)}, bf16[512,256]{1,0:T(8,128)(2,1)S(1)}, u32[]{:S(2)}, u32[]{:S(2)}) collective-permute-start(bf16[512,256]{1,0:T(8,128)(2,1)S(1)} %slice.6.own), channel_id=1, source_target_pairs={{0,8},{1,9},{2,10},{3,11},{4,12},{5,13},{6,14},{7,15},{8,16},{9,17... | collective-permute-start | bytes 786440 | tf_op jit(solution)/shard_map/ppermute | solution.py:33
  49.4 2.6 %collective-permute-start.6 = (bf16[512,256]{1,0:T(8,128)(2,1)S(1)}, bf16[512,256]{1,0:T(8,128)(2,1)}, u32[]{:S(2)}, u32[]{:S(2)}) collective-permute-start(bf16[512,256]{1,0:T(8,128)(2,1)S(1)} %slice.6.own), channel_id=1, source_target_pairs={{0,24},{1,25},{2,26},{3,27},{4,28},{5,29},{6,30},{7,31},{8,0},{9,1... | collective-permute-start | bytes 786440 | tf_op jit(solution)/shard_map/ppermute | solution.py:33
  52.1 3.4 %collective-permute-done.7.refs_5_ = bf16[128,2048]{1,0:T(8,128)(2,1)} collective-permute-done((bf16[128,2048]{1,0:T(8,128)(2,1)S(1)}, bf16[128,2048]{1,0:T(8,128)(2,1)}, u32[]{:S(2)}, u32[]{:S(2)}) %collective-permute-start.7) | collective-permute-done | bytes 524320 | tf_op jit(solution)/shard_map/ppermute | solution.py:33
  55.4 3.6 %collective-permute-start.10 = (bf16[128,2048]{1,0:T(8,128)(2,1)}, bf16[128,2048]{1,0:T(8,128)(2,1)}, u32[]{:S(2)}, u32[]{:S(2)}) collective-permute-start(bf16[128,2048]{1,0:T(8,128)(2,1)} %copy-done.2), channel_id=1, source_target_pairs={{0,6},{1,7},{2,0},{3,1},{4,2},{5,3},{6,4},{7,5},{8,14},{9,15},{10,... | collective-permute-start | bytes 1572872 | tf_op jit(solution)/shard_map/ppermute | solution.py:33
  61.2 1.3 collective-permute-start.13
  62.5 2.3 %collective-permute-start.14 = (bf16[512,512]{1,0:T(8,128)(2,1)S(1)}, bf16[512,512]{1,0:T(8,128)(2,1)S(1)}, u32[]{:S(2)}, u32[]{:S(2)}) collective-permute-start(bf16[512,512]{1,0:T(8,128)(2,1)S(1)} %slice.7.own), channel_id=1, source_target_pairs={{0,24},{1,25},{2,26},{3,27},{4,28},{5,29},{6,30},{7,31},{8,0},{9,1... | collective-permute-start | bytes 1572872 | tf_op jit(solution)/shard_map/ppermute | solution.py:33
  64.8 3.2 %collective-permute-done.10.refs_7_ = bf16[128,2048]{1,0:T(8,128)(2,1)} collective-permute-done((bf16[128,2048]{1,0:T(8,128)(2,1)}, bf16[128,2048]{1,0:T(8,128)(2,1)}, u32[]{:S(2)}, u32[]{:S(2)}) %collective-permute-start.10) | collective-permute-done | bytes 524320 | tf_op jit(solution)/shard_map/ppermute | solution.py:33
  69.3 1.5 %shard_map.68 = (bf16[1024,2048]{1,0:T(8,128)(2,1)S(1)}, bf16[16,128]{1,0:T(8,128)(2,1)S(1)}) custom-call(s32[4]{0:T(128)S(1)} %pad_add_fusion.idx, bf16[144,2048]{1,0:T(8,128)(2,1)S(1)} %get-tuple-element.45.refs_0_, bf16[144,2048]{1,0:T(8,128)(2,1)S(1)} %collective-permute-done.3.refs_1_, bf16[144,2048]{1,0:T(8,128)(2,1)S(1)} %collective-permute-done.8.refs_2_, ...), custom_call_target="tpu_custom_call" | custom-call | bytes 8388608 | tf_op jit(solution)/shard_map/pallas_call | solution.py:255
  70.8 2.3 %shard_map.69 = (f32[512,256]{1,0:T(8,128)S(1)}, f32[512,256]{1,0:T(8,128)S(1)}) custom-call(s32[4]{0:T(128)S(1)} %pad_add_fusion.idx, bf16[1024,2048]{1,0:T(8,128)(2,1)S(1)} %get-tuple-element.65.x_all, bf16[512,256]{1,0:T(8,128)(2,1)S(1)} %slice.6.own, bf16[512,256]{1,0:T(8,128)(2,1)S(1)} %collective-permute-done.5.up, ...), custom_call_target="tpu_custom_call" | custom-call | flops 1073741824 | bytes 10485760 | tf_op jit(solution)/shard_map/pallas_call | solution.py:255
  73.2 5.7 %collective-permute-done.13.up = bf16[512,512]{1,0:T(8,128)(2,1)S(1)} collective-permute-done((bf16[512,512]{1,0:T(8,128)(2,1)S(1)}, bf16[512,512]{1,0:T(8,128)(2,1)S(1)}, u32[]{:S(2)}, u32[]{:S(2)}) %collective-permute-start.13) | collective-permute-done | bytes 524320 | tf_op jit(solution)/shard_map/ppermute | solution.py:33
  78.9 2.1 %collective-permute-start.15 = (bf16[512,512]{1,0:T(8,128)(2,1)S(1)}, bf16[512,512]{1,0:T(8,128)(2,1)S(1)}, u32[]{:S(2)}, u32[]{:S(2)}) collective-permute-start(bf16[512,512]{1,0:T(8,128)(2,1)S(1)} %collective-permute-done.14.down), channel_id=1, source_target_pairs={{0,24},{1,25},{2,26},{3,27},{4,28},{5,29},{6,30},{7,31},{8,0},{9,1... | collective-permute-start | bytes 1572872 | tf_op jit(solution)/shard_map/ppermute | solution.py:33
  81.9 3.2 %collective-permute-start.19 = (bf16[1040,128]{1,0:T(8,128)(2,1)S(1)}, bf16[1040,128]{1,0:T(8,128)(2,1)S(1)}, u32[]{:S(2)}, u32[]{:S(2)}) collective-permute-start(bf16[1040,128]{1,0:T(8,128)(2,1)S(1)} %shard_map.70.refs_4_), channel_id=1, source_target_pairs={{0,16},{1,17},{2,18},{3,19},{4,20},{5,21},{6,22},{7,23},{8,24},{9,... | collective-permute-start | bytes 798728 | tf_op jit(solution)/shard_map/ppermute | solution.py:33
  85.2 14.1 %collective-permute-done.15.far = bf16[512,512]{1,0:T(8,128)(2,1)S(1)} collective-permute-done((bf16[512,512]{1,0:T(8,128)(2,1)S(1)}, bf16[512,512]{1,0:T(8,128)(2,1)S(1)}, u32[]{:S(2)}, u32[]{:S(2)}) %collective-permute-start.15) | collective-permute-done | bytes 524320 | tf_op jit(solution)/shard_map/ppermute | solution.py:33
  99.3 3.1 %shard_map.71 = (f32[512,512]{1,0:T(8,128)S(1)}, f32[512,512]{1,0:T(8,128)S(1)}) custom-call(s32[4]{0:T(128)S(1)} %pad_add_fusion.idx, bf16[1024,2048]{1,0:T(8,128)(2,1)S(1)} %get-tuple-element.65.x_all, bf16[512,512]{1,0:T(8,128)(2,1)S(1)} %slice.7.own, bf16[512,512]{1,0:T(8,128)(2,1)S(1)} %collective-permute-done.13.up, ...), custom_call_target="tpu_custom_call" | custom-call | flops 2147483648 | bytes 10485760 | tf_op jit(solution)/shard_map/pallas_call | solution.py:255
  102.5 1.3 collective-permute-done.18.refs_1_
  103.8 3.8 %collective-permute-done.20.refs_3_ = bf16[1040,128]{1,0:T(8,128)(2,1)S(1)} collective-permute-done((bf16[1040,128]{1,0:T(8,128)(2,1)S(1)}, bf16[1040,128]{1,0:T(8,128)(2,1)S(1)}, u32[]{:S(2)}, u32[]{:S(2)}) %collective-permute-start.20) | collective-permute-done | bytes 266272 | tf_op jit(solution)/shard_map/ppermute | solution.py:33
  107.6 1.4 %shard_map.73 = (bf16[20,2,128,128]{3,2,1,0:T(8,128)(2,1)S(1)}, s32[4,1,512]{2,1,0:T(1,128)S(1)}) custom-call(s32[4]{0:T(128)S(1)} %pad_add_fusion.idx, bf16[1040,128]{1,0:T(8,128)(2,1)S(1)} %collective-permute-done.17.refs_0_, bf16[1040,128]{1,0:T(8,128)(2,1)S(1)} %collective-permute-done.18.refs_1_, bf16[1040,128]{1,0:T(8,128)(2,1)S(1)} %collective-permute-done.19.refs_2_, ...), custom_call_target="tpu_custom_call" | custom-call | flops 68719476736 | bytes 4194304 | tf_op jit(solution)/shard_map/pallas_call | solution.py:255
  110.0 10.7 %shard_map.74 = (bf16[128,512]{1,0:T(8,128)(2,1)S(1)}, bf16[128,512]{1,0:T(8,128)(2,1)S(1)}, bf16[128,512]{1,0:T(8,128)(2,1)S(1)}, bf16[128,512]{1,0:T(8,128)(2,1)S(1)}) custom-call(s32[4]{0:T(128)S(1)} %pad_add_fusion.idx, bf16[4,512,128]{2,1,0:T(8,128)(2,1)S(1)} %shard_map.72.query, bf16[20,2,128,128]{3,2,1,0:T(8,128)(2,1)S(1)} %get-tuple-element.71.kv, ...), custom_call_target="tpu_custom_call" | custom-call | flops 2147483648 | bytes 4194304 | tf_op jit(solution)/shard_map/pallas_call | solution.py:255
  122.3 4.6 %collective-permute-start.23 = (bf16[128,512]{1,0:T(8,128)(2,1)S(1)}, bf16[128,512]{1,0:T(8,128)(2,1)S(1)}, u32[]{:S(2)}, u32[]{:S(2)}) collective-permute-start(bf16[128,512]{1,0:T(8,128)(2,1)S(1)} %get-tuple-element.75), channel_id=1, source_target_pairs={{0,4},{1,6},{2,0},{3,2},{4,5},{5,7},{6,1},{7,3},{8,12},{9,14},{10,... | collective-permute-start | bytes 393224 | tf_op jit(solution)/shard_map/ppermute | solution.py:33
  126.9 1.9 %collective-permute-start.24 = (bf16[128,512]{1,0:T(8,128)(2,1)S(1)}, bf16[128,512]{1,0:T(8,128)(2,1)S(1)}, u32[]{:S(2)}, u32[]{:S(2)}) collective-permute-start(bf16[128,512]{1,0:T(8,128)(2,1)S(1)} %get-tuple-element.76), channel_id=1, source_target_pairs={{0,6},{1,4},{2,2},{3,0},{4,7},{5,5},{6,3},{7,1},{8,14},{9,12},{10,... | collective-permute-start | bytes 393224 | tf_op jit(solution)/shard_map/ppermute | solution.py:33
  128.9 1.4 %collective-permute-done.23.refs_2_ = bf16[128,512]{1,0:T(8,128)(2,1)S(1)} collective-permute-done((bf16[128,512]{1,0:T(8,128)(2,1)S(1)}, bf16[128,512]{1,0:T(8,128)(2,1)S(1)}, u32[]{:S(2)}, u32[]{:S(2)}) %collective-permute-start.23) | collective-permute-done | bytes 131104 | tf_op jit(solution)/shard_map/ppermute | solution.py:33
  130.3 2.9 %collective-permute-done.24.refs_3_ = bf16[128,512]{1,0:T(8,128)(2,1)S(1)} collective-permute-done((bf16[128,512]{1,0:T(8,128)(2,1)S(1)}, bf16[128,512]{1,0:T(8,128)(2,1)S(1)}, u32[]{:S(2)}, u32[]{:S(2)}) %collective-permute-start.24) | collective-permute-done | bytes 131104 | tf_op jit(solution)/shard_map/ppermute | solution.py:33
  133.2 1.4 %shard_map.75 = bf16[2,128,1024]{2,1,0:T(8,128)(2,1)} custom-call(s32[4]{0:T(128)S(1)} %pad_add_fusion.idx, bf16[128,512]{1,0:T(8,128)(2,1)S(1)} %collective-permute-done.21.refs_0_, bf16[128,512]{1,0:T(8,128)(2,1)S(1)} %collective-permute-done.22.refs_1_, bf16[128,512]{1,0:T(8,128)(2,1)S(1)} %collective-permute-done.23.refs_2_, ...), custom_call_target="tpu_custom_call" | custom-call | bytes 1048576 | tf_op jit(solution)/shard_map/pallas_call | solution.py:255
  (58 shorter events, 19.5 us)
Async XLA Ops:
  0.0 1.2 copy-start
  1.5 7.2 %collective-permute-start.2 = (f32[256,128]{1,0:T(8,128)S(1)}, f32[256,128]{1,0:T(8,128)S(1)}, u32[]{:S(2)}, u32[]{:S(2)}) collective-permute-start(f32[256,128]{1,0:T(8,128)S(1)} %shard_map.65.squares), channel_id=1, source_target_pairs={{0,1},{1,0},{2,3},{3,2},{4,5},{5,4},{6,7},{7,6},{8,9},{9,8},{10,11... | collective-permute-start | bytes 393224 | tf_op jit(solution)/shard_map/ppermute | solution.py:33
  1.7 0.8 copy-start.4
  4.5 8.1 %collective-permute-start = (bf16[32,768]{1,0:T(8,128)(2,1)S(1)}, bf16[32,768]{1,0:T(8,128)(2,1)S(1)}, u32[]{:S(2)}, u32[]{:S(2)}) collective-permute-start(bf16[32,768]{1,0:T(8,128)(2,1)S(1)} %get-tuple-element.41), channel_id=1, source_target_pairs={{0,0},{1,4},{2,2},{3,6},{4,8},{5,12},{6,10},{7,14},{8,16},{9,20},{... | collective-permute-start | bytes 147464 | tf_op jit(solution)/shard_map/ppermute | solution.py:33
  7.0 7.6 %collective-permute-start.1 = (bf16[32,768]{1,0:T(8,128)(2,1)S(1)}, bf16[32,768]{1,0:T(8,128)(2,1)S(1)}, u32[]{:S(2)}, u32[]{:S(2)}) collective-permute-start(bf16[32,768]{1,0:T(8,128)(2,1)S(1)} %get-tuple-element.42), channel_id=1, source_target_pairs={{0,2},{1,6},{2,0},{3,4},{4,10},{5,14},{6,8},{7,12},{8,18},{9,22},{... | collective-permute-start | bytes 147464 | tf_op jit(solution)/shard_map/ppermute | solution.py:33
  8.7 1.2 copy-start.1
  16.2 30.0 %all-to-all-start = ((bf16[8,64,768]{2,1,0:T(8,128)(2,1)}), bf16[8,64,768]{2,1,0:T(8,128)(2,1)S(1)}, u32[]{:S(2)}, u32[]{:S(2)}) async-start(bf16[8,64,768]{2,1,0:T(8,128)(2,1)} %broadcast_in_dim.2), calls=%async_computation | async-start | bytes 1572864 | tf_op jit(solution)/shard_map/all_to_all | solution.py:275
  27.4 18.4 %collective-permute-start.3 = (bf16[144,2048]{1,0:T(8,128)(2,1)S(1)}, bf16[144,2048]{1,0:T(8,128)(2,1)S(1)}, u32[]{:S(2)}, u32[]{:S(2)}) collective-permute-start(bf16[144,2048]{1,0:T(8,128)(2,1)S(1)} %get-tuple-element.45.refs_0_), channel_id=1, source_target_pairs={{0,2},{1,3},{2,4},{3,5},{4,6},{5,7},{6,0},{7,1},{8,10},{9,11},{10,... | collective-permute-start | bytes 1769480 | tf_op jit(solution)/shard_map/ppermute | solution.py:33
  28.8 15.1 %collective-permute-start.4 = (bf16[128,2048]{1,0:T(8,128)(2,1)S(1)}, bf16[128,2048]{1,0:T(8,128)(2,1)S(1)}, u32[]{:S(2)}, u32[]{:S(2)}) collective-permute-start(bf16[128,2048]{1,0:T(8,128)(2,1)S(1)} %get-tuple-element.48.refs_4_), channel_id=1, source_target_pairs={{0,6},{1,7},{2,0},{3,1},{4,2},{5,3},{6,4},{7,5},{8,14},{9,15},{10,... | collective-permute-start | bytes 1572872 | tf_op jit(solution)/shard_map/ppermute | solution.py:33
  31.6 23.9 %collective-permute-start.7 = (bf16[128,2048]{1,0:T(8,128)(2,1)S(1)}, bf16[128,2048]{1,0:T(8,128)(2,1)}, u32[]{:S(2)}, u32[]{:S(2)}) collective-permute-start(bf16[128,2048]{1,0:T(8,128)(2,1)S(1)} %get-tuple-element.48.refs_4_), channel_id=1, source_target_pairs={{0,2},{1,3},{2,4},{3,5},{4,6},{5,7},{6,0},{7,1},{8,10},{9,11},{10,... | collective-permute-start | bytes 1572872 | tf_op jit(solution)/shard_map/ppermute | solution.py:33
  31.6 28.5 %collective-permute-start.8 = (bf16[144,2048]{1,0:T(8,128)(2,1)S(1)}, bf16[144,2048]{1,0:T(8,128)(2,1)S(1)}, u32[]{:S(2)}, u32[]{:S(2)}) collective-permute-start(bf16[144,2048]{1,0:T(8,128)(2,1)S(1)} %get-tuple-element.45.refs_0_), channel_id=1, source_target_pairs={{0,6},{1,7},{2,0},{3,1},{4,2},{5,3},{6,4},{7,5},{8,14},{9,15},{10,... | collective-permute-start | bytes 1769480 | tf_op jit(solution)/shard_map/ppermute | solution.py:33
  43.9 0.8 copy-start.2
  46.1 0.9 copy-start.8
  47.0 13.1 %collective-permute-start.5 = (bf16[512,256]{1,0:T(8,128)(2,1)S(1)}, bf16[512,256]{1,0:T(8,128)(2,1)S(1)}, u32[]{:S(2)}, u32[]{:S(2)}) collective-permute-start(bf16[512,256]{1,0:T(8,128)(2,1)S(1)} %slice.6.own), channel_id=1, source_target_pairs={{0,8},{1,9},{2,10},{3,11},{4,12},{5,13},{6,14},{7,15},{8,16},{9,17... | collective-permute-start | bytes 786440 | tf_op jit(solution)/shard_map/ppermute | solution.py:33
  49.4 10.7 %collective-permute-start.6 = (bf16[512,256]{1,0:T(8,128)(2,1)S(1)}, bf16[512,256]{1,0:T(8,128)(2,1)}, u32[]{:S(2)}, u32[]{:S(2)}) collective-permute-start(bf16[512,256]{1,0:T(8,128)(2,1)S(1)} %slice.6.own), channel_id=1, source_target_pairs={{0,24},{1,25},{2,26},{3,27},{4,28},{5,29},{6,30},{7,31},{8,0},{9,1... | collective-permute-start | bytes 786440 | tf_op jit(solution)/shard_map/ppermute | solution.py:33
  52.1 16.2 %collective-permute-start.9 = (bf16[144,2048]{1,0:T(8,128)(2,1)S(1)}, bf16[144,2048]{1,0:T(8,128)(2,1)S(1)}, u32[]{:S(2)}, u32[]{:S(2)}) collective-permute-start(bf16[144,2048]{1,0:T(8,128)(2,1)S(1)} %collective-permute-done.3.refs_1_), channel_id=1, source_target_pairs={{0,2},{1,3},{2,4},{3,5},{4,6},{5,7},{6,0},{7,1},{8,10},{9,11},{10,... | collective-permute-start | bytes 1769480 | tf_op jit(solution)/shard_map/ppermute | solution.py:33
  55.4 12.6 %collective-permute-start.10 = (bf16[128,2048]{1,0:T(8,128)(2,1)}, bf16[128,2048]{1,0:T(8,128)(2,1)}, u32[]{:S(2)}, u32[]{:S(2)}) collective-permute-start(bf16[128,2048]{1,0:T(8,128)(2,1)} %copy-done.2), channel_id=1, source_target_pairs={{0,6},{1,7},{2,0},{3,1},{4,2},{5,3},{6,4},{7,5},{8,14},{9,15},{10,... | collective-permute-start | bytes 1572872 | tf_op jit(solution)/shard_map/ppermute | solution.py:33
  60.1 10.7 %collective-permute-start.11 = (bf16[512,256]{1,0:T(8,128)(2,1)S(1)}, bf16[512,256]{1,0:T(8,128)(2,1)S(1)}, u32[]{:S(2)}, u32[]{:S(2)}) collective-permute-start(bf16[512,256]{1,0:T(8,128)(2,1)S(1)} %collective-permute-done.5.up), channel_id=1, source_target_pairs={{0,8},{1,9},{2,10},{3,11},{4,12},{5,13},{6,14},{7,15},{8,16},{9,17... | collective-permute-start | bytes 786440 | tf_op jit(solution)/shard_map/ppermute | solution.py:33
  61.2 17.6 %collective-permute-start.13 = (bf16[512,512]{1,0:T(8,128)(2,1)S(1)}, bf16[512,512]{1,0:T(8,128)(2,1)S(1)}, u32[]{:S(2)}, u32[]{:S(2)}) collective-permute-start(bf16[512,512]{1,0:T(8,128)(2,1)S(1)} %slice.7.own), channel_id=1, source_target_pairs={{0,8},{1,9},{2,10},{3,11},{4,12},{5,13},{6,14},{7,15},{8,16},{9,17... | collective-permute-start | bytes 1572872 | tf_op jit(solution)/shard_map/ppermute | solution.py:33
  62.5 16.3 %collective-permute-start.14 = (bf16[512,512]{1,0:T(8,128)(2,1)S(1)}, bf16[512,512]{1,0:T(8,128)(2,1)S(1)}, u32[]{:S(2)}, u32[]{:S(2)}) collective-permute-start(bf16[512,512]{1,0:T(8,128)(2,1)S(1)} %slice.7.own), channel_id=1, source_target_pairs={{0,24},{1,25},{2,26},{3,27},{4,28},{5,29},{6,30},{7,31},{8,0},{9,1... | collective-permute-start | bytes 1572872 | tf_op jit(solution)/shard_map/ppermute | solution.py:33
  68.2 1.0 copy-start.3
  73.1 5.8 %collective-permute-start.12 = (f32[512,256]{1,0:T(8,128)S(1)}, f32[512,256]{1,0:T(8,128)S(1)}, u32[]{:S(2)}, u32[]{:S(2)}) collective-permute-start(f32[512,256]{1,0:T(8,128)S(1)} %get-tuple-element.59), channel_id=1, source_target_pairs={{0,1},{1,0},{2,3},{3,2},{4,5},{5,4},{6,7},{7,6},{8,9},{9,8},{10,11... | collective-permute-start | bytes 1572872 | tf_op jit(solution)/shard_map/ppermute | solution.py:33
  78.9 20.4 %collective-permute-start.15 = (bf16[512,512]{1,0:T(8,128)(2,1)S(1)}, bf16[512,512]{1,0:T(8,128)(2,1)S(1)}, u32[]{:S(2)}, u32[]{:S(2)}) collective-permute-start(bf16[512,512]{1,0:T(8,128)(2,1)S(1)} %collective-permute-done.14.down), channel_id=1, source_target_pairs={{0,24},{1,25},{2,26},{3,27},{4,28},{5,29},{6,30},{7,31},{8,0},{9,1... | collective-permute-start | bytes 1572872 | tf_op jit(solution)/shard_map/ppermute | solution.py:33
  81.3 21.2 %collective-permute-start.17 = (bf16[1040,128]{1,0:T(8,128)(2,1)S(1)}, bf16[1040,128]{1,0:T(8,128)(2,1)S(1)}, u32[]{:S(2)}, u32[]{:S(2)}) collective-permute-start(bf16[1040,128]{1,0:T(8,128)(2,1)S(1)} %shard_map.70.refs_4_), channel_id=1, source_target_pairs={{0,32},{1,33},{2,34},{3,35},{4,36},{5,37},{6,38},{7,39},{8,40},{9,... | collective-permute-start | bytes 798728 | tf_op jit(solution)/shard_map/ppermute | solution.py:33
  81.9 21.9 %collective-permute-start.18 = (bf16[1040,128]{1,0:T(8,128)(2,1)S(1)}, bf16[1040,128]{1,0:T(8,128)(2,1)S(1)}, u32[]{:S(2)}, u32[]{:S(2)}) collective-permute-start(bf16[1040,128]{1,0:T(8,128)(2,1)S(1)} %shard_map.70.refs_4_), channel_id=1, source_target_pairs={{0,24},{1,25},{2,26},{3,27},{4,28},{5,29},{6,30},{7,31},{8,32},{9,... | collective-permute-start | bytes 798728 | tf_op jit(solution)/shard_map/ppermute | solution.py:33
  81.9 21.9 %collective-permute-start.19 = (bf16[1040,128]{1,0:T(8,128)(2,1)S(1)}, bf16[1040,128]{1,0:T(8,128)(2,1)S(1)}, u32[]{:S(2)}, u32[]{:S(2)}) collective-permute-start(bf16[1040,128]{1,0:T(8,128)(2,1)S(1)} %shard_map.70.refs_4_), channel_id=1, source_target_pairs={{0,16},{1,17},{2,18},{3,19},{4,20},{5,21},{6,22},{7,23},{8,24},{9,... | collective-permute-start | bytes 798728 | tf_op jit(solution)/shard_map/ppermute | solution.py:33
  85.1 22.5 %collective-permute-start.20 = (bf16[1040,128]{1,0:T(8,128)(2,1)S(1)}, bf16[1040,128]{1,0:T(8,128)(2,1)S(1)}, u32[]{:S(2)}, u32[]{:S(2)}) collective-permute-start(bf16[1040,128]{1,0:T(8,128)(2,1)S(1)} %shard_map.70.refs_4_), channel_id=1, source_target_pairs={{0,8},{1,9},{2,10},{3,11},{4,12},{5,13},{6,14},{7,15},{8,16},{9,17... | collective-permute-start | bytes 798728 | tf_op jit(solution)/shard_map/ppermute | solution.py:33
  102.4 6.7 %collective-permute-start.16 = (f32[512,512]{1,0:T(8,128)S(1)}, f32[512,512]{1,0:T(8,128)S(1)}, u32[]{:S(2)}, u32[]{:S(2)}) collective-permute-start(f32[512,512]{1,0:T(8,128)S(1)} %get-tuple-element.69), channel_id=1, source_target_pairs={{0,1},{1,0},{2,3},{3,2},{4,5},{5,4},{6,7},{7,6},{8,9},{9,8},{10,11... | collective-permute-start | bytes 3145736 | tf_op jit(solution)/shard_map/ppermute | solution.py:33
  120.7 8.1 %collective-permute-start.21 = (bf16[128,512]{1,0:T(8,128)(2,1)S(1)}, bf16[128,512]{1,0:T(8,128)(2,1)S(1)}, u32[]{:S(2)}, u32[]{:S(2)}) collective-permute-start(bf16[128,512]{1,0:T(8,128)(2,1)S(1)} %get-tuple-element.73), channel_id=1, source_target_pairs={{0,0},{1,2},{2,4},{3,6},{4,1},{5,3},{6,5},{7,7},{8,8},{9,10},{10,1... | collective-permute-start | bytes 393224 | tf_op jit(solution)/shard_map/ppermute | solution.py:33
  121.4 7.5 %collective-permute-start.22 = (bf16[128,512]{1,0:T(8,128)(2,1)S(1)}, bf16[128,512]{1,0:T(8,128)(2,1)S(1)}, u32[]{:S(2)}, u32[]{:S(2)}) collective-permute-start(bf16[128,512]{1,0:T(8,128)(2,1)S(1)} %get-tuple-element.74), channel_id=1, source_target_pairs={{0,2},{1,0},{2,6},{3,4},{4,3},{5,1},{6,7},{7,5},{8,10},{9,8},{10,1... | collective-permute-start | bytes 393224 | tf_op jit(solution)/shard_map/ppermute | solution.py:33
  122.3 7.9 %collective-permute-start.23 = (bf16[128,512]{1,0:T(8,128)(2,1)S(1)}, bf16[128,512]{1,0:T(8,128)(2,1)S(1)}, u32[]{:S(2)}, u32[]{:S(2)}) collective-permute-start(bf16[128,512]{1,0:T(8,128)(2,1)S(1)} %get-tuple-element.75), channel_id=1, source_target_pairs={{0,4},{1,6},{2,0},{3,2},{4,5},{5,7},{6,1},{7,3},{8,12},{9,14},{10,... | collective-permute-start | bytes 393224 | tf_op jit(solution)/shard_map/ppermute | solution.py:33
  126.9 6.3 %collective-permute-start.24 = (bf16[128,512]{1,0:T(8,128)(2,1)S(1)}, bf16[128,512]{1,0:T(8,128)(2,1)S(1)}, u32[]{:S(2)}, u32[]{:S(2)}) collective-permute-start(bf16[128,512]{1,0:T(8,128)(2,1)S(1)} %get-tuple-element.76), channel_id=1, source_target_pairs={{0,6},{1,4},{2,2},{3,0},{4,7},{5,5},{6,3},{7,1},{8,14},{9,12},{10,... | collective-permute-start | bytes 393224 | tf_op jit(solution)/shard_map/ppermute | solution.py:33
  (3 other events, 2.1 us)

commit v5 on v4

--- a/solution.py
+++ b/solution.py
@@ -337,7 +337,7 @@
     )
     got = permute(send, lambda z, y, x, c: (z, y, x, 1 - c))
     got, q_up, q_down = tie(got, q_up, q_down)
-    q_far = along_y(q_down, -1)
+    q_far = along_y(q_up, 1)
     own = call(
         rotate_kv_kernel,
         shape((ROWS, HD), BF),

time: 136 us -> 136 us (level)
  the two profiles are of different devices: /device:TPU:128 before, /device:TPU:32 now
where the time goes in v5:
time: 136 us; the launch traced here: 133 us
  starting transfers between devices  50.4 us (37%)
  waiting for transfers between devices  49.4 us (36%)
  Pallas kernels  21.3 us (16%)
  local copies, waits for them, and re-layouts  10.9 us (8%)
    ppermute x25, waiting for transfers between devices, permute(): return lax.ppermute(value, AXES, pairs)  45.2 us
    ppermute x25, starting transfers between devices, permute(): return lax.ppermute(value, AXES, pairs)  40.5 us
    pallas_call x12, Pallas kernels, call(): pl.pallas_call(kernel, out_shape=shapes, in_specs=[SMEM] * smem + [VMEM]...  21.3 us
    all_to_all x1, starting transfers between devices, copies(): lax.all_to_all(jnp.broadcast_to(value[None], (count, *value.shape)), axis...  9.9 us
    unnamed x18, local copies, waits for them, and re-layouts  8.13 us
    all_to_all x1, waiting for transfers between devices, copies(): lax.all_to_all(jnp.broadcast_to(value[None], (count, *value.shape)), axis...  4.24 us
  transfers between devices with their start and end apart: 26, of which 12 were waited for; matrix products, arithmetic and copies ran while one was open for 2% of the time, Pallas kernels for 8%

profile of v5, /device:TPU:32, one launch (start us, length us, event | category | flops | bytes accessed | tf_op | source)
XLA Modules:
  0.0 133.3 jit_solution(16923673722340819807)
XLA Ops:
  4.5 3.8 %collective-permute-start = (bf16[32,768]{1,0:T(8,128)(2,1)S(1)}, bf16[32,768]{1,0:T(8,128)(2,1)S(1)}, u32[]{:S(2)}, u32[]{:S(2)}) collective-permute-start(bf16[32,768]{1,0:T(8,128)(2,1)S(1)} %get-tuple-element.41), channel_id=1, source_target_pairs={{0,0},{1,4},{2,2},{3,6},{4,8},{5,12},{6,10},{7,14},{8,16},{9,20},{... | collective-permute-start | bytes 147464 | tf_op jit(solution)/shard_map/ppermute | solution.py:33
  8.3 5.5 %collective-permute-start.1 = (bf16[32,768]{1,0:T(8,128)(2,1)S(1)}, bf16[32,768]{1,0:T(8,128)(2,1)S(1)}, u32[]{:S(2)}, u32[]{:S(2)}) collective-permute-start(bf16[32,768]{1,0:T(8,128)(2,1)S(1)} %get-tuple-element.42), channel_id=1, source_target_pairs={{0,2},{1,6},{2,0},{3,4},{4,10},{5,14},{6,8},{7,12},{8,18},{9,22},{... | collective-permute-start | bytes 147464 | tf_op jit(solution)/shard_map/ppermute | solution.py:33
  18.9 9.9 %all-to-all-start = ((bf16[8,64,768]{2,1,0:T(8,128)(2,1)}), bf16[8,64,768]{2,1,0:T(8,128)(2,1)S(1)}, u32[]{:S(2)}, u32[]{:S(2)}) async-start(bf16[8,64,768]{2,1,0:T(8,128)(2,1)} %broadcast_in_dim.2), calls=%async_computation | async-start | bytes 1572864 | tf_op jit(solution)/shard_map/all_to_all | solution.py:275
  28.8 1.4 %collective-permute-start.3 = (bf16[144,2048]{1,0:T(8,128)(2,1)S(1)}, bf16[144,2048]{1,0:T(8,128)(2,1)S(1)}, u32[]{:S(2)}, u32[]{:S(2)}) collective-permute-start(bf16[144,2048]{1,0:T(8,128)(2,1)S(1)} %get-tuple-element.45.refs_0_), channel_id=1, source_target_pairs={{0,2},{1,3},{2,4},{3,5},{4,6},{5,7},{6,0},{7,1},{8,10},{9,11},{10,... | collective-permute-start | bytes 1769480 | tf_op jit(solution)/shard_map/ppermute | solution.py:33
  30.2 2.7 %collective-permute-start.4 = (bf16[128,2048]{1,0:T(8,128)(2,1)S(1)}, bf16[128,2048]{1,0:T(8,128)(2,1)S(1)}, u32[]{:S(2)}, u32[]{:S(2)}) collective-permute-start(bf16[128,2048]{1,0:T(8,128)(2,1)S(1)} %get-tuple-element.48.refs_4_), channel_id=1, source_target_pairs={{0,6},{1,7},{2,0},{3,1},{4,2},{5,3},{6,4},{7,5},{8,14},{9,15},{10,... | collective-permute-start | bytes 1572872 | tf_op jit(solution)/shard_map/ppermute | solution.py:33
  32.9 3.2 %collective-permute-start.8 = (bf16[144,2048]{1,0:T(8,128)(2,1)S(1)}, bf16[144,2048]{1,0:T(8,128)(2,1)S(1)}, u32[]{:S(2)}, u32[]{:S(2)}) collective-permute-start(bf16[144,2048]{1,0:T(8,128)(2,1)S(1)} %get-tuple-element.45.refs_0_), channel_id=1, source_target_pairs={{0,6},{1,7},{2,0},{3,1},{4,2},{5,3},{6,4},{7,5},{8,14},{9,15},{10,... | collective-permute-start | bytes 1769480 | tf_op jit(solution)/shard_map/ppermute | solution.py:33
  36.2 9.1 %collective-permute-done.4.refs_6_ = bf16[128,2048]{1,0:T(8,128)(2,1)S(1)} collective-permute-done((bf16[128,2048]{1,0:T(8,128)(2,1)S(1)}, bf16[128,2048]{1,0:T(8,128)(2,1)S(1)}, u32[]{:S(2)}, u32[]{:S(2)}) %collective-permute-start.4) | collective-permute-done | bytes 524320 | tf_op jit(solution)/shard_map/ppermute | solution.py:33
  47.2 4.2 %all-to-all-done = bf16[8,64,768]{2,1,0:T(8,128)(2,1)S(1)} async-done(((bf16[8,64,768]{2,1,0:T(8,128)(2,1)}), bf16[8,64,768]{2,1,0:T(8,128)(2,1)S(1)}, u32[]{:S(2)}, u32[]{:S(2)}) %all-to-all-start) | async-done | bytes 786464 | tf_op jit(solution)/shard_map/all_to_all | solution.py:275
  52.3 2.2 %collective-permute-start.5 = (bf16[512,256]{1,0:T(8,128)(2,1)S(1)}, bf16[512,256]{1,0:T(8,128)(2,1)S(1)}, u32[]{:S(2)}, u32[]{:S(2)}) collective-permute-start(bf16[512,256]{1,0:T(8,128)(2,1)S(1)} %slice.6.own), channel_id=1, source_target_pairs={{0,8},{1,9},{2,10},{3,11},{4,12},{5,13},{6,14},{7,15},{8,16},{9,17... | collective-permute-start | bytes 786440 | tf_op jit(solution)/shard_map/ppermute | solution.py:33
  54.5 2.8 %collective-permute-start.6 = (bf16[512,256]{1,0:T(8,128)(2,1)S(1)}, bf16[512,256]{1,0:T(8,128)(2,1)}, u32[]{:S(2)}, u32[]{:S(2)}) collective-permute-start(bf16[512,256]{1,0:T(8,128)(2,1)S(1)} %slice.6.own), channel_id=1, source_target_pairs={{0,24},{1,25},{2,26},{3,27},{4,28},{5,29},{6,30},{7,31},{8,0},{9,1... | collective-permute-start | bytes 786440 | tf_op jit(solution)/shard_map/ppermute | solution.py:33
  57.3 3.2 %collective-permute-start.10 = (bf16[128,2048]{1,0:T(8,128)(2,1)}, bf16[128,2048]{1,0:T(8,128)(2,1)}, u32[]{:S(2)}, u32[]{:S(2)}) collective-permute-start(bf16[128,2048]{1,0:T(8,128)(2,1)} %copy-done.2), channel_id=1, source_target_pairs={{0,6},{1,7},{2,0},{3,1},{4,2},{5,3},{6,4},{7,5},{8,14},{9,15},{10,... | collective-permute-start | bytes 1572872 | tf_op jit(solution)/shard_map/ppermute | solution.py:33
  61.7 1.9 %collective-permute-done.5.up = bf16[512,256]{1,0:T(8,128)(2,1)S(1)} collective-permute-done((bf16[512,256]{1,0:T(8,128)(2,1)S(1)}, bf16[512,256]{1,0:T(8,128)(2,1)S(1)}, u32[]{:S(2)}, u32[]{:S(2)}) %collective-permute-start.5) | collective-permute-done | bytes 262176 | tf_op jit(solution)/shard_map/ppermute | solution.py:33
  63.6 1.2 collective-permute-start.11
  65.8 1.8 %collective-permute-start.13 = (bf16[512,512]{1,0:T(8,128)(2,1)S(1)}, bf16[512,512]{1,0:T(8,128)(2,1)S(1)}, u32[]{:S(2)}, u32[]{:S(2)}) collective-permute-start(bf16[512,512]{1,0:T(8,128)(2,1)S(1)} %slice.7.own), channel_id=1, source_target_pairs={{0,8},{1,9},{2,10},{3,11},{4,12},{5,13},{6,14},{7,15},{8,16},{9,17... | collective-permute-start | bytes 1572872 | tf_op jit(solution)/shard_map/ppermute | solution.py:33
  67.6 1.5 %collective-permute-start.14 = (bf16[512,512]{1,0:T(8,128)(2,1)S(1)}, bf16[512,512]{1,0:T(8,128)(2,1)S(1)}, u32[]{:S(2)}, u32[]{:S(2)}) collective-permute-start(bf16[512,512]{1,0:T(8,128)(2,1)S(1)} %slice.7.own), channel_id=1, source_target_pairs={{0,24},{1,25},{2,26},{3,27},{4,28},{5,29},{6,30},{7,31},{8,0},{9,1... | collective-permute-start | bytes 1572872 | tf_op jit(solution)/shard_map/ppermute | solution.py:33
  69.1 2.4 %collective-permute-done.10.refs_7_ = bf16[128,2048]{1,0:T(8,128)(2,1)} collective-permute-done((bf16[128,2048]{1,0:T(8,128)(2,1)}, bf16[128,2048]{1,0:T(8,128)(2,1)}, u32[]{:S(2)}, u32[]{:S(2)}) %collective-permute-start.10) | collective-permute-done | bytes 524320 | tf_op jit(solution)/shard_map/ppermute | solution.py:33
  71.5 1.8 %collective-permute-done.9.refs_3_ = bf16[144,2048]{1,0:T(8,128)(2,1)S(1)} collective-permute-done((bf16[144,2048]{1,0:T(8,128)(2,1)S(1)}, bf16[144,2048]{1,0:T(8,128)(2,1)S(1)}, u32[]{:S(2)}, u32[]{:S(2)}) %collective-permute-start.9) | collective-permute-done | bytes 589856 | tf_op jit(solution)/shard_map/ppermute | solution.py:33
  74.4 1.5 %shard_map.68 = (bf16[1024,2048]{1,0:T(8,128)(2,1)S(1)}, bf16[16,128]{1,0:T(8,128)(2,1)S(1)}) custom-call(s32[4]{0:T(128)S(1)} %pad_add_fusion.idx, bf16[144,2048]{1,0:T(8,128)(2,1)S(1)} %get-tuple-element.45.refs_0_, bf16[144,2048]{1,0:T(8,128)(2,1)S(1)} %collective-permute-done.3.refs_1_, bf16[144,2048]{1,0:T(8,128)(2,1)S(1)} %collective-permute-done.8.refs_2_, ...), custom_call_target="tpu_custom_call" | custom-call | bytes 8388608 | tf_op jit(solution)/shard_map/pallas_call | solution.py:255
  75.9 2.3 %shard_map.69 = (f32[512,256]{1,0:T(8,128)S(1)}, f32[512,256]{1,0:T(8,128)S(1)}) custom-call(s32[4]{0:T(128)S(1)} %pad_add_fusion.idx, bf16[1024,2048]{1,0:T(8,128)(2,1)S(1)} %get-tuple-element.65.x_all, bf16[512,256]{1,0:T(8,128)(2,1)S(1)} %slice.6.own, bf16[512,256]{1,0:T(8,128)(2,1)S(1)} %collective-permute-done.5.up, ...), custom_call_target="tpu_custom_call" | custom-call | flops 1073741824 | bytes 10485760 | tf_op jit(solution)/shard_map/pallas_call | solution.py:255
  78.3 5.3 %collective-permute-done.13.up = bf16[512,512]{1,0:T(8,128)(2,1)S(1)} collective-permute-done((bf16[512,512]{1,0:T(8,128)(2,1)S(1)}, bf16[512,512]{1,0:T(8,128)(2,1)S(1)}, u32[]{:S(2)}, u32[]{:S(2)}) %collective-permute-start.13) | collective-permute-done | bytes 524320 | tf_op jit(solution)/shard_map/ppermute | solution.py:33
  84.0 3.3 %collective-permute-start.18 = (bf16[1040,128]{1,0:T(8,128)(2,1)S(1)}, bf16[1040,128]{1,0:T(8,128)(2,1)S(1)}, u32[]{:S(2)}, u32[]{:S(2)}) collective-permute-start(bf16[1040,128]{1,0:T(8,128)(2,1)S(1)} %shard_map.70.refs_4_), channel_id=1, source_target_pairs={{0,24},{1,25},{2,26},{3,27},{4,28},{5,29},{6,30},{7,31},{8,32},{9,... | collective-permute-start | bytes 798728 | tf_op jit(solution)/shard_map/ppermute | solution.py:33
  88.3 9.8 %collective-permute-done.15.far = bf16[512,512]{1,0:T(8,128)(2,1)S(1)} collective-permute-done((bf16[512,512]{1,0:T(8,128)(2,1)S(1)}, bf16[512,512]{1,0:T(8,128)(2,1)S(1)}, u32[]{:S(2)}, u32[]{:S(2)}) %collective-permute-start.15) | collective-permute-done | bytes 524320 | tf_op jit(solution)/shard_map/ppermute | solution.py:33
  98.1 3.1 %shard_map.71 = (f32[512,512]{1,0:T(8,128)S(1)}, f32[512,512]{1,0:T(8,128)S(1)}) custom-call(s32[4]{0:T(128)S(1)} %pad_add_fusion.idx, bf16[1024,2048]{1,0:T(8,128)(2,1)S(1)} %get-tuple-element.65.x_all, bf16[512,512]{1,0:T(8,128)(2,1)S(1)} %slice.7.own, bf16[512,512]{1,0:T(8,128)(2,1)S(1)} %collective-permute-done.13.up, ...), custom_call_target="tpu_custom_call" | custom-call | flops 2147483648 | bytes 10485760 | tf_op jit(solution)/shard_map/pallas_call | solution.py:255
  101.3 4.5 %collective-permute-done.19.refs_2_ = bf16[1040,128]{1,0:T(8,128)(2,1)S(1)} collective-permute-done((bf16[1040,128]{1,0:T(8,128)(2,1)S(1)}, bf16[1040,128]{1,0:T(8,128)(2,1)S(1)}, u32[]{:S(2)}, u32[]{:S(2)}) %collective-permute-start.19) | collective-permute-done | bytes 266272 | tf_op jit(solution)/shard_map/ppermute | solution.py:33
  105.7 4.9 %collective-permute-done.20.refs_3_ = bf16[1040,128]{1,0:T(8,128)(2,1)S(1)} collective-permute-done((bf16[1040,128]{1,0:T(8,128)(2,1)S(1)}, bf16[1040,128]{1,0:T(8,128)(2,1)S(1)}, u32[]{:S(2)}, u32[]{:S(2)}) %collective-permute-start.20) | collective-permute-done | bytes 266272 | tf_op jit(solution)/shard_map/ppermute | solution.py:33
  110.6 1.4 %shard_map.73 = (bf16[20,2,128,128]{3,2,1,0:T(8,128)(2,1)S(1)}, s32[4,1,512]{2,1,0:T(1,128)S(1)}) custom-call(s32[4]{0:T(128)S(1)} %pad_add_fusion.idx, bf16[1040,128]{1,0:T(8,128)(2,1)S(1)} %collective-permute-done.17.refs_0_, bf16[1040,128]{1,0:T(8,128)(2,1)S(1)} %collective-permute-done.18.refs_1_, bf16[1040,128]{1,0:T(8,128)(2,1)S(1)} %collective-permute-done.19.refs_2_, ...), custom_call_target="tpu_custom_call" | custom-call | flops 68719476736 | bytes 4194304 | tf_op jit(solution)/shard_map/pallas_call | solution.py:255
  113.0 8.2 %shard_map.74 = (bf16[128,512]{1,0:T(8,128)(2,1)S(1)}, bf16[128,512]{1,0:T(8,128)(2,1)S(1)}, bf16[128,512]{1,0:T(8,128)(2,1)S(1)}, bf16[128,512]{1,0:T(8,128)(2,1)S(1)}) custom-call(s32[4]{0:T(128)S(1)} %pad_add_fusion.idx, bf16[4,512,128]{2,1,0:T(8,128)(2,1)S(1)} %shard_map.72.query, bf16[20,2,128,128]{3,2,1,0:T(8,128)(2,1)S(1)} %get-tuple-element.71.kv, ...), custom_call_target="tpu_custom_call" | custom-call | flops 2147483648 | bytes 4194304 | tf_op jit(solution)/shard_map/pallas_call | solution.py:255
  122.3 3.3 %collective-permute-start.23 = (bf16[128,512]{1,0:T(8,128)(2,1)S(1)}, bf16[128,512]{1,0:T(8,128)(2,1)S(1)}, u32[]{:S(2)}, u32[]{:S(2)}) collective-permute-start(bf16[128,512]{1,0:T(8,128)(2,1)S(1)} %get-tuple-element.75), channel_id=1, source_target_pairs={{0,4},{1,6},{2,0},{3,2},{4,5},{5,7},{6,1},{7,3},{8,12},{9,14},{10,... | collective-permute-start | bytes 393224 | tf_op jit(solution)/shard_map/ppermute | solution.py:33
  125.7 1.9 %collective-permute-start.24 = (bf16[128,512]{1,0:T(8,128)(2,1)S(1)}, bf16[128,512]{1,0:T(8,128)(2,1)S(1)}, u32[]{:S(2)}, u32[]{:S(2)}) collective-permute-start(bf16[128,512]{1,0:T(8,128)(2,1)S(1)} %get-tuple-element.76), channel_id=1, source_target_pairs={{0,6},{1,4},{2,2},{3,0},{4,7},{5,5},{6,3},{7,1},{8,14},{9,12},{10,... | collective-permute-start | bytes 393224 | tf_op jit(solution)/shard_map/ppermute | solution.py:33
  127.6 1.4 %collective-permute-done.23.refs_2_ = bf16[128,512]{1,0:T(8,128)(2,1)S(1)} collective-permute-done((bf16[128,512]{1,0:T(8,128)(2,1)S(1)}, bf16[128,512]{1,0:T(8,128)(2,1)S(1)}, u32[]{:S(2)}, u32[]{:S(2)}) %collective-permute-start.23) | collective-permute-done | bytes 131104 | tf_op jit(solution)/shard_map/ppermute | solution.py:33
  129.0 2.9 %collective-permute-done.24.refs_3_ = bf16[128,512]{1,0:T(8,128)(2,1)S(1)} collective-permute-done((bf16[128,512]{1,0:T(8,128)(2,1)S(1)}, bf16[128,512]{1,0:T(8,128)(2,1)S(1)}, u32[]{:S(2)}, u32[]{:S(2)}) %collective-permute-start.24) | collective-permute-done | bytes 131104 | tf_op jit(solution)/shard_map/ppermute | solution.py:33
  132.0 1.4 %shard_map.75 = bf16[2,128,1024]{2,1,0:T(8,128)(2,1)} custom-call(s32[4]{0:T(128)S(1)} %pad_add_fusion.idx, bf16[128,512]{1,0:T(8,128)(2,1)S(1)} %collective-permute-done.21.refs_0_, bf16[128,512]{1,0:T(8,128)(2,1)S(1)} %collective-permute-done.22.refs_1_, bf16[128,512]{1,0:T(8,128)(2,1)S(1)} %collective-permute-done.23.refs_2_, ...), custom_call_target="tpu_custom_call" | custom-call | bytes 1048576 | tf_op jit(solution)/shard_map/pallas_call | solution.py:255
  (58 shorter events, 19.0 us)
Async XLA Ops:
  0.0 1.2 copy-start
  1.5 13.0 %collective-permute-start.2 = (f32[256,128]{1,0:T(8,128)S(1)}, f32[256,128]{1,0:T(8,128)S(1)}, u32[]{:S(2)}, u32[]{:S(2)}) collective-permute-start(f32[256,128]{1,0:T(8,128)S(1)} %shard_map.65.squares), channel_id=1, source_target_pairs={{0,1},{1,0},{2,3},{3,2},{4,5},{5,4},{6,7},{7,6},{8,9},{9,8},{10,11... | collective-permute-start | bytes 393224 | tf_op jit(solution)/shard_map/ppermute | solution.py:33
  1.7 0.8 copy-start.4
  4.5 12.8 %collective-permute-start = (bf16[32,768]{1,0:T(8,128)(2,1)S(1)}, bf16[32,768]{1,0:T(8,128)(2,1)S(1)}, u32[]{:S(2)}, u32[]{:S(2)}) collective-permute-start(bf16[32,768]{1,0:T(8,128)(2,1)S(1)} %get-tuple-element.41), channel_id=1, source_target_pairs={{0,0},{1,4},{2,2},{3,6},{4,8},{5,12},{6,10},{7,14},{8,16},{9,20},{... | collective-permute-start | bytes 147464 | tf_op jit(solution)/shard_map/ppermute | solution.py:33
  8.3 9.0 %collective-permute-start.1 = (bf16[32,768]{1,0:T(8,128)(2,1)S(1)}, bf16[32,768]{1,0:T(8,128)(2,1)S(1)}, u32[]{:S(2)}, u32[]{:S(2)}) collective-permute-start(bf16[32,768]{1,0:T(8,128)(2,1)S(1)} %get-tuple-element.42), channel_id=1, source_target_pairs={{0,2},{1,6},{2,0},{3,4},{4,10},{5,14},{6,8},{7,12},{8,18},{9,22},{... | collective-permute-start | bytes 147464 | tf_op jit(solution)/shard_map/ppermute | solution.py:33
  14.5 1.2 copy-start.1
  18.9 32.5 %all-to-all-start = ((bf16[8,64,768]{2,1,0:T(8,128)(2,1)}), bf16[8,64,768]{2,1,0:T(8,128)(2,1)S(1)}, u32[]{:S(2)}, u32[]{:S(2)}) async-start(bf16[8,64,768]{2,1,0:T(8,128)(2,1)} %broadcast_in_dim.2), calls=%async_computation | async-start | bytes 1572864 | tf_op jit(solution)/shard_map/all_to_all | solution.py:275
  28.8 18.4 %collective-permute-start.3 = (bf16[144,2048]{1,0:T(8,128)(2,1)S(1)}, bf16[144,2048]{1,0:T(8,128)(2,1)S(1)}, u32[]{:S(2)}, u32[]{:S(2)}) collective-permute-start(bf16[144,2048]{1,0:T(8,128)(2,1)S(1)} %get-tuple-element.45.refs_0_), channel_id=1, source_target_pairs={{0,2},{1,3},{2,4},{3,5},{4,6},{5,7},{6,0},{7,1},{8,10},{9,11},{10,... | collective-permute-start | bytes 1769480 | tf_op jit(solution)/shard_map/ppermute | solution.py:33
  30.2 15.1 %collective-permute-start.4 = (bf16[128,2048]{1,0:T(8,128)(2,1)S(1)}, bf16[128,2048]{1,0:T(8,128)(2,1)S(1)}, u32[]{:S(2)}, u32[]{:S(2)}) collective-permute-start(bf16[128,2048]{1,0:T(8,128)(2,1)S(1)} %get-tuple-element.48.refs_4_), channel_id=1, source_target_pairs={{0,6},{1,7},{2,0},{3,1},{4,2},{5,3},{6,4},{7,5},{8,14},{9,15},{10,... | collective-permute-start | bytes 1572872 | tf_op jit(solution)/shard_map/ppermute | solution.py:33
  32.9 24.4 %collective-permute-start.7 = (bf16[128,2048]{1,0:T(8,128)(2,1)S(1)}, bf16[128,2048]{1,0:T(8,128)(2,1)}, u32[]{:S(2)}, u32[]{:S(2)}) collective-permute-start(bf16[128,2048]{1,0:T(8,128)(2,1)S(1)} %get-tuple-element.48.refs_4_), channel_id=1, source_target_pairs={{0,2},{1,3},{2,4},{3,5},{4,6},{5,7},{6,0},{7,1},{8,10},{9,11},{10,... | collective-permute-start | bytes 1572872 | tf_op jit(solution)/shard_map/ppermute | solution.py:33
  32.9 28.7 %collective-permute-start.8 = (bf16[144,2048]{1,0:T(8,128)(2,1)S(1)}, bf16[144,2048]{1,0:T(8,128)(2,1)S(1)}, u32[]{:S(2)}, u32[]{:S(2)}) collective-permute-start(bf16[144,2048]{1,0:T(8,128)(2,1)S(1)} %get-tuple-element.45.refs_0_), channel_id=1, source_target_pairs={{0,6},{1,7},{2,0},{3,1},{4,2},{5,3},{6,4},{7,5},{8,14},{9,15},{10,... | collective-permute-start | bytes 1769480 | tf_op jit(solution)/shard_map/ppermute | solution.py:33
  45.3 0.8 copy-start.2
  51.4 0.9 copy-start.8
  52.3 11.3 %collective-permute-start.5 = (bf16[512,256]{1,0:T(8,128)(2,1)S(1)}, bf16[512,256]{1,0:T(8,128)(2,1)S(1)}, u32[]{:S(2)}, u32[]{:S(2)}) collective-permute-start(bf16[512,256]{1,0:T(8,128)(2,1)S(1)} %slice.6.own), channel_id=1, source_target_pairs={{0,8},{1,9},{2,10},{3,11},{4,12},{5,13},{6,14},{7,15},{8,16},{9,17... | collective-permute-start | bytes 786440 | tf_op jit(solution)/shard_map/ppermute | solution.py:33
  54.5 9.1 %collective-permute-start.6 = (bf16[512,256]{1,0:T(8,128)(2,1)S(1)}, bf16[512,256]{1,0:T(8,128)(2,1)}, u32[]{:S(2)}, u32[]{:S(2)}) collective-permute-start(bf16[512,256]{1,0:T(8,128)(2,1)S(1)} %slice.6.own), channel_id=1, source_target_pairs={{0,24},{1,25},{2,26},{3,27},{4,28},{5,29},{6,30},{7,31},{8,0},{9,1... | collective-permute-start | bytes 786440 | tf_op jit(solution)/shard_map/ppermute | solution.py:33
  57.3 16.0 %collective-permute-start.9 = (bf16[144,2048]{1,0:T(8,128)(2,1)S(1)}, bf16[144,2048]{1,0:T(8,128)(2,1)S(1)}, u32[]{:S(2)}, u32[]{:S(2)}) collective-permute-start(bf16[144,2048]{1,0:T(8,128)(2,1)S(1)} %collective-permute-done.3.refs_1_), channel_id=1, source_target_pairs={{0,2},{1,3},{2,4},{3,5},{4,6},{5,7},{6,0},{7,1},{8,10},{9,11},{10,... | collective-permute-start | bytes 1769480 | tf_op jit(solution)/shard_map/ppermute | solution.py:33
  57.3 14.2 %collective-permute-start.10 = (bf16[128,2048]{1,0:T(8,128)(2,1)}, bf16[128,2048]{1,0:T(8,128)(2,1)}, u32[]{:S(2)}, u32[]{:S(2)}) collective-permute-start(bf16[128,2048]{1,0:T(8,128)(2,1)} %copy-done.2), channel_id=1, source_target_pairs={{0,6},{1,7},{2,0},{3,1},{4,2},{5,3},{6,4},{7,5},{8,14},{9,15},{10,... | collective-permute-start | bytes 1572872 | tf_op jit(solution)/shard_map/ppermute | solution.py:33
  63.6 12.3 %collective-permute-start.11 = (bf16[512,256]{1,0:T(8,128)(2,1)S(1)}, bf16[512,256]{1,0:T(8,128)(2,1)S(1)}, u32[]{:S(2)}, u32[]{:S(2)}) collective-permute-start(bf16[512,256]{1,0:T(8,128)(2,1)S(1)} %collective-permute-done.5.up), channel_id=1, source_target_pairs={{0,8},{1,9},{2,10},{3,11},{4,12},{5,13},{6,14},{7,15},{8,16},{9,17... | collective-permute-start | bytes 786440 | tf_op jit(solution)/shard_map/ppermute | solution.py:33
  65.8 17.7 %collective-permute-start.13 = (bf16[512,512]{1,0:T(8,128)(2,1)S(1)}, bf16[512,512]{1,0:T(8,128)(2,1)S(1)}, u32[]{:S(2)}, u32[]{:S(2)}) collective-permute-start(bf16[512,512]{1,0:T(8,128)(2,1)S(1)} %slice.7.own), channel_id=1, source_target_pairs={{0,8},{1,9},{2,10},{3,11},{4,12},{5,13},{6,14},{7,15},{8,16},{9,17... | collective-permute-start | bytes 1572872 | tf_op jit(solution)/shard_map/ppermute | solution.py:33
  67.6 15.9 %collective-permute-start.14 = (bf16[512,512]{1,0:T(8,128)(2,1)S(1)}, bf16[512,512]{1,0:T(8,128)(2,1)S(1)}, u32[]{:S(2)}, u32[]{:S(2)}) collective-permute-start(bf16[512,512]{1,0:T(8,128)(2,1)S(1)} %slice.7.own), channel_id=1, source_target_pairs={{0,24},{1,25},{2,26},{3,27},{4,28},{5,29},{6,30},{7,31},{8,0},{9,1... | collective-permute-start | bytes 1572872 | tf_op jit(solution)/shard_map/ppermute | solution.py:33
  73.4 1.0 copy-start.3
  78.2 5.4 %collective-permute-start.12 = (f32[512,256]{1,0:T(8,128)S(1)}, f32[512,256]{1,0:T(8,128)S(1)}, u32[]{:S(2)}, u32[]{:S(2)}) collective-permute-start(f32[512,256]{1,0:T(8,128)S(1)} %get-tuple-element.59), channel_id=1, source_target_pairs={{0,1},{1,0},{2,3},{3,2},{4,5},{5,4},{6,7},{7,6},{8,9},{9,8},{10,11... | collective-permute-start | bytes 1572872 | tf_op jit(solution)/shard_map/ppermute | solution.py:33
  83.6 14.5 %collective-permute-start.15 = (bf16[512,512]{1,0:T(8,128)(2,1)S(1)}, bf16[512,512]{1,0:T(8,128)(2,1)S(1)}, u32[]{:S(2)}, u32[]{:S(2)}) collective-permute-start(bf16[512,512]{1,0:T(8,128)(2,1)S(1)} %collective-permute-done.13.up), channel_id=1, source_target_pairs={{0,8},{1,9},{2,10},{3,11},{4,12},{5,13},{6,14},{7,15},{8,16},{9,17... | collective-permute-start | bytes 1572872 | tf_op jit(solution)/shard_map/ppermute | solution.py:33
  83.9 17.3 %collective-permute-start.17 = (bf16[1040,128]{1,0:T(8,128)(2,1)S(1)}, bf16[1040,128]{1,0:T(8,128)(2,1)S(1)}, u32[]{:S(2)}, u32[]{:S(2)}) collective-permute-start(bf16[1040,128]{1,0:T(8,128)(2,1)S(1)} %shard_map.70.refs_4_), channel_id=1, source_target_pairs={{0,32},{1,33},{2,34},{3,35},{4,36},{5,37},{6,38},{7,39},{8,40},{9,... | collective-permute-start | bytes 798728 | tf_op jit(solution)/shard_map/ppermute | solution.py:33
  84.0 17.2 %collective-permute-start.18 = (bf16[1040,128]{1,0:T(8,128)(2,1)S(1)}, bf16[1040,128]{1,0:T(8,128)(2,1)S(1)}, u32[]{:S(2)}, u32[]{:S(2)}) collective-permute-start(bf16[1040,128]{1,0:T(8,128)(2,1)S(1)} %shard_map.70.refs_4_), channel_id=1, source_target_pairs={{0,24},{1,25},{2,26},{3,27},{4,28},{5,29},{6,30},{7,31},{8,32},{9,... | collective-permute-start | bytes 798728 | tf_op jit(solution)/shard_map/ppermute | solution.py:33
  87.3 18.4 %collective-permute-start.19 = (bf16[1040,128]{1,0:T(8,128)(2,1)S(1)}, bf16[1040,128]{1,0:T(8,128)(2,1)S(1)}, u32[]{:S(2)}, u32[]{:S(2)}) collective-permute-start(bf16[1040,128]{1,0:T(8,128)(2,1)S(1)} %shard_map.70.refs_4_), channel_id=1, source_target_pairs={{0,16},{1,17},{2,18},{3,19},{4,20},{5,21},{6,22},{7,23},{8,24},{9,... | collective-permute-start | bytes 798728 | tf_op jit(solution)/shard_map/ppermute | solution.py:33
  87.3 23.3 %collective-permute-start.20 = (bf16[1040,128]{1,0:T(8,128)(2,1)S(1)}, bf16[1040,128]{1,0:T(8,128)(2,1)S(1)}, u32[]{:S(2)}, u32[]{:S(2)}) collective-permute-start(bf16[1040,128]{1,0:T(8,128)(2,1)S(1)} %shard_map.70.refs_4_), channel_id=1, source_target_pairs={{0,8},{1,9},{2,10},{3,11},{4,12},{5,13},{6,14},{7,15},{8,16},{9,17... | collective-permute-start | bytes 798728 | tf_op jit(solution)/shard_map/ppermute | solution.py:33
  101.1 11.0 %collective-permute-start.16 = (f32[512,512]{1,0:T(8,128)S(1)}, f32[512,512]{1,0:T(8,128)S(1)}, u32[]{:S(2)}, u32[]{:S(2)}) collective-permute-start(f32[512,512]{1,0:T(8,128)S(1)} %get-tuple-element.69), channel_id=1, source_target_pairs={{0,1},{1,0},{2,3},{3,2},{4,5},{5,4},{6,7},{7,6},{8,9},{9,8},{10,11... | collective-permute-start | bytes 3145736 | tf_op jit(solution)/shard_map/ppermute | solution.py:33
  121.2 6.4 %collective-permute-start.21 = (bf16[128,512]{1,0:T(8,128)(2,1)S(1)}, bf16[128,512]{1,0:T(8,128)(2,1)S(1)}, u32[]{:S(2)}, u32[]{:S(2)}) collective-permute-start(bf16[128,512]{1,0:T(8,128)(2,1)S(1)} %get-tuple-element.73), channel_id=1, source_target_pairs={{0,0},{1,2},{2,4},{3,6},{4,1},{5,3},{6,5},{7,7},{8,8},{9,10},{10,1... | collective-permute-start | bytes 393224 | tf_op jit(solution)/shard_map/ppermute | solution.py:33
  121.9 5.7 %collective-permute-start.22 = (bf16[128,512]{1,0:T(8,128)(2,1)S(1)}, bf16[128,512]{1,0:T(8,128)(2,1)S(1)}, u32[]{:S(2)}, u32[]{:S(2)}) collective-permute-start(bf16[128,512]{1,0:T(8,128)(2,1)S(1)} %get-tuple-element.74), channel_id=1, source_target_pairs={{0,2},{1,0},{2,6},{3,4},{4,3},{5,1},{6,7},{7,5},{8,10},{9,8},{10,1... | collective-permute-start | bytes 393224 | tf_op jit(solution)/shard_map/ppermute | solution.py:33
  122.3 6.7 %collective-permute-start.23 = (bf16[128,512]{1,0:T(8,128)(2,1)S(1)}, bf16[128,512]{1,0:T(8,128)(2,1)S(1)}, u32[]{:S(2)}, u32[]{:S(2)}) collective-permute-start(bf16[128,512]{1,0:T(8,128)(2,1)S(1)} %get-tuple-element.75), channel_id=1, source_target_pairs={{0,4},{1,6},{2,0},{3,2},{4,5},{5,7},{6,1},{7,3},{8,12},{9,14},{10,... | collective-permute-start | bytes 393224 | tf_op jit(solution)/shard_map/ppermute | solution.py:33
  125.7 6.3 %collective-permute-start.24 = (bf16[128,512]{1,0:T(8,128)(2,1)S(1)}, bf16[128,512]{1,0:T(8,128)(2,1)S(1)}, u32[]{:S(2)}, u32[]{:S(2)}) collective-permute-start(bf16[128,512]{1,0:T(8,128)(2,1)S(1)} %get-tuple-element.76), channel_id=1, source_target_pairs={{0,6},{1,4},{2,2},{3,0},{4,7},{5,5},{6,3},{7,1},{8,14},{9,12},{10,... | collective-permute-start | bytes 393224 | tf_op jit(solution)/shard_map/ppermute | solution.py:33
  (3 other events, 2.1 us)
